TPU v7x, 32 devices: a whole 2x2x4 slice. The times are simulated.
32 devices in a mesh: angle: 4 (over y, x), row: 8 (over z, core).
Axes of the slice: x: 2, y: 2, z: 4, core: 2. Of those that a mesh axis runs over, the one named last changes fastest.
Arguments:
- intensity: float32 [512, 8, 4096], P('angle', 'row'), may hold values from 0.036 to 1
- flat_field: float32 [8, 4096], P('row'), may hold values from 1 to 2
- dark_field: float32 [8, 4096], P('row'), may hold values from 0 to 0.02
- correlation: int32 [1], replicated, may hold values from 512 to 1536
- blend_width: int32 [1], replicated, may hold values from 64 to 511
- padding: int32 [1], replicated, may hold values from 1024 to 4096
- cutoff: int32 [1], replicated, may hold values from 1 to 8
Outputs:
- sinogram: float32 [256, 8, 8192], P('angle', 'row')
All inputs are finite; a program needn't handle non-finite values.
Results may differ from a plain program's by a relative error of at most 0.00023.
Values sent between devices are 32-bit elements; how exact they have to be, the bound alone decides.
No kernel may reach another device: no remote copies, remote signals or barrier semaphores. Data moves between devices by JAX's collectives and lax.ppermute only.
A program may use at most 128 MiB of HBM per device.

v0:
```python
import math

import jax
import jax.numpy as jnp
from jax import lax
from jax.sharding import PartitionSpec as P

KMAX = 8
FCUT = 512


def swapped(value, axis, bit):
    mask = 2**bit
    pairs = [(source, source ^ mask) for source in range(lax.axis_size(axis))]
    return lax.ppermute(value, axis, pairs)


def matmul_hi(left_side, right_side):
    return jnp.dot(
        left_side, right_side, precision=lax.Precision.HIGHEST, preferred_element_type=jnp.float32
    )


def einsum_hi(pattern, left_side, right_side):
    return jnp.einsum(
        pattern,
        left_side,
        right_side,
        precision=lax.Precision.HIGHEST,
        preferred_element_type=jnp.float32,
    )


def phase_table(first_index, second, modulus):
    angle_value = (first_index[:, None] * second[None, :] % modulus).astype(jnp.float32) * (
        2.0 * math.pi / modulus
    )
    return (jnp.cos(angle_value), jnp.sin(angle_value))


def stitch(main_view, back_view, correlation, blend_size):
    pixels = main_view.shape[-1]
    leading = main_view.shape[:-1]
    last_axis = main_view.ndim - 1
    empty = jnp.zeros(leading + (pixels,), main_view.dtype)
    edge_hold = jnp.broadcast_to(main_view[..., -1:], leading + (pixels,))
    extended_main = jnp.concatenate([empty, main_view, edge_hold], axis=-1)
    right_side = lax.dynamic_slice_in_dim(extended_main, correlation, 2 * pixels, last_axis)
    left_side = jnp.concatenate([jnp.flip(back_view, -1), empty], axis=-1)
    position = jnp.arange(2 * pixels).astype(main_view.dtype)
    center = pixels - correlation.astype(main_view.dtype) / 2.0
    weight_right = jnp.clip(
        (position + 0.5 - center) / blend_size.astype(main_view.dtype) + 0.5, 0.0, 1.0
    )
    return left_side * (1.0 - weight_right) + right_side * weight_right


def extend(stitched, padding, length):
    width_now = stitched.shape[-1]
    leading = stitched.shape[:-1]
    base_row = jnp.concatenate(
        [stitched, jnp.zeros(leading + (length - width_now,), stitched.dtype)], axis=-1
    )
    index_list = jnp.arange(length, dtype=jnp.int32)
    right_mask = (index_list >= width_now) & (index_list < width_now + padding)
    left_mask = index_list >= length - padding
    return (
        base_row
        + jnp.where(right_mask, stitched[..., -1:], 0.0)
        + jnp.where(left_mask, stitched[..., :1], 0.0)
    )


def forward_transform(signal, factor_size):
    row_total = signal.shape[0]
    length = factor_size * factor_size
    blocks = signal.reshape(row_total, factor_size, factor_size)
    steps = jnp.arange(factor_size, dtype=jnp.int32)
    half_steps = jnp.arange(factor_size // 2, dtype=jnp.int32)
    cos_first, sin_first = phase_table(steps, steps, factor_size)
    part_re = einsum_hi("mab,ak->mkb", blocks, cos_first)
    part_im = -einsum_hi("mab,ak->mkb", blocks, sin_first)
    cos_turn, sin_turn = phase_table(steps, steps, length)
    turned_re = part_re * cos_turn + part_im * sin_turn
    turned_im = part_im * cos_turn - part_re * sin_turn
    cos_last, sin_last = phase_table(steps, half_steps, factor_size)
    result_re = einsum_hi("mkb,bj->mjk", turned_re, cos_last) + einsum_hi(
        "mkb,bj->mjk", turned_im, sin_last
    )
    result_im = einsum_hi("mkb,bj->mjk", turned_im, cos_last) - einsum_hi(
        "mkb,bj->mjk", turned_re, sin_last
    )
    return (result_re.reshape(row_total, length // 2), result_im.reshape(row_total, length // 2))


def inverse_transform(spec_re, spec_im, factor_size):
    row_total = spec_re.shape[0]
    length = factor_size * factor_size
    steps = jnp.arange(factor_size, dtype=jnp.int32)
    half_steps = jnp.arange(factor_size // 2, dtype=jnp.int32)
    grid_re = spec_re.reshape(row_total, factor_size // 2, factor_size)
    grid_im = spec_im.reshape(row_total, factor_size // 2, factor_size)
    cos_first, sin_first = phase_table(half_steps, steps, factor_size)
    inner_re = einsum_hi("mjk,ja->mak", grid_re, cos_first) - einsum_hi(
        "mjk,ja->mak", grid_im, sin_first
    )
    inner_im = einsum_hi("mjk,ja->mak", grid_im, cos_first) + einsum_hi(
        "mjk,ja->mak", grid_re, sin_first
    )
    cos_turn, sin_turn = phase_table(steps, steps, length)
    turned_re = inner_re * cos_turn - inner_im * sin_turn
    turned_im = inner_im * cos_turn + inner_re * sin_turn
    cos_last, sin_last = phase_table(steps, half_steps, factor_size)
    result = einsum_hi("mak,kb->mba", turned_re, cos_last) - einsum_hi(
        "mak,kb->mba", turned_im, sin_last
    )
    return result.reshape(row_total, length // 2) * (2.0 / length)


def stitched_angle(block_index, offset, half_block, angle_count):
    halves = angle_count // 2
    return block_index % halves * 2 * half_block + block_index // halves * half_block + offset


def mode_tables(angle_list, half_turn):
    orders = jnp.arange(-(KMAX - 1), KMAX, dtype=jnp.int32)
    return phase_table(orders, angle_list, half_turn)


def project_modes(flat_re, flat_im, cos_modes, sin_modes):
    modes_re = matmul_hi(cos_modes, flat_re) + matmul_hi(sin_modes, flat_im)
    modes_im = matmul_hi(cos_modes, flat_im) - matmul_hi(sin_modes, flat_re)
    return (modes_re, modes_im)


def remove_modes(flat_re, flat_im, modes_re, modes_im, cos_modes, sin_modes, weight):
    scaled_re = modes_re * weight
    scaled_im = modes_im * weight
    low_re = matmul_hi(cos_modes.T, scaled_re) - matmul_hi(sin_modes.T, scaled_im)
    low_im = matmul_hi(cos_modes.T, scaled_im) + matmul_hi(sin_modes.T, scaled_re)
    return (flat_re - low_re, flat_im - low_im)


def local(intensity, flat_field, dark_field, correlation, blend_width, padding, cutoff):
    angle_count = lax.axis_size("angle")
    row_devices = lax.axis_size("row")
    angle_place = lax.axis_index("angle")
    row_place = lax.axis_index("row")
    half_block = intensity.shape[0] // 2
    local_rows = intensity.shape[1]
    pixels = intensity.shape[2]
    length = 4 * pixels
    kept_bins = 2 * pixels
    factor_size = math.isqrt(length)
    half_turn = half_block * angle_count
    projected = -jnp.log((intensity - dark_field) / (flat_field - dark_field))
    upper_half = angle_place >= angle_count // 2
    outgoing = lax.dynamic_slice_in_dim(
        projected, jnp.where(upper_half, 0, half_block), half_block, 0
    )
    partner = swapped(outgoing, "angle", angle_count.bit_length() - 2)
    staying = lax.dynamic_slice_in_dim(
        projected, jnp.where(upper_half, half_block, 0), half_block, 0
    )
    main_view = jnp.where(upper_half, partner, staying)
    back_view = jnp.where(upper_half, staying, partner)
    stitched = stitch(main_view, back_view, correlation[0], blend_width[0])
    extended = extend(stitched, padding[0], length)
    spec_re, spec_im = forward_transform(
        extended.reshape(half_block * local_rows, length), factor_size
    )
    frequency = jnp.arange(kept_bins).astype(jnp.float32)
    ramp_gain = frequency / kept_bins * (1.0 + jnp.cos(math.pi * frequency / kept_bins))
    drop_gain = 1.0 - 1.0 / (1.0 + (frequency / FCUT) ** 8)
    orders = jnp.arange(-(KMAX - 1), KMAX, dtype=jnp.int32)
    chosen = (jnp.abs(orders) < cutoff[0]).astype(jnp.float32)[:, None] / half_turn
    piece_width = kept_bins // (angle_count * row_devices)
    shaped_re = spec_re.reshape(
        1, half_block, 1, local_rows, angle_count, row_devices * piece_width
    )
    shaped_im = spec_im.reshape(
        1, half_block, 1, local_rows, angle_count, row_devices * piece_width
    )
    moved_re, moved_im = (
        lax.all_to_all(
            lax.all_to_all(shaped_re, "angle", split_axis=4, concat_axis=0, tiled=True),
            "row",
            split_axis=5,
            concat_axis=2,
            tiled=True,
        ),
        lax.all_to_all(
            lax.all_to_all(shaped_im, "angle", split_axis=4, concat_axis=0, tiled=True),
            "row",
            split_axis=5,
            concat_axis=2,
            tiled=True,
        ),
    )
    angle_list = stitched_angle(
        jnp.arange(angle_count, dtype=jnp.int32)[:, None],
        jnp.arange(half_block, dtype=jnp.int32)[None, :],
        half_block,
        angle_count,
    ).reshape(-1)
    cos_modes, sin_modes = mode_tables(angle_list, half_turn)
    column_total = row_devices * local_rows * piece_width
    flat_re = moved_re.reshape(angle_count * half_block, column_total)
    flat_im = moved_im.reshape(angle_count * half_block, column_total)
    modes_re, modes_im = project_modes(flat_re, flat_im, cos_modes, sin_modes)
    local_drop = lax.dynamic_slice_in_dim(
        drop_gain, (angle_place * row_devices + row_place) * piece_width, piece_width, 0
    )
    weight = chosen * jnp.tile(local_drop, row_devices * local_rows)[None, :]
    fixed_re, fixed_im = remove_modes(
        flat_re, flat_im, modes_re, modes_im, cos_modes, sin_modes, weight
    )
    layout = (angle_count, half_block, row_devices, local_rows, 1, piece_width)
    back_re, back_im = (
        lax.all_to_all(
            lax.all_to_all(
                fixed_re.reshape(layout), "angle", split_axis=0, concat_axis=4, tiled=True
            ),
            "row",
            split_axis=2,
            concat_axis=5,
            tiled=True,
        ),
        lax.all_to_all(
            lax.all_to_all(
                fixed_im.reshape(layout), "angle", split_axis=0, concat_axis=4, tiled=True
            ),
            "row",
            split_axis=2,
            concat_axis=5,
            tiled=True,
        ),
    )
    new_re = back_re.reshape(half_block, local_rows * kept_bins)
    new_im = back_im.reshape(half_block, local_rows * kept_bins)
    filtered_re = new_re * ramp_gain
    filtered_im = new_im * ramp_gain
    cleaned = inverse_transform(filtered_re, filtered_im, factor_size)
    return cleaned.reshape(half_block, local_rows, 2 * pixels)


def solution(mesh):
    placed = (P("angle", "row", None), P("row", None), P("row", None), P(), P(), P(), P())
    return jax.shard_map(
        local, mesh=mesh, in_specs=placed, out_specs=P("angle", "row", None), check_vma=False
    )
```

profile of v0, /device:TPU:0, one launch (start us, length us, event | category | flops | bytes accessed | tf_op | source)
XLA Modules:
  0.0 490.6 jit_solution(12838392834874085553)
XLA Ops:
  0.8 4.2 log_negate_fusion
  10.9 20.4 %collective-permute-done = f32[64,1,4096]{2,1,0:T(1,128)} collective-permute-done((f32[64,1,4096]{2,1,0:T(1,128)S(1)}, f32[64,1,4096]{2,1,0:T(1,128)}, u32[]{:S(2)}, u32[]{:S(2)}) %collective-permute-start) | collective-permute-done | bytes 1048608 | tf_op jit(solution)/shard_map/ppermute | solution.py:15
  36.4 17.5 %rev.4 = f32[64,1,4096]{2,1,0:T(1,128)} reverse(f32[64,1,4096]{2,1,0:T(1,128)} %get-tuple-element.8), dimensions={2} | reverse | bytes 2097152 | tf_op jit(solution)/shard_map/jit(_flip)/rev | solution.py:49
  54.5 10.2 %multiply_add_fusion.1 = f32[64,1,8192]{2,1,0:T(1,128)S(1)} fusion(f32[64,1,4096]{2,1,0:T(1,128)} %rev.4, s32[]{:T(128)S(6)} %select_n.193, f32[64,1,4096]{2,1,0:T(1,128)S(1)} %broadcast_in_dim.37, f32[64,1,4096]{2,1,0:T(1,128)S(1)} %get-tuple-element.7, f32[8192]{0:T(1024)S(1)} %pad_dynamic-slice_fusion.2, f32[8192]{0:T(1024)S(1)} %get-tuple-element.9, ...), kind=kLoop, calls=%fused_computation.44 | loop fusion | flops 2621440 | bytes 5341188 | tf_op jit(solution)/shard_map/add | solution.py:55
  65.8 7.4 %fusion.1 = f32[64,1,16384]{2,1,0:T(1,128)S(1)} fusion(pred[16384]{0:T(1024)(128)(4,1)S(1)} %get-tuple-element.12, pred[16384]{0:T(1024)(128)(4,1)S(1)} %get-tuple-element.11, f32[64,1,8192]{2,1,0:T(1,128)S(1)} %multiply_add_fusion.1, f32[64]{0:T(128)S(1)} %get-tuple-element.6, f32[64]{0:T(128)S(1)} %get-tuple-element.5), kind=kLoop, calls=%fused_computation.3 | loop fusion | flops 4194304 | bytes 6324736 | tf_op jit(solution)/shard_map/add | solution.py:68
  77.3 4.5 fusion.51
  81.8 5.0 %fusion.6 = f32[64,64,128]{2,0,1:T(8,128)S(1)} fusion(f32[128,64,128]{2,0,1:T(8,128)S(1)} %fusion.51, f32[128,64,128]{2,0,1:T(8,128)S(1)} %fusion.49, f32[128,128]{1,0:T(8,128)S(1)} %copy.51, f32[128,128]{1,0:T(8,128)S(1)} %copy.50), kind=kOutput, calls=%fused_computation.8 | convolution fusion | flops 809615360 | bytes 10616832 | tf_op jit(solution)/shard_map/mkb,bj->mjk/dot_general | solution.py:25
  86.8 5.0 %subtract_bitcast_fusion = f32[64,64,128]{2,1,0:T(8,128)S(1)} fusion(f32[64,64,128]{2,0,1:T(8,128)S(1)} %fusion.6, f32[128,64,128]{2,0,1:T(8,128)S(1)} %fusion.51, f32[128,64,128]{2,0,1:T(8,128)S(1)} %fusion.49, f32[128,128]{1,0:T(8,128)S(1)} %copy.51, f32[128,128]{1,0:T(8,128)S(1)} %copy.50), kind=kOutput, calls=%fused_computation.38 | convolution fusion | flops 810139648 | bytes 12713984 | tf_op jit(solution)/shard_map/mkb,bj->mjk/dot_general | solution.py:25
  101.7 8.0 %fusion.8 = f32[64,64,128]{2,0,1:T(8,128)S(1)} fusion(f32[128,64,128]{2,0,1:T(8,128)} %copy-done.2, f32[128,64,128]{2,0,1:T(8,128)} %copy-done, f32[128,128]{1,0:T(8,128)S(1)} %copy.51, f32[128,128]{1,0:T(8,128)S(1)} %copy.50), kind=kOutput, calls=%fused_computation.10 | convolution fusion | flops 809615360 | bytes 10616832 | tf_op jit(solution)/shard_map/mkb,bj->mjk/dot_general | solution.py:25
  109.8 6.3 %add_bitcast_fusion = f32[64,64,128]{2,1,0:T(8,128)} fusion(f32[64,64,128]{2,0,1:T(8,128)S(1)} %fusion.8, f32[128,64,128]{2,0,1:T(8,128)S(1)} %copy-done.3, f32[128,64,128]{2,0,1:T(8,128)S(1)} %copy-done.1, f32[128,128]{1,0:T(8,128)S(1)} %copy.51, f32[128,128]{1,0:T(8,128)S(1)} %copy.50), kind=kOutput, calls=%fused_computation.39 | convolution fusion | flops 810139648 | bytes 12713984 | tf_op jit(solution)/shard_map/mkb,bj->mjk/dot_general | solution.py:25
  126.0 4.5 all-to-all-start
  133.6 7.9 %reshape.330 = f32[8,1,65536]{2,1,0:T(1,128)} reshape(f32[2048,1,1,1,4,64]{5,4,3,2,1,0:T(4,128)} %bitcast.145) | data formatting | bytes 4194304
  141.4 13.4 %all-to-all-done = f32[1,64,1,1,4,2048]{5,1,3,2,0,4:T(8,128)} async-done(((f32[1,64,1,1,4,2048]{5,1,3,2,0,4:T(8,128)}), f32[1,64,1,1,4,2048]{5,1,3,2,0,4:T(8,128)}, u32[]{:S(2)}, u32[]{:S(2)}) %all-to-all-start) | async-done | bytes 2097184 | tf_op jit(solution)/shard_map/all_to_all | solution.py:186
  154.8 4.8 all-to-all-start.3
  159.6 4.8 copy.53
  164.3 7.8 %reshape.328 = f32[8,1,65536]{2,1,0:T(1,128)} reshape(f32[2048,1,1,1,4,64]{5,4,3,2,1,0:T(4,128)} %bitcast.146) | data formatting | bytes 4194304
  172.2 36.4 %all-to-all-done.3 = f32[8,1,65536]{2,1,0:T(1,128)S(1)} async-done(((f32[8,1,65536]{2,1,0:T(1,128)}), f32[8,1,65536]{2,1,0:T(1,128)S(1)}, u32[]{:S(2)}, u32[]{:S(2)}) %all-to-all-start.3) | async-done | bytes 2097184 | tf_op jit(solution)/shard_map/all_to_all | solution.py:192
  210.0 4.6 all-to-all-start.1
  216.0 7.1 %reduce.7 = f32[8,65536]{1,0:T(8,128)S(1)} reduce(f32[8,1,65536]{2,1,0:T(1,128)} %copy-done.6, f32[]{:T(128)} %broadcast.519), dimensions={1}, to_apply=%all_to_all.97.reduce_sub_computation | reduce | bytes 4194308 | tf_op jit(solution)/shard_map/all_to_all | solution.py:192
  223.2 4.8 reshape.331
  228.0 5.2 %copy.57 = f32[4,64,1,1,1,2048]{5,1,0,4,3,2:T(8,128)} copy(f32[4,64,1,1,1,2048]{1,0,4,3,2,5:T(4,128)} %bitcast.147) | data formatting | bytes 4194304 | tf_op jit(solution)/shard_map/all_to_all | solution.py:192
  233.1 30.5 %all-to-all-done.1 = f32[8,1,65536]{2,1,0:T(1,128)} async-done(((f32[8,1,65536]{2,1,0:T(1,128)}), f32[8,1,65536]{2,1,0:T(1,128)}, u32[]{:S(2)}, u32[]{:S(2)}) %all-to-all-start.1) | async-done | bytes 2097184 | tf_op jit(solution)/shard_map/all_to_all | solution.py:185
  263.6 7.1 %reduce.6 = f32[8,65536]{1,0:T(8,128)S(1)} reduce(f32[8,1,65536]{2,1,0:T(1,128)} %all-to-all-done.1, f32[]{:T(128)} %broadcast.519), dimensions={1}, to_apply=%all_to_all.92.reduce_sub_computation | reduce | bytes 4194308 | tf_op jit(solution)/shard_map/all_to_all | solution.py:185
  270.8 4.8 reshape.329
  292.5 4.6 all-to-all-start.6
  303.5 18.6 %all-to-all-done.6 = f32[4,64,8,1,1,256]{5,2,1,4,3,0:T(8,128)} async-done(((f32[4,64,8,1,1,256]{5,2,1,4,3,0:T(8,128)}), f32[4,64,8,1,1,256]{5,2,1,4,3,0:T(8,128)}, u32[]{:S(2)}, u32[]{:S(2)}) %all-to-all-start.6) | async-done | bytes 2097184 | tf_op jit(solution)/shard_map/all_to_all | solution.py:230
  329.3 20.8 %all-to-all-done.4 = f32[4,64,8,1,1,256]{5,2,1,4,3,0:T(8,128)S(1)} async-done(((f32[4,64,8,1,1,256]{5,2,1,4,3,0:T(8,128)}), f32[4,64,8,1,1,256]{5,2,1,4,3,0:T(8,128)S(1)}, u32[]{:S(2)}, u32[]{:S(2)}) %all-to-all-start.4) | async-done | bytes 2097184 | tf_op jit(solution)/shard_map/all_to_all | solution.py:221
  358.6 45.4 %all-to-all-done.7 = f32[1,64,8,1,4,256]{5,1,4,3,0,2:T(8,128)S(1)} async-done(((f32[1,64,8,1,4,256]{5,1,4,3,0,2:T(8,128)}), f32[1,64,8,1,4,256]{5,1,4,3,0,2:T(8,128)S(1)}, u32[]{:S(2)}, u32[]{:S(2)}) %all-to-all-start.7) | async-done | bytes 2097184 | tf_op jit(solution)/shard_map/all_to_all | solution.py:229
  404.0 4.4 all-to-all-start.5
  412.6 44.8 %all-to-all-done.5 = f32[1,64,8,1,4,256]{5,1,4,3,0,2:T(8,128)} async-done(((f32[1,64,8,1,4,256]{5,1,4,3,0,2:T(8,128)}), f32[1,64,8,1,4,256]{5,1,4,3,0,2:T(8,128)}, u32[]{:S(2)}, u32[]{:S(2)}) %all-to-all-start.5) | async-done | bytes 2097184 | tf_op jit(solution)/shard_map/all_to_all | solution.py:220
  479.2 4.9 fusion.2
  484.0 6.1 %subtract_multiply_fusion = f32[64,64,128]{2,0,1:T(8,128)} fusion(f32[64,64,128]{2,0,1:T(8,128)S(1)} %fusion.2, f32[128,64,128]{2,0,1:T(8,128)S(1)} %convolution_add_fusion.2, f32[128,64,128]{2,0,1:T(8,128)S(1)} %convolution_subtract_fusion.2, f32[128,128]{1,0:T(8,128)S(1)} %copy.51, f32[128,128]{1,0:T(8,128)S(1)} %copy.50), kind=kOutput, calls=%fused_computation.37 | convolution fusion | flops 809615360 | bytes 12713984 | tf_op jit(solution)/shard_map/mak,kb->mba/dot_general | solution.py:25
  (73 shorter events, 105.6 us)
Async XLA Ops:
  5.1 26.3 %collective-permute-start = (f32[64,1,4096]{2,1,0:T(1,128)S(1)}, f32[64,1,4096]{2,1,0:T(1,128)}, u32[]{:S(2)}, u32[]{:S(2)}) collective-permute-start(f32[64,1,4096]{2,1,0:T(1,128)S(1)} %constant_dynamic-slice_fusion), channel_id=1, source_target_pairs={{0,16},{8,24},{16,0},{24,8},{1,17},{9,25},{17,1},{25,9},{2,18},{10... | collective-permute-start | bytes 3145736 | tf_op jit(solution)/shard_map/ppermute | solution.py:15
  77.3 9.5 %copy-start = (f32[128,64,128]{2,0,1:T(8,128)}, f32[128,64,128]{2,0,1:T(8,128)S(1)}, u32[]{:S(2)}) copy-start(f32[128,64,128]{2,0,1:T(8,128)S(1)} %fusion.49) | copy-start | bytes 12582916
  81.8 5.0 %copy-start.2 = (f32[128,64,128]{2,0,1:T(8,128)}, f32[128,64,128]{2,0,1:T(8,128)S(1)}, u32[]{:S(2)}) copy-start(f32[128,64,128]{2,0,1:T(8,128)S(1)} %fusion.51) | copy-start | bytes 12582916
  97.8 28.2 %all-to-all-start.2 = ((f32[1,64,1,1,4,2048]{5,1,3,2,0,4:T(8,128)}), f32[1,64,1,1,4,2048]{5,1,3,2,0,4:T(8,128)S(1)}, u32[]{:S(2)}, u32[]{:S(2)}) async-start(f32[1,64,1,1,4,2048]{5,1,3,2,0,4:T(8,128)} %copy.55), calls=%async_computation.2 | async-start | bytes 4194304 | tf_op jit(solution)/shard_map/all_to_all | solution.py:193
  101.7 8.0 %copy-start.1 = (f32[128,64,128]{2,0,1:T(8,128)S(1)}, f32[128,64,128]{2,0,1:T(8,128)}, u32[]{:S(2)}) copy-start(f32[128,64,128]{2,0,1:T(8,128)} %copy-done) | copy-start | bytes 12582916
  101.7 8.0 %copy-start.3 = (f32[128,64,128]{2,0,1:T(8,128)S(1)}, f32[128,64,128]{2,0,1:T(8,128)}, u32[]{:S(2)}) copy-start(f32[128,64,128]{2,0,1:T(8,128)} %copy-done.2) | copy-start | bytes 12582916
  126.0 28.8 %all-to-all-start = ((f32[1,64,1,1,4,2048]{5,1,3,2,0,4:T(8,128)}), f32[1,64,1,1,4,2048]{5,1,3,2,0,4:T(8,128)}, u32[]{:S(2)}, u32[]{:S(2)}) async-start(f32[1,64,1,1,4,2048]{5,1,3,2,0,4:T(8,128)} %copy.52), calls=%async_computation | async-start | bytes 4194304 | tf_op jit(solution)/shard_map/all_to_all | solution.py:186
  154.8 53.8 %all-to-all-start.3 = ((f32[8,1,65536]{2,1,0:T(1,128)}), f32[8,1,65536]{2,1,0:T(1,128)S(1)}, u32[]{:S(2)}, u32[]{:S(2)}) async-start(f32[8,1,65536]{2,1,0:T(1,128)} %reshape.330), calls=%async_computation.3 | async-start | bytes 4194304 | tf_op jit(solution)/shard_map/all_to_all | solution.py:192
  208.6 1.3 copy-start.6
  210.0 53.6 %all-to-all-start.1 = ((f32[8,1,65536]{2,1,0:T(1,128)}), f32[8,1,65536]{2,1,0:T(1,128)}, u32[]{:S(2)}, u32[]{:S(2)}) async-start(f32[8,1,65536]{2,1,0:T(1,128)} %reshape.328), calls=%async_computation.1 | async-start | bytes 4194304 | tf_op jit(solution)/shard_map/all_to_all | solution.py:185
  283.6 3.2 copy-start.4
  292.5 29.6 %all-to-all-start.6 = ((f32[4,64,8,1,1,256]{5,2,1,4,3,0:T(8,128)}), f32[4,64,8,1,1,256]{5,2,1,4,3,0:T(8,128)}, u32[]{:S(2)}, u32[]{:S(2)}) async-start(f32[4,64,8,1,1,256]{5,2,1,4,3,0:T(8,128)} %bitcast.152), calls=%async_computation.6 | async-start | bytes 4194304 | tf_op jit(solution)/shard_map/all_to_all | solution.py:230
  322.1 28.0 %all-to-all-start.4 = ((f32[4,64,8,1,1,256]{5,2,1,4,3,0:T(8,128)}), f32[4,64,8,1,1,256]{5,2,1,4,3,0:T(8,128)S(1)}, u32[]{:S(2)}, u32[]{:S(2)}) async-start(f32[4,64,8,1,1,256]{5,2,1,4,3,0:T(8,128)} %bitcast.153), calls=%async_computation.4 | async-start | bytes 4194304 | tf_op jit(solution)/shard_map/all_to_all | solution.py:221
  350.0 1.3 copy-start.7
  351.4 52.6 %all-to-all-start.7 = ((f32[1,64,8,1,4,256]{5,1,4,3,0,2:T(8,128)}), f32[1,64,8,1,4,256]{5,1,4,3,0,2:T(8,128)S(1)}, u32[]{:S(2)}, u32[]{:S(2)}) async-start(f32[1,64,8,1,4,256]{5,1,4,3,0,2:T(8,128)} %copy.62), calls=%async_computation.7 | async-start | bytes 4194304 | tf_op jit(solution)/shard_map/all_to_all | solution.py:229
  404.0 53.4 %all-to-all-start.5 = ((f32[1,64,8,1,4,256]{5,1,4,3,0,2:T(8,128)}), f32[1,64,8,1,4,256]{5,1,4,3,0,2:T(8,128)}, u32[]{:S(2)}, u32[]{:S(2)}) async-start(f32[1,64,8,1,4,256]{5,1,4,3,0,2:T(8,128)} %copy.59), calls=%async_computation.5 | async-start | bytes 4194304 | tf_op jit(solution)/shard_map/all_to_all | solution.py:220
  464.3 3.6 copy-start.5
where the time goes:
time: 500 us; the launch traced here: 491 us
  waiting for transfers between devices  233 us (47%)
  local copies, waits for them, and re-layouts  102 us (20%)
  matrix products  73.3 us (15%)
  other arithmetic  41.8 us (8%)
  starting transfers between devices  37 us (7%)
    dot_general x12, matrix products, einsum_hi(): jnp.einsum(pattern, left_side, right_side, precision=lax.Precision.HIGHES...  58.5 us
    all_to_all x1, waiting for transfers between devices, local(): lax.all_to_all(lax.all_to_all(fixed_im.reshape(layout), 'angle', split_ax...  45.4 us
    all_to_all x1, waiting for transfers between devices, local(): lax.all_to_all(lax.all_to_all(fixed_re.reshape(layout), 'angle', split_ax...  44.8 us
    all_to_all x1, waiting for transfers between devices, local(): lax.all_to_all(lax.all_to_all(shaped_im, 'angle', split_axis=4, concat_ax...  36.4 us
    unnamed x24, local copies, waits for them, and re-layouts  32.4 us
    all_to_all x1, waiting for transfers between devices, local(): lax.all_to_all(lax.all_to_all(shaped_re, 'angle', split_axis=4, concat_ax...  30.5 us
    all_to_all x1, waiting for transfers between devices, local(): lax.all_to_all(fixed_re.reshape(layout), 'angle', split_axis=0, concat_ax...  20.8 us
    ppermute x1, waiting for transfers between devices, swapped(): return lax.ppermute(value, axis, pairs)  20.4 us
  transfers between devices with their start and end apart: 9, of which 9 were waited for; matrix products, arithmetic and copies ran while one was open for 17% of the time, Pallas kernels for 0%

commit v1 on v0

v1 whole, which is shorter than its diff:
```python
import functools
import math

import jax
import jax.numpy as jnp
import ml_dtypes
import numpy as np
from jax import lax
from jax.experimental import pallas as pl
from jax.experimental.pallas import tpu as pltpu
from jax.sharding import PartitionSpec as P

KMAX = 8
FCUT = 512
SIDE = 128
HALF_SIDE = SIDE // 2
QUARTER = SIDE // 4
MODES = 2 * KMAX
GROUP = 4
CHUNKS = (16, 16, 16, 16)
BF16 = jnp.bfloat16
F32 = jnp.float32


def swapped(value, axis, bit):
    mask = 2**bit
    pairs = [(source, source ^ mask) for source in range(lax.axis_size(axis))]
    return lax.ppermute(value, axis, pairs)


def np_split(table):
    high = table.astype(ml_dtypes.bfloat16)
    low = (table - high.astype(np.float64)).astype(ml_dtypes.bfloat16)
    return high, low


@functools.cache
def transform_tables():
    n = SIDE * SIDE
    a = np.arange(SIDE)
    k = np.arange(HALF_SIDE)
    angle = 2 * np.pi * (k[:, None] * a[None, :] % SIDE) / SIDE
    first = np.concatenate([np.cos(angle), -np.sin(angle)])
    first[HALF_SIDE] = 1.0 - 2.0 * (a % 2)
    first_hi, first_lo = np_split(first)
    head = slice(0, HALF_SIDE)
    tail = slice(HALF_SIDE, SIDE)
    first_pack = np.concatenate([first_hi[:, head], first_hi[:, head], first_lo[:, head]], axis=1)
    edge_pack = np.concatenate([first_hi[:, tail], first_lo[:, tail]], axis=1)
    bins = np.stack([k, np.where(k == 0, HALF_SIDE, k)]).reshape(-1)
    turn = 2 * np.pi * (bins[:, None] * a[None, :]) / n
    twiddle = np.concatenate([np.cos(turn), np.sin(turn)], axis=1).astype(np.float32)
    inner = 2 * np.pi * (a[:, None] * a[None, :] % SIDE) / SIDE
    c, s = np.cos(inner), np.sin(inner)
    forward_hi, forward_lo = np_split(np.block([[c, -s], [s, c]]))
    back_hi, back_lo = np_split(np.block([[c, s], [-s, c]]))
    forward = np.concatenate([forward_hi, forward_hi, forward_lo])
    back = np.concatenate([back_hi, back_hi, back_lo])
    f = bins[:, None] + SIDE * a[None, :]
    f = np.minimum(f, n - f).astype(np.float64)
    kept = n // 2
    ramp = f / kept * (1.0 + np.cos(np.pi * f / kept)) / n
    drop = 1.0 - 1.0 / (1.0 + (f / FCUT) ** 8)
    last = 2.0 * first[:, :HALF_SIDE].T
    last[:, 0] = 1.0
    last[:, HALF_SIDE] = 1.0 - 2.0 * (np.arange(HALF_SIDE) % 2)
    last_hi, last_lo = np_split(last)
    last_pack = np.concatenate([last_hi, last_hi, last_lo], axis=1)
    return {
        "first": first_pack,
        "edge": edge_pack,
        "twiddle": twiddle,
        "forward": forward,
        "back": back,
        "ramp": np.concatenate([ramp, ramp], axis=1).astype(np.float32),
        "ramp_drop": np.concatenate([ramp * drop, ramp * drop], axis=1).astype(np.float32),
        "last": last_pack,
    }


@functools.cache
def mode_basis(count, half_turn):
    order = np.arange(KMAX)
    angle = 2 * np.pi * (np.arange(count)[:, None] * order[None, :] % half_turn) / half_turn
    return np.concatenate([np.cos(angle), np.sin(angle)], axis=1)


def phase_rows(starts, half_turn):
    order = np.arange(KMAX)
    angle = 2 * np.pi * (np.asarray(starts)[:, None] * order[None, :] % half_turn) / half_turn
    return np.concatenate([np.cos(angle), np.sin(angle)], axis=1).astype(np.float32).reshape(-1)


def split(value):
    high = value.astype(BF16)
    low = (value - high.astype(F32)).astype(BF16)
    return high, low


def dot(left, right):
    return jnp.dot(left, right, preferred_element_type=F32)


def lanes_flipped(block):
    rows = block.shape[0]
    lane = SIDE - 1 - lax.broadcasted_iota(jnp.int32, (rows, SIDE), 1)
    turned = jnp.take_along_axis(block, lane, axis=1)
    row = rows - 1 - lax.broadcasted_iota(jnp.int32, (rows, SIDE), 0)
    return jnp.take_along_axis(turned, row, axis=0)


def flipped(sheet):
    blocks = [lanes_flipped(sheet[8 * i : 8 * i + 8]) for i in range(QUARTER // 8)]
    return jnp.concatenate(blocks[::-1], axis=0)


def swap_first_rows(upper_part, lower_part):
    row = lax.broadcasted_iota(jnp.int32, upper_part.shape, 0)
    return (
        jnp.where(row == 0, lower_part, upper_part),
        jnp.where(row == 0, upper_part, lower_part),
    )


def blend_weight(correlation, blend):
    position = (
        lax.broadcasted_iota(jnp.int32, (HALF_SIDE, SIDE), 0) * SIDE
        + lax.broadcasted_iota(jnp.int32, (HALF_SIDE, SIDE), 1)
    ).astype(F32)
    pixels = QUARTER * SIDE
    center = pixels - correlation.astype(F32) / 2.0
    return jnp.clip((position + 0.5 - center) / blend.astype(F32) + 0.5, 0.0, 1.0)


def edge_response(edge_table, padding):
    index = (
        lax.broadcasted_iota(jnp.int32, (HALF_SIDE, SIDE), 0) * SIDE
        + lax.broadcasted_iota(jnp.int32, (HALF_SIDE, SIDE), 1)
    )
    after = (index < padding).astype(F32)
    before = (index >= HALF_SIDE * SIDE - padding).astype(F32)
    boxes = jnp.concatenate([after, before], axis=1)
    boxes = jnp.concatenate([boxes, boxes], axis=0).astype(BF16)
    return dot(edge_table, boxes)


def transform_group(views, weight, correlation, edges, tables, gain, shifted, count):
    whole = correlation // SIDE
    part = correlation % SIDE
    lane = lax.broadcasted_iota(jnp.int32, (HALF_SIDE, SIDE), 1)
    in_row = lane < SIDE - part
    keep = 1.0 - weight[:QUARTER]
    stitched = []
    for i, (main, back) in enumerate(views):
        rolled = pltpu.roll(main, SIDE - part, 1)
        last = jnp.broadcast_to(main[QUARTER - 1 :, SIDE - 1 :], (QUARTER + 8, SIDE))
        shifted[i, QUARTER : 2 * QUARTER, :] = rolled
        shifted[i, 2 * QUARTER :, :] = last
        right = jnp.where(
            in_row,
            shifted[i, pl.ds(whole, HALF_SIDE), :],
            shifted[i, pl.ds(whole + 1, HALF_SIDE), :],
        )
        sheet = weight * right
        top = sheet[:QUARTER] + keep * flipped(back)
        stitched.append(jnp.concatenate([top, sheet[QUARTER:]], axis=0))
    high, low = split(jnp.concatenate(stitched, axis=1))
    grown = dot(tables["first"][...], jnp.concatenate([high, low, high], axis=0))
    after, before = edges[:, :SIDE], edges[:, SIDE:]
    cos_turn, sin_turn = tables["twiddle"][:, :SIDE], tables["twiddle"][:, SIDE:]
    real, imag = [], []
    for i, sheet in enumerate(stitched):
        ends = (
            grown[:, i * SIDE : (i + 1) * SIDE]
            + sheet[HALF_SIDE - 1 :, SIDE - 1 :] * after
            + sheet[:1, :1] * before
        )
        real.append(ends[:HALF_SIDE])
        imag.append(ends[HALF_SIDE:])
    for i in range(0, count, 2):
        imag[i], real[i + 1] = swap_first_rows(imag[i], real[i + 1])
    turned = []
    for i in range(count):
        rows = slice((i % 2) * HALF_SIDE, (i % 2 + 1) * HALF_SIDE)
        c, s = cos_turn[rows], sin_turn[rows]
        turned.append(jnp.concatenate([real[i] * c + imag[i] * s, imag[i] * c - real[i] * s], axis=1))
    high, low = split(jnp.concatenate(turned, axis=0))
    spectrum = dot(jnp.concatenate([high, low, high], axis=1), tables["forward"][...])
    gains = jnp.concatenate([gain[...]] * (count // 2), axis=0)
    high, low = split(spectrum * gains)
    inner = dot(jnp.concatenate([high, low, high], axis=1), tables["back"][...])
    real, imag = [], []
    for i in range(count):
        rows = slice((i % 2) * HALF_SIDE, (i % 2 + 1) * HALF_SIDE)
        c, s = cos_turn[rows], sin_turn[rows]
        block = inner[i * HALF_SIDE : (i + 1) * HALF_SIDE]
        real.append(block[:, :SIDE] * c - block[:, SIDE:] * s)
        imag.append(block[:, SIDE:] * c + block[:, :SIDE] * s)
    for i in range(0, count, 2):
        imag[i], real[i + 1] = swap_first_rows(imag[i], real[i + 1])
    columns = jnp.concatenate(
        [jnp.concatenate([real[i], imag[i]], axis=0) for i in range(count)], axis=1
    )
    high, low = split(columns)
    result = dot(tables["last"][...], jnp.concatenate([high, low, high], axis=0))
    return [result[:, i * SIDE : (i + 1) * SIDE] for i in range(count)]


TABLES = ("first", "edge", "twiddle", "forward", "back", "last")


def modes_kernel(halves, raw, flat, dark, phase, basis_hi, basis_lo, mine, other, total):
    step = pl.program_id(0)
    level = jnp.log(flat[...] - dark[...])
    projected = level - jnp.log(raw[...] - dark[...])
    count = raw.shape[0]
    columns = jnp.concatenate(
        [
            projected[:, 8 * i : 8 * i + 8, :].reshape(count * 8, SIDE)
            for i in range(QUARTER // 8)
        ],
        axis=1,
    )
    high, low = split(columns)
    partial = dot(basis_hi[...], high) + dot(basis_hi[...], low) + dot(basis_lo[...], high)

    @pl.when(step == 0)
    def _():
        total[...] = partial

    @pl.when(step > 0)
    def _():
        total[...] += partial

    @pl.when(step == pl.num_programs(0) - 1)
    def _():
        place = lax.axis_index("angle")
        base = (place % halves) * MODES
        odd = place % 2
        half = KMAX // 2
        for k in range(KMAX):
            c = phase[base + k]
            s = phase[base + KMAX + k]
            even_part = total[8 * k : 8 * k + 8, :]
            odd_part = total[8 * (KMAX + k) : 8 * (KMAX + k) + 8, :]
            cos_mode = even_part * c - odd_part * s
            sin_mode = odd_part * c + even_part * s
            low_half = k < half
            spot = k % half
            is_mine = (odd == 0) if low_half else (odd == 1)

            def put(ref):
                for i in range(QUARTER // 8):
                    lanes = slice(i * SIDE, (i + 1) * SIDE)
                    ref[spot, 8 * i : 8 * i + 8, :] = cos_mode[:, lanes]
                    ref[half + spot, 8 * i : 8 * i + 8, :] = sin_mode[:, lanes]

            @pl.when(is_mine)
            def _():
                put(mine)

            @pl.when(jnp.logical_not(is_mine))
            def _():
                put(other)


def filter_modes_kernel(
    halves, half_turn, mine, other_a, other_b, far_mine, far_other,
    correlation, blend, padding, cutoff, phase, *refs,
):
    names = TABLES + ("ramp_drop",)
    tables = dict(zip(names, refs))
    out_hi, out_lo, side, shifted, result = refs[len(names) :]
    place = lax.axis_index("angle")
    odd = place % 2
    upper = place // halves
    half = KMAX // 2
    side[upper, odd] = mine[...]
    side[upper, 1 - odd] = other_a[...] + other_b[...]
    side[1 - upper, odd] = far_mine[...]
    side[1 - upper, 1 - odd] = far_other[...]
    shifted[:, :QUARTER, :] = jnp.zeros((GROUP, QUARTER, SIDE), F32)
    weight = blend_weight(correlation[0], blend[0])
    edges = edge_response(tables["edge"][...], padding[0])
    for first in range(0, MODES, GROUP):
        views = [
            (side[0, m // KMAX, m % KMAX], side[1, m // KMAX, m % KMAX])
            for m in range(first, first + GROUP)
        ]
        sheets = transform_group(
            views, weight, correlation[0], edges, tables, tables["ramp_drop"], shifted, GROUP
        )
        for i, sheet in enumerate(sheets):
            result[first + i] = sheet
    base = place * MODES
    for k in range(KMAX):
        spot = (k // half) * KMAX + k % half
        scale = jnp.where(k < cutoff[0], (1.0 if k == 0 else 2.0) / half_turn, 0.0)
        c = phase[base + k] * scale
        s = phase[base + KMAX + k] * scale
        cos_sheet, sin_sheet = result[spot], result[spot + half]
        for row, sheet in (
            (k, cos_sheet * c + sin_sheet * s),
            (KMAX + k, sin_sheet * c - cos_sheet * s),
        ):
            high, low = split(sheet)
            for i in range(HALF_SIDE // 8):
                lanes = slice(i * SIDE, (i + 1) * SIDE)
                out_hi[8 * row : 8 * row + 8, lanes] = high[8 * i : 8 * i + 8]
                out_lo[8 * row : 8 * row + 8, lanes] = low[8 * i : 8 * i + 8]


def sheets_kernel(
    halves, offset, count, raw, partner, flat, dark,
    correlation, blend, padding, modes_hi, modes_lo, basis_hi, basis_lo, *refs,
):
    names = TABLES + ("ramp",)
    tables = dict(zip(names, refs))
    out, own, shifted, low, done, in_sem, out_sem = refs[-7:]
    place = lax.axis_index("angle")
    is_upper = place >= halves
    half_block = raw.shape[0] // 2
    start = jnp.where(is_upper, half_block, 0) + offset
    fetch = pltpu.make_async_copy(raw.at[pl.ds(start, count)], own, in_sem)
    fetch.start()
    shifted[:, :QUARTER, :] = jnp.zeros((GROUP, QUARTER, SIDE), F32)
    weight = blend_weight(correlation[0], blend[0])
    edges = edge_response(tables["edge"][...], padding[0])
    level = jnp.log(flat[...] - dark[...])
    low[...] = (
        dot(basis_hi[...], modes_hi[...])
        + dot(basis_hi[...], modes_lo[...])
        + dot(basis_lo[...], modes_hi[...])
    )
    fetch.wait()

    def project(sheet):
        return level - jnp.log(sheet - dark[...])

    def body(step, carry):
        first = step * GROUP
        views = []
        for i in range(GROUP):
            here, there = project(own[first + i]), project(partner[first + i])
            views.append((jnp.where(is_upper, there, here), jnp.where(is_upper, here, there)))
        sheets = transform_group(
            views, weight, correlation[0], edges, tables, tables["ramp"], shifted, GROUP
        )
        for i, sheet in enumerate(sheets):
            rows = pl.ds(pl.multiple_of((first + i) * 8, 8), 8)
            for j in range(HALF_SIDE // 8):
                done[first + i, 8 * j : 8 * j + 8, :] = (
                    sheet[8 * j : 8 * j + 8] - low[rows, j * SIDE : (j + 1) * SIDE]
                )
        return carry

    lax.fori_loop(0, count // GROUP, body, 0)
    store = pltpu.make_async_copy(done, out.at[pl.ds(offset, count)], out_sem)
    store.start()
    store.wait()


VMEM_SPEC = pl.BlockSpec(memory_space=pltpu.VMEM)
SMEM_SPEC = pl.BlockSpec(memory_space=pltpu.SMEM)
ANY_SPEC = pl.BlockSpec(memory_space=pl.ANY)
PARAMS = pltpu.CompilerParams(vmem_limit_bytes=40 * 2**20)


def partial_modes(raw, flat, dark, halves, half_turn):
    angles = raw.shape[0]
    block = 32
    steps = angles // block
    basis = mode_basis(angles, half_turn)
    spread = np.kron(basis.T, np.eye(8))
    hi, lo = np_split(spread)
    phase = phase_rows(np.arange(halves) * angles, half_turn)
    shape = jax.ShapeDtypeStruct((KMAX, QUARTER, SIDE), F32)
    whole = pl.BlockSpec((QUARTER, SIDE), lambda i: (0, 0))
    return pl.pallas_call(
        functools.partial(modes_kernel, halves),
        grid=(steps,),
        out_shape=(shape, shape),
        in_specs=[
            pl.BlockSpec((block, QUARTER, SIDE), lambda i: (i, 0, 0)),
            whole,
            whole,
            SMEM_SPEC,
            pl.BlockSpec((8 * MODES, 8 * block), lambda i: (0, i)),
            pl.BlockSpec((8 * MODES, 8 * block), lambda i: (0, i)),
        ],
        out_specs=[pl.BlockSpec((KMAX, QUARTER, SIDE), lambda i: (0, 0, 0))] * 2,
        scratch_shapes=[pltpu.VMEM((8 * MODES, QUARTER // 8 * SIDE), F32)],
        compiler_params=PARAMS,
        name="partial_modes",
    )(raw, flat, dark, jnp.asarray(phase), jnp.asarray(hi), jnp.asarray(lo))


def filtered_modes(parts, scalars, halves, half_turn, half_block):
    tables = transform_tables()
    place = np.arange(2 * halves)
    starts = place % halves * 2 * half_block + place // halves * half_block
    phase = phase_rows(starts, half_turn)
    shape = jax.ShapeDtypeStruct((8 * MODES, HALF_SIDE // 8 * SIDE), BF16)
    names = TABLES + ("ramp_drop",)
    return pl.pallas_call(
        functools.partial(filter_modes_kernel, halves, half_turn),
        out_shape=(shape, shape),
        in_specs=[VMEM_SPEC] * 5 + [SMEM_SPEC] * 5 + [VMEM_SPEC] * len(names),
        out_specs=(VMEM_SPEC, VMEM_SPEC),
        scratch_shapes=[
            pltpu.VMEM((2, 2, KMAX, QUARTER, SIDE), F32),
            pltpu.VMEM((GROUP, 3 * QUARTER + 8, SIDE), F32),
            pltpu.VMEM((MODES, HALF_SIDE, SIDE), F32),
        ],
        compiler_params=PARAMS,
        name="filtered_modes",
    )(*parts, *scalars, jnp.asarray(phase), *(jnp.asarray(tables[name]) for name in names))


def filtered_sheets(raw, partner, flat, dark, scalars, modes, out, offset, halves, half_turn):
    tables = transform_tables()
    count = partner.shape[0]
    half_block = raw.shape[0] // 2
    basis = mode_basis(half_block, half_turn)[offset : offset + count]
    hi, lo = np_split(np.kron(basis, np.eye(8)))
    names = TABLES + ("ramp",)
    operands = [raw, partner, flat, dark, *scalars, *modes, jnp.asarray(hi), jnp.asarray(lo)]
    operands += [jnp.asarray(tables[name]) for name in names]
    specs = [ANY_SPEC] + [VMEM_SPEC] * 3 + [SMEM_SPEC] * 3 + [VMEM_SPEC] * (4 + len(names))
    aliases = {}
    if out is not None:
        aliases = {len(operands): 0}
        operands.append(out)
        specs.append(ANY_SPEC)
    return pl.pallas_call(
        functools.partial(sheets_kernel, halves, offset, count),
        out_shape=jax.ShapeDtypeStruct((half_block, HALF_SIDE, SIDE), F32),
        in_specs=specs,
        out_specs=ANY_SPEC,
        scratch_shapes=[
            pltpu.VMEM((count, QUARTER, SIDE), F32),
            pltpu.VMEM((GROUP, 3 * QUARTER + 8, SIDE), F32),
            pltpu.VMEM((8 * count, HALF_SIDE // 8 * SIDE), F32),
            pltpu.VMEM((count, HALF_SIDE, SIDE), F32),
            pltpu.SemaphoreType.DMA,
            pltpu.SemaphoreType.DMA,
        ],
        input_output_aliases=aliases,
        compiler_params=PARAMS,
        name="filtered_sheets",
    )(*operands)


def local(intensity, flat_field, dark_field, correlation, blend_width, padding, cutoff):
    angle_count = lax.axis_size("angle")
    angle_place = lax.axis_index("angle")
    halves = angle_count // 2
    top_bit = angle_count.bit_length() - 2
    angles, local_rows, pixels = intensity.shape
    half_block = angles // 2
    half_turn = half_block * angle_count
    raw = intensity.reshape(angles, QUARTER, SIDE)
    flat = flat_field.reshape(QUARTER, SIDE)
    dark = dark_field.reshape(QUARTER, SIDE)
    send_from = jnp.where(angle_place >= halves, 0, half_block)
    partners = []
    offset = 0
    for count in CHUNKS:
        outgoing = lax.dynamic_slice_in_dim(raw, send_from + offset, count, 0)
        partners.append(swapped(outgoing, "angle", top_bit))
        offset += count
    mine, other = partial_modes(raw, flat, dark, halves, half_turn)
    for bit in range(1, top_bit):
        mine = mine + swapped(mine, "angle", bit)
        other = other + swapped(other, "angle", bit)
    mine_sum = mine + swapped(other, "angle", 0)
    other_more = swapped(mine, "angle", 0)
    far_mine = swapped(mine_sum, "angle", top_bit)
    far_other = swapped(far_mine, "angle", 0)
    scalars = (correlation, blend_width, padding)
    modes = filtered_modes(
        (mine_sum, other, other_more, far_mine, far_other),
        scalars + (cutoff,), halves, half_turn, half_block,
    )
    out = None
    offset = 0
    for count, partner in zip(CHUNKS, partners):
        out = filtered_sheets(
            raw, partner, flat, dark, scalars, modes, out, offset, halves, half_turn
        )
        offset += count
    return out.reshape(half_block, local_rows, 2 * pixels)


def solution(mesh):
    placed = (P("angle", "row", None), P("row", None), P("row", None), P(), P(), P(), P())
    return jax.shard_map(
        local, mesh=mesh, in_specs=placed, out_specs=P("angle", "row", None), check_vma=False
    )
```

time: 500 us -> 55.6 us (0.11); the launches traced: 491 us -> 55.2 us
  waiting for transfers between devices: 233 us -> 4.94 us
  local copies, waits for them, and re-layouts: 102 us -> 5.78 us
  matrix products: 73.3 us -> 0 us
  other arithmetic: 41.8 us -> 0.99 us
  Pallas kernels: 0 us -> 29.3 us
  starting transfers between devices: 37 us -> 11.2 us
    all_to_all x8 -> x0, waiting for transfers between devices: 213 us -> none  [the longest x1 45.4 us: local(): lax.all_to_all(lax.all_to_all(fixed_im.reshape(layout), 'angle', split_ax...]
    dot_general x20 -> x0, matrix products: 73.3 us -> none  [the longest x12 58.5 us: einsum_hi(): jnp.einsum(pattern, left_side, right_side, precision=lax.Precision.HIGHES...]
    all_to_all x8 -> x0, starting transfers between devices: 33.9 us -> none  [the longest x1 4.78 us: local(): lax.all_to_all(lax.all_to_all(shaped_im, 'angle', split_axis=4, concat_ax...]
    all_to_all x9 -> x0, local copies, waits for them, and re-layouts: 31.4 us -> none  [the longest x1 5.16 us: local(): lax.all_to_all(lax.all_to_all(shaped_im, 'angle', split_axis=4, concat_ax...]
    pallas_call x0 -> x6, Pallas kernels: none -> 29.3 us  [the longest x4 22.2 us: filtered_sheets(): pl.pallas_call(functools.partial(sheets_kernel, halves, offset, count), o...]
    unnamed x24 -> x52, local copies, waits for them, and re-layouts: 32.4 us -> 5.69 us
    rev x1 -> x0, local copies, waits for them, and re-layouts: 17.5 us -> none  [stitch(): left_side = jnp.concatenate([jnp.flip(back_view, -1), empty], axis=-1)]
    add x5 -> x1, other arithmetic: 17.7 us -> 0.99 us  [local(): mine_sum = mine + swapped(other, 'angle', 0)]
  transfers between devices with their start and end apart: 9 -> 8, of which waited for: 9 -> 3; matrix products, arithmetic and copies ran while one was open for 17% -> 2% of each run, Pallas kernels for 0% -> 38%
where the time goes in v1:
time: 55.6 us; the launch traced here: 55.2 us
  Pallas kernels  29.3 us (53%)
  starting transfers between devices  11.2 us (20%)
  local copies, waits for them, and re-layouts  5.78 us (10%)
  waiting for transfers between devices  4.94 us (9%)
  between operations  2.92 us (5%)
  other arithmetic  0.99 us (2%)
    pallas_call x4, Pallas kernels, filtered_sheets(): pl.pallas_call(functools.partial(sheets_kernel, halves, offset, count), o...  22.2 us
    ppermute x8, starting transfers between devices, swapped(): return lax.ppermute(value, axis, pairs)  11.2 us
    unnamed x52, local copies, waits for them, and re-layouts  5.69 us
    ppermute x8, waiting for transfers between devices, swapped(): return lax.ppermute(value, axis, pairs)  4.94 us
    pallas_call x1, Pallas kernels, filtered_modes(): pl.pallas_call(functools.partial(filter_modes_kernel, halves, half_turn),...  4.09 us
    pallas_call x1, Pallas kernels, partial_modes(): pl.pallas_call(functools.partial(modes_kernel, halves), grid=(steps,), ou...  3.08 us
  transfers between devices with their start and end apart: 8, of which 3 were waited for; matrix products, arithmetic and copies ran while one was open for 2% of the time, Pallas kernels for 38%

profile of v1, /device:TPU:0, one launch (start us, length us, event | category | flops | bytes accessed | tf_op | source)
XLA Modules:
  0.0 55.2 jit_solution(4529141722150337529)
XLA Ops:
  0.0 1.6 %copy-done = f32[128,1,4096]{2,1,0:T(1,128)S(1)} copy-done((f32[128,1,4096]{2,1,0:T(1,128)S(1)}, f32[128,1,4096]{2,1,0:T(1,128)}, u32[]{:S(2)}) %copy-start) | copy-done | bytes 2097176
  1.6 0.7 %copy-done.9 = f32[1,4096]{1,0:T(1,128)S(1)} copy-done((f32[1,4096]{1,0:T(1,128)S(1)}, f32[1,4096]{1,0:T(1,128)}, u32[]{:S(2)}) %copy-start.9) | copy-done | bytes 16408
  2.3 0.7 %copy-done.11 = f32[1,4096]{1,0:T(1,128)S(1)} copy-done((f32[1,4096]{1,0:T(1,128)S(1)}, f32[1,4096]{1,0:T(1,128)}, u32[]{:S(2)}) %copy-start.11) | copy-done | bytes 16408
  3.0 0.9 %copy-done.13 = bf16[128,1024]{1,0:T(8,128)(2,1)S(1)} copy-done((bf16[128,1024]{1,0:T(8,128)(2,1)S(1)}, bf16[128,1024]{1,0:T(8,128)(2,1)}, u32[]{:S(2)}) %copy-start.13) | copy-done | bytes 262168
  4.0 0.9 %copy-done.14 = bf16[128,1024]{1,0:T(8,128)(2,1)S(1)} copy-done((bf16[128,1024]{1,0:T(8,128)(2,1)S(1)}, bf16[128,1024]{1,0:T(8,128)(2,1)}, u32[]{:S(2)}) %copy-start.14) | copy-done | bytes 262168
  4.9 0.7 %copy-done.25 = f32[32]{0:T(128)S(1)} copy-done((f32[32]{0:T(128)S(1)}, f32[32]{0:T(128)}, u32[]{:S(2)}) %copy-start.25) | copy-done | bytes 152
  5.6 0.0 copy-start.7
  5.6 0.0 copy-start.8
  5.6 0.0 copy-start.15
  5.6 3.1 %partial_modes.1 = (f32[8,32,128]{2,1,0:T(8,128)}, f32[8,32,128]{2,1,0:T(8,128)S(1)}) custom-call(f32[128,32,128]{2,1,0:T(8,128)S(1)} %bitcast.4, f32[32,128]{1,0:T(8,128)S(1)} %bitcast.10, f32[32,128]{1,0:T(8,128)S(1)} %bitcast.15, f32[32]{0:T(128)S(1)} %copy-done.25, bf16[128,1024]{1,0:T(8,128)(2,1)S(1)} %copy-done.14, bf16[128,1024]{1,0:T(8,128)(2,1)S(1)} %copy-done.13), custom_call_target="tpu_custom_call" | custom-call | tf_op jit(solution)/shard_map/partial_modes/pallas_call | solution.py:379
  8.7 2.9 %collective-permute-start.1 = (f32[8,32,128]{2,1,0:T(8,128)S(1)}, f32[8,32,128]{2,1,0:T(8,128)}, u32[]{:S(2)}, u32[]{:S(2)}) collective-permute-start(f32[8,32,128]{2,1,0:T(8,128)S(1)} %get-tuple-element.10.other_a), channel_id=1, source_target_pairs={{0,8},{8,0},{16,24},{24,16},{1,9},{9,1},{17,25},{25,17},{2,10},{10... | collective-permute-start | bytes 393224 | tf_op jit(solution)/shard_map/ppermute | solution.py:28
  11.7 0.0 collective-permute-start.2
  11.7 0.0 copy-start.22
  11.7 0.0 copy-start.23
  11.7 4.4 %collective-permute-done.1 = f32[8,32,128]{2,1,0:T(8,128)} collective-permute-done((f32[8,32,128]{2,1,0:T(8,128)S(1)}, f32[8,32,128]{2,1,0:T(8,128)}, u32[]{:S(2)}, u32[]{:S(2)}) %collective-permute-start.1) | collective-permute-done | bytes 131104 | tf_op jit(solution)/shard_map/ppermute | solution.py:28
  16.1 1.0 %add.30.mine = f32[8,32,128]{2,1,0:T(8,128)S(1)} add(f32[8,32,128]{2,1,0:T(8,128)} %get-tuple-element.9, f32[8,32,128]{2,1,0:T(8,128)} %collective-permute-done.1) | non-fusion elementwise | flops 32768 | bytes 393216 | tf_op jit(solution)/shard_map/add | solution.py:476
  17.1 2.1 %collective-permute-start.3 = (f32[8,32,128]{2,1,0:T(8,128)S(1)}, f32[8,32,128]{2,1,0:T(8,128)S(1)}, u32[]{:S(2)}, u32[]{:S(2)}) collective-permute-start(f32[8,32,128]{2,1,0:T(8,128)S(1)} %add.30.mine), channel_id=1, source_target_pairs={{0,16},{8,24},{16,0},{24,8},{1,17},{9,25},{17,1},{25,9},{2,18},{10... | collective-permute-start | bytes 393224 | tf_op jit(solution)/shard_map/ppermute | solution.py:28
  19.2 0.1 constant_dynamic-slice_fusion
  19.3 0.1 collective-permute-start.7
  19.4 2.0 %collective-permute-start.6 = (f32[16,32,128]{2,1,0:T(8,128)S(1)}, f32[16,32,128]{2,1,0:T(8,128)S(1)}, u32[]{:S(2)}, u32[]{:S(2)}) collective-permute-start(f32[16,32,128]{2,1,0:T(8,128)S(1)} %get-tuple-element.14), channel_id=1, source_target_pairs={{0,16},{8,24},{16,0},{24,8},{1,17},{9,25},{17,1},{25,9},{2,18},{10... | collective-permute-start | bytes 786440 | tf_op jit(solution)/shard_map/ppermute | solution.py:28
  21.4 0.1 collective-permute-start.5
  21.5 1.9 %collective-permute-start = (f32[16,32,128]{2,1,0:T(8,128)S(1)}, f32[16,32,128]{2,1,0:T(8,128)S(1)}, u32[]{:S(2)}, u32[]{:S(2)}) collective-permute-start(f32[16,32,128]{2,1,0:T(8,128)S(1)} %get-tuple-element.16), channel_id=1, source_target_pairs={{0,16},{8,24},{16,0},{24,8},{1,17},{9,25},{17,1},{25,9},{2,18},{10... | collective-permute-start | bytes 786440 | tf_op jit(solution)/shard_map/ppermute | solution.py:28
  23.5 0.2 collective-permute-done.3.far_mine
  23.7 2.0 %collective-permute-start.4 = (f32[8,32,128]{2,1,0:T(8,128)S(1)}, f32[8,32,128]{2,1,0:T(8,128)S(1)}, u32[]{:S(2)}, u32[]{:S(2)}) collective-permute-start(f32[8,32,128]{2,1,0:T(8,128)S(1)} %collective-permute-done.3.far_mine), channel_id=1, source_target_pairs={{0,8},{8,0},{16,24},{24,16},{1,9},{9,1},{17,25},{25,17},{2,10},{10... | collective-permute-start | bytes 393224 | tf_op jit(solution)/shard_map/ppermute | solution.py:28
  28.3 0.4 collective-permute-done.4.far_other
  28.7 4.1 %filtered_modes.1 = (bf16[128,1024]{1,0:T(8,128)(2,1)S(1)}, bf16[128,1024]{1,0:T(8,128)(2,1)S(1)}) custom-call(f32[8,32,128]{2,1,0:T(8,128)S(1)} %add.30.mine, f32[8,32,128]{2,1,0:T(8,128)S(1)} %get-tuple-element.10.other_a, f32[8,32,128]{2,1,0:T(8,128)S(1)} %collective-permute-done.2.other_b, f32[8,32,128]{2,1,0:T(8,128)S(1)} %collective-permute-done.3.far_mine, ...), custom_call_target="tpu_custom_call" | custom-call | tf_op jit(solution)/shard_map/filtered_modes/pallas_call | solution.py:405
  32.8 0.0 copy-start.20
  32.9 0.0 copy-start.21
  32.9 5.5 %filtered_sheets.4.refs_7_ = f32[64,64,128]{2,1,0:T(8,128)} custom-call(f32[128,32,128]{2,1,0:T(8,128)S(1)} %bitcast.6, f32[16,32,128]{2,1,0:T(8,128)S(1)} %collective-permute-done.7.partner, f32[32,128]{1,0:T(8,128)S(1)} %bitcast.11, f32[32,128]{1,0:T(8,128)S(1)} %bitcast.16, s32[1]{0:T(128)S(6)} %copy.35.correlation, s32[1]{0:T(128)S(6)} %copy.36.blend, ...), custom_call_target="tpu_custom_call" | custom-call | tf_op jit(solution)/shard_map/filtered_sheets/pallas_call | solution.py:435
  38.5 5.5 %filtered_sheets.5.refs_7_ = f32[64,64,128]{2,1,0:T(8,128)} custom-call(f32[128,32,128]{2,1,0:T(8,128)S(1)} %bitcast.7, f32[16,32,128]{2,1,0:T(8,128)S(1)} %collective-permute-done.6.partner, f32[32,128]{1,0:T(8,128)S(1)} %bitcast.12, f32[32,128]{1,0:T(8,128)S(1)} %bitcast.17, s32[1]{0:T(128)S(6)} %copy.35.correlation, ...), custom_call_target="tpu_custom_call", output_to_operand_aliasing={{}: (18, {})} | custom-call | tf_op jit(solution)/shard_map/filtered_sheets/pallas_call | solution.py:435
  44.1 5.5 %filtered_sheets.6.refs_7_ = f32[64,64,128]{2,1,0:T(8,128)} custom-call(f32[128,32,128]{2,1,0:T(8,128)S(1)} %bitcast.8, f32[16,32,128]{2,1,0:T(8,128)S(1)} %collective-permute-done.5.partner, f32[32,128]{1,0:T(8,128)S(1)} %bitcast.13, f32[32,128]{1,0:T(8,128)S(1)} %bitcast.18, s32[1]{0:T(128)S(6)} %copy.35.correlation, ...), custom_call_target="tpu_custom_call", output_to_operand_aliasing={{}: (18, {})} | custom-call | tf_op jit(solution)/shard_map/filtered_sheets/pallas_call | solution.py:435
  49.7 5.5 %filtered_sheets.7 = f32[64,64,128]{2,1,0:T(8,128)} custom-call(f32[128,32,128]{2,1,0:T(8,128)S(1)} %bitcast.9, f32[16,32,128]{2,1,0:T(8,128)S(1)} %collective-permute-done.partner, f32[32,128]{1,0:T(8,128)S(1)} %bitcast.14, f32[32,128]{1,0:T(8,128)S(1)} %bitcast.19, s32[1]{0:T(128)S(6)} %copy.35.correlation, ...), custom_call_target="tpu_custom_call", output_to_operand_aliasing={{}: (18, {})} | custom-call | tf_op jit(solution)/shard_map/filtered_sheets/pallas_call | solution.py:435
  (44 shorter events, 0.1 us)
Async XLA Ops:
  0.0 1.6 %copy-start = (f32[128,1,4096]{2,1,0:T(1,128)S(1)}, f32[128,1,4096]{2,1,0:T(1,128)}, u32[]{:S(2)}) copy-start(f32[128,1,4096]{2,1,0:T(1,128)} %param.27) | copy-start | bytes 6291460
  1.6 0.7 %copy-start.9 = (f32[1,4096]{1,0:T(1,128)S(1)}, f32[1,4096]{1,0:T(1,128)}, u32[]{:S(2)}) copy-start(f32[1,4096]{1,0:T(1,128)} %param.28) | copy-start | bytes 49156
  3.0 0.9 %copy-start.13 = (bf16[128,1024]{1,0:T(8,128)(2,1)S(1)}, bf16[128,1024]{1,0:T(8,128)(2,1)}, u32[]{:S(2)}) copy-start(bf16[128,1024]{1,0:T(8,128)(2,1)} %constant.67.clone.basis_lo) | copy-start | bytes 786436
  4.0 0.9 %copy-start.14 = (bf16[128,1024]{1,0:T(8,128)(2,1)S(1)}, bf16[128,1024]{1,0:T(8,128)(2,1)}, u32[]{:S(2)}) copy-start(bf16[128,1024]{1,0:T(8,128)(2,1)} %constant.66.clone.basis_hi) | copy-start | bytes 786436
  5.6 13.7 %copy-start.1 = (f32[128,1,4096]{2,1,0:T(1,128)S(1)}, f32[128,1,4096]{2,1,0:T(1,128)}, u32[]{:S(2)}) copy-start(f32[128,1,4096]{2,1,0:T(1,128)} %param.27) | copy-start | bytes 6291460
  5.6 23.0 %copy-start.2 = (bf16[768,256]{1,0:T(8,128)(2,1)S(1)}, bf16[768,256]{1,0:T(8,128)(2,1)}, u32[]{:S(2)}) copy-start(bf16[768,256]{1,0:T(8,128)(2,1)} %constant.73.clone.refs_4_) | copy-start | bytes 1179652
  5.6 23.0 %copy-start.3 = (bf16[768,256]{1,0:T(8,128)(2,1)S(1)}, bf16[768,256]{1,0:T(8,128)(2,1)}, u32[]{:S(2)}) copy-start(bf16[768,256]{1,0:T(8,128)(2,1)} %constant.72.clone.refs_3_) | copy-start | bytes 1179652
  5.6 23.0 %copy-start.4 = (f32[128,256]{1,0:T(8,128)S(1)}, f32[128,256]{1,0:T(8,128)}, u32[]{:S(2)}) copy-start(f32[128,256]{1,0:T(8,128)} %constant.71.clone.refs_2_) | copy-start | bytes 393220
  5.6 23.0 %copy-start.6 = (bf16[128,192]{1,0:T(8,128)(2,1)S(1)}, bf16[128,192]{1,0:T(8,128)(2,1)}, u32[]{:S(2)}) copy-start(bf16[128,192]{1,0:T(8,128)(2,1)} %constant.69.clone.refs_0_) | copy-start | bytes 147460
  5.6 23.0 %copy-start.7 = (bf16[64,384]{1,0:T(8,128)(2,1)S(1)}, bf16[64,384]{1,0:T(8,128)(2,1)}, u32[]{:S(2)}) copy-start(bf16[64,384]{1,0:T(8,128)(2,1)} %constant.74.clone.refs_5_) | copy-start | bytes 147460
  5.6 23.0 %copy-start.8 = (bf16[128,128]{1,0:T(8,128)(2,1)S(1)}, bf16[128,128]{1,0:T(8,128)(2,1)}, u32[]{:S(2)}) copy-start(bf16[128,128]{1,0:T(8,128)(2,1)} %constant.70.clone.refs_1_) | copy-start | bytes 98308
  5.6 23.0 %copy-start.15 = (f32[128,256]{1,0:T(8,128)S(1)}, f32[128,256]{1,0:T(8,128)}, u32[]{:S(2)}) copy-start(f32[128,256]{1,0:T(8,128)} %constant.75.clone.refs_6_) | copy-start | bytes 393220
  8.7 7.4 %collective-permute-start.1 = (f32[8,32,128]{2,1,0:T(8,128)S(1)}, f32[8,32,128]{2,1,0:T(8,128)}, u32[]{:S(2)}, u32[]{:S(2)}) collective-permute-start(f32[8,32,128]{2,1,0:T(8,128)S(1)} %get-tuple-element.10.other_a), channel_id=1, source_target_pairs={{0,8},{8,0},{16,24},{24,16},{1,9},{9,1},{17,25},{25,17},{2,10},{10... | collective-permute-start | bytes 393224 | tf_op jit(solution)/shard_map/ppermute | solution.py:28
  11.7 9.8 %collective-permute-start.2 = (f32[8,32,128]{2,1,0:T(8,128)}, f32[8,32,128]{2,1,0:T(8,128)S(1)}, u32[]{:S(2)}, u32[]{:S(2)}) collective-permute-start(f32[8,32,128]{2,1,0:T(8,128)} %get-tuple-element.9), channel_id=1, source_target_pairs={{0,8},{8,0},{16,24},{24,16},{1,9},{9,1},{17,25},{25,17},{2,10},{10... | collective-permute-start | bytes 393224 | tf_op jit(solution)/shard_map/ppermute | solution.py:28
  11.7 17.0 %copy-start.24 = (f32[64]{0:T(128)S(1)}, f32[64]{0:T(128)}, u32[]{:S(2)}) copy-start(f32[64]{0:T(128)} %constant.68.clone.phase) | copy-start | bytes 772
  11.7 21.1 %copy-start.5 = (f32[128,256]{1,0:T(8,128)S(1)}, f32[128,256]{1,0:T(8,128)}, u32[]{:S(2)}) copy-start(f32[128,256]{1,0:T(8,128)} %constant.78.clone.refs_6_) | copy-start | bytes 393220
  11.7 21.1 %copy-start.10 = (f32[1,4096]{1,0:T(1,128)S(1)}, f32[1,4096]{1,0:T(1,128)}, u32[]{:S(2)}) copy-start(f32[1,4096]{1,0:T(1,128)} %param.28) | copy-start | bytes 49156
  11.7 21.1 %copy-start.12 = (f32[1,4096]{1,0:T(1,128)S(1)}, f32[1,4096]{1,0:T(1,128)}, u32[]{:S(2)}) copy-start(f32[1,4096]{1,0:T(1,128)} %param.29) | copy-start | bytes 49156
  11.7 21.1 %copy-start.22 = (bf16[128,128]{1,0:T(8,128)(2,1)S(1)}, bf16[128,128]{1,0:T(8,128)(2,1)}, u32[]{:S(2)}) copy-start(bf16[128,128]{1,0:T(8,128)(2,1)} %constant.77.clone.basis_lo) | copy-start | bytes 98308
  11.7 21.1 %copy-start.23 = (bf16[128,128]{1,0:T(8,128)(2,1)S(1)}, bf16[128,128]{1,0:T(8,128)(2,1)}, u32[]{:S(2)}) copy-start(bf16[128,128]{1,0:T(8,128)(2,1)} %constant.76.clone.basis_hi) | copy-start | bytes 98308
  17.1 6.6 %collective-permute-start.3 = (f32[8,32,128]{2,1,0:T(8,128)S(1)}, f32[8,32,128]{2,1,0:T(8,128)S(1)}, u32[]{:S(2)}, u32[]{:S(2)}) collective-permute-start(f32[8,32,128]{2,1,0:T(8,128)S(1)} %add.30.mine), channel_id=1, source_target_pairs={{0,16},{8,24},{16,0},{24,8},{1,17},{9,25},{17,1},{25,9},{2,18},{10... | collective-permute-start | bytes 393224 | tf_op jit(solution)/shard_map/ppermute | solution.py:28
  19.3 13.4 %collective-permute-start.7 = (f32[16,32,128]{2,1,0:T(8,128)S(1)}, f32[16,32,128]{2,1,0:T(8,128)S(1)}, u32[]{:S(2)}, u32[]{:S(2)}) collective-permute-start(f32[16,32,128]{2,1,0:T(8,128)S(1)} %get-tuple-element.13), channel_id=1, source_target_pairs={{0,16},{8,24},{16,0},{24,8},{1,17},{9,25},{17,1},{25,9},{2,18},{10... | collective-permute-start | bytes 786440 | tf_op jit(solution)/shard_map/ppermute | solution.py:28
  19.4 19.0 %collective-permute-start.6 = (f32[16,32,128]{2,1,0:T(8,128)S(1)}, f32[16,32,128]{2,1,0:T(8,128)S(1)}, u32[]{:S(2)}, u32[]{:S(2)}) collective-permute-start(f32[16,32,128]{2,1,0:T(8,128)S(1)} %get-tuple-element.14), channel_id=1, source_target_pairs={{0,16},{8,24},{16,0},{24,8},{1,17},{9,25},{17,1},{25,9},{2,18},{10... | collective-permute-start | bytes 786440 | tf_op jit(solution)/shard_map/ppermute | solution.py:28
  21.4 22.6 %collective-permute-start.5 = (f32[16,32,128]{2,1,0:T(8,128)S(1)}, f32[16,32,128]{2,1,0:T(8,128)S(1)}, u32[]{:S(2)}, u32[]{:S(2)}) collective-permute-start(f32[16,32,128]{2,1,0:T(8,128)S(1)} %get-tuple-element.15), channel_id=1, source_target_pairs={{0,16},{8,24},{16,0},{24,8},{1,17},{9,25},{17,1},{25,9},{2,18},{10... | collective-permute-start | bytes 786440 | tf_op jit(solution)/shard_map/ppermute | solution.py:28
  21.5 28.1 %collective-permute-start = (f32[16,32,128]{2,1,0:T(8,128)S(1)}, f32[16,32,128]{2,1,0:T(8,128)S(1)}, u32[]{:S(2)}, u32[]{:S(2)}) collective-permute-start(f32[16,32,128]{2,1,0:T(8,128)S(1)} %get-tuple-element.16), channel_id=1, source_target_pairs={{0,16},{8,24},{16,0},{24,8},{1,17},{9,25},{17,1},{25,9},{2,18},{10... | collective-permute-start | bytes 786440 | tf_op jit(solution)/shard_map/ppermute | solution.py:28
  23.7 5.0 %collective-permute-start.4 = (f32[8,32,128]{2,1,0:T(8,128)S(1)}, f32[8,32,128]{2,1,0:T(8,128)S(1)}, u32[]{:S(2)}, u32[]{:S(2)}) collective-permute-start(f32[8,32,128]{2,1,0:T(8,128)S(1)} %collective-permute-done.3.far_mine), channel_id=1, source_target_pairs={{0,8},{8,0},{16,24},{24,16},{1,9},{9,1},{17,25},{25,17},{2,10},{10... | collective-permute-start | bytes 393224 | tf_op jit(solution)/shard_map/ppermute | solution.py:28
  32.8 5.6 %copy-start.20 = (bf16[128,128]{1,0:T(8,128)(2,1)S(1)}, bf16[128,128]{1,0:T(8,128)(2,1)}, u32[]{:S(2)}) copy-start(bf16[128,128]{1,0:T(8,128)(2,1)} %constant.80.clone.basis_lo) | copy-start | bytes 98308
  32.9 5.6 %copy-start.21 = (bf16[128,128]{1,0:T(8,128)(2,1)S(1)}, bf16[128,128]{1,0:T(8,128)(2,1)}, u32[]{:S(2)}) copy-start(bf16[128,128]{1,0:T(8,128)(2,1)} %constant.79.clone.basis_hi) | copy-start | bytes 98308
  38.4 5.6 %copy-start.18 = (bf16[128,128]{1,0:T(8,128)(2,1)S(1)}, bf16[128,128]{1,0:T(8,128)(2,1)}, u32[]{:S(2)}) copy-start(bf16[128,128]{1,0:T(8,128)(2,1)} %constant.82.clone.basis_lo) | copy-start | bytes 98308
  38.4 5.6 %copy-start.19 = (bf16[128,128]{1,0:T(8,128)(2,1)S(1)}, bf16[128,128]{1,0:T(8,128)(2,1)}, u32[]{:S(2)}) copy-start(bf16[128,128]{1,0:T(8,128)(2,1)} %constant.81.clone.basis_hi) | copy-start | bytes 98308
  44.0 5.6 %copy-start.16 = (bf16[128,128]{1,0:T(8,128)(2,1)S(1)}, bf16[128,128]{1,0:T(8,128)(2,1)}, u32[]{:S(2)}) copy-start(bf16[128,128]{1,0:T(8,128)(2,1)} %constant.84.clone.basis_lo) | copy-start | bytes 98308
  44.0 5.6 %copy-start.17 = (bf16[128,128]{1,0:T(8,128)(2,1)S(1)}, bf16[128,128]{1,0:T(8,128)(2,1)}, u32[]{:S(2)}) copy-start(bf16[128,128]{1,0:T(8,128)(2,1)} %constant.83.clone.basis_hi) | copy-start | bytes 98308
  (2 other events, 1.4 us)

commit v2 on v1

v2 whole, which is shorter than its diff:
```python
import functools
import math

import jax
import jax.numpy as jnp
import ml_dtypes
import numpy as np
from jax import lax
from jax.experimental import pallas as pl
from jax.experimental.pallas import tpu as pltpu
from jax.sharding import PartitionSpec as P

KMAX = 8
FCUT = 512
SIDE = 128
HALF_SIDE = SIDE // 2
QUARTER = SIDE // 4
MODES = 2 * KMAX
CHUNKS = ((12,), (10,), (16,), (14,), (12,))
BF16 = jnp.bfloat16
F32 = jnp.float32


def swapped(value, axis, bit):
    mask = 2**bit
    pairs = [(source, source ^ mask) for source in range(lax.axis_size(axis))]
    return lax.ppermute(value, axis, pairs)


def np_split(table):
    high = table.astype(ml_dtypes.bfloat16)
    low = (table - high.astype(np.float64)).astype(ml_dtypes.bfloat16)
    return high, low


@functools.cache
def transform_tables():
    n = SIDE * SIDE
    a = np.arange(SIDE)
    k = np.arange(HALF_SIDE)
    angle = 2 * np.pi * (k[:, None] * a[None, :] % SIDE) / SIDE
    first = np.concatenate([np.cos(angle), -np.sin(angle)])
    first[HALF_SIDE] = 1.0 - 2.0 * (a % 2)
    first_hi, first_lo = np_split(first)
    head = slice(0, HALF_SIDE)
    tail = slice(HALF_SIDE, SIDE)
    first_pack = np.concatenate([first_hi[:, head], first_hi[:, head], first_lo[:, head]], axis=1)
    edge_pack = np.concatenate([first_hi[:, tail], first_lo[:, tail]], axis=1)
    bins = np.stack([k, np.where(k == 0, HALF_SIDE, k)]).reshape(-1)
    turn = 2 * np.pi * (bins[:, None] * a[None, :]) / n
    twiddle = np.concatenate([np.cos(turn), np.sin(turn)], axis=1).astype(np.float32)
    inner = 2 * np.pi * (a[:, None] * a[None, :] % SIDE) / SIDE
    c, s = np.cos(inner), np.sin(inner)
    forward_hi, forward_lo = np_split(np.block([[c, -s], [s, c]]))
    back_hi, back_lo = np_split(np.block([[c, s], [-s, c]]))
    forward = np.concatenate([forward_hi, forward_hi, forward_lo])
    back = np.concatenate([back_hi, back_hi, back_lo])
    f = bins[:, None] + SIDE * a[None, :]
    f = np.minimum(f, n - f).astype(np.float64)
    kept = n // 2
    ramp = f / kept * (1.0 + np.cos(np.pi * f / kept)) / n
    drop = 1.0 - 1.0 / (1.0 + (f / FCUT) ** 8)
    last = 2.0 * first[:, :HALF_SIDE].T
    last[:, 0] = 1.0
    last[:, HALF_SIDE] = 1.0 - 2.0 * (np.arange(HALF_SIDE) % 2)
    last_hi, last_lo = np_split(last)
    last_pack = np.concatenate([last_hi, last_hi, last_lo], axis=1)
    return {
        "first": first_pack,
        "edge": edge_pack,
        "twiddle": twiddle,
        "forward": forward,
        "back": back,
        "ramp": np.concatenate([ramp, ramp], axis=1).astype(np.float32),
        "ramp_drop": np.concatenate([ramp * drop, ramp * drop], axis=1).astype(np.float32),
        "last": last_pack,
    }


@functools.cache
def mode_basis(count, half_turn):
    order = np.arange(KMAX)
    angle = 2 * np.pi * (np.arange(count)[:, None] * order[None, :] % half_turn) / half_turn
    return np.concatenate([np.cos(angle), np.sin(angle)], axis=1)


def phase_rows(starts, half_turn):
    order = np.arange(KMAX)
    angle = 2 * np.pi * (np.asarray(starts)[:, None] * order[None, :] % half_turn) / half_turn
    return np.concatenate([np.cos(angle), np.sin(angle)], axis=1).astype(np.float32)


def split(value):
    high = value.astype(BF16)
    low = (value - high.astype(F32)).astype(BF16)
    return high, low


def dot(left, right):
    return jnp.dot(left, right, preferred_element_type=F32)


def lanes_flipped(block):
    rows = block.shape[0]
    lane = SIDE - 1 - lax.broadcasted_iota(jnp.int32, (rows, SIDE), 1)
    turned = jnp.take_along_axis(block, lane, axis=1)
    row = rows - 1 - lax.broadcasted_iota(jnp.int32, (rows, SIDE), 0)
    return jnp.take_along_axis(turned, row, axis=0)


def flipped(sheet):
    blocks = [lanes_flipped(sheet[8 * i : 8 * i + 8]) for i in range(QUARTER // 8)]
    return jnp.concatenate(blocks[::-1], axis=0)


def swap_first_rows(upper_part, lower_part):
    row = lax.broadcasted_iota(jnp.int32, upper_part.shape, 0)
    return (
        jnp.where(row == 0, lower_part, upper_part),
        jnp.where(row == 0, upper_part, lower_part),
    )


def blend_weight(correlation, blend):
    position = (
        lax.broadcasted_iota(jnp.int32, (HALF_SIDE, SIDE), 0) * SIDE
        + lax.broadcasted_iota(jnp.int32, (HALF_SIDE, SIDE), 1)
    ).astype(F32)
    pixels = QUARTER * SIDE
    center = pixels - correlation.astype(F32) / 2.0
    return jnp.clip((position + 0.5 - center) / blend.astype(F32) + 0.5, 0.0, 1.0)


def edge_response(edge_table, padding):
    index = (
        lax.broadcasted_iota(jnp.int32, (HALF_SIDE, SIDE), 0) * SIDE
        + lax.broadcasted_iota(jnp.int32, (HALF_SIDE, SIDE), 1)
    )
    after = (index < padding).astype(F32)
    before = (index >= HALF_SIDE * SIDE - padding).astype(F32)
    boxes = jnp.concatenate([after, before], axis=1)
    boxes = jnp.concatenate([boxes, boxes], axis=0).astype(BF16)
    return dot(edge_table, boxes)


def transform_group(views, weight, correlation, edges, tables, gain, shifted, count):
    whole = correlation // SIDE
    part = correlation % SIDE
    lane = lax.broadcasted_iota(jnp.int32, (HALF_SIDE, SIDE), 1)
    in_row = lane < SIDE - part
    keep = 1.0 - weight[:QUARTER]
    stitched = []
    for i, (main, back) in enumerate(views):
        rolled = pltpu.roll(main, SIDE - part, 1)
        last = jnp.broadcast_to(main[QUARTER - 1 :, SIDE - 1 :], (QUARTER + 8, SIDE))
        shifted[i, QUARTER : 2 * QUARTER, :] = rolled
        shifted[i, 2 * QUARTER :, :] = last
        right = jnp.where(
            in_row,
            shifted[i, pl.ds(whole, HALF_SIDE), :],
            shifted[i, pl.ds(whole + 1, HALF_SIDE), :],
        )
        sheet = weight * right
        top = sheet[:QUARTER] + keep * flipped(back)
        stitched.append(jnp.concatenate([top, sheet[QUARTER:]], axis=0))
    high, low = split(jnp.concatenate(stitched, axis=1))
    grown = dot(tables["first"][...], jnp.concatenate([high, low, high], axis=0))
    after, before = edges[:, :SIDE], edges[:, SIDE:]
    cos_turn, sin_turn = tables["twiddle"][:, :SIDE], tables["twiddle"][:, SIDE:]
    real, imag = [], []
    for i, sheet in enumerate(stitched):
        ends = (
            grown[:, i * SIDE : (i + 1) * SIDE]
            + sheet[HALF_SIDE - 1 :, SIDE - 1 :] * after
            + sheet[:1, :1] * before
        )
        real.append(ends[:HALF_SIDE])
        imag.append(ends[HALF_SIDE:])
    for i in range(0, count, 2):
        imag[i], real[i + 1] = swap_first_rows(imag[i], real[i + 1])
    turned = []
    for i in range(count):
        rows = slice((i % 2) * HALF_SIDE, (i % 2 + 1) * HALF_SIDE)
        c, s = cos_turn[rows], sin_turn[rows]
        turned.append(jnp.concatenate([real[i] * c + imag[i] * s, imag[i] * c - real[i] * s], axis=1))
    high, low = split(jnp.concatenate(turned, axis=0))
    spectrum = dot(jnp.concatenate([high, low, high], axis=1), tables["forward"][...])
    gains = jnp.concatenate([gain[...]] * (count // 2), axis=0)
    high, low = split(spectrum * gains)
    inner = dot(jnp.concatenate([high, low, high], axis=1), tables["back"][...])
    real, imag = [], []
    for i in range(count):
        rows = slice((i % 2) * HALF_SIDE, (i % 2 + 1) * HALF_SIDE)
        c, s = cos_turn[rows], sin_turn[rows]
        block = inner[i * HALF_SIDE : (i + 1) * HALF_SIDE]
        real.append(block[:, :SIDE] * c - block[:, SIDE:] * s)
        imag.append(block[:, SIDE:] * c + block[:, :SIDE] * s)
    for i in range(0, count, 2):
        imag[i], real[i + 1] = swap_first_rows(imag[i], real[i + 1])
    columns = jnp.concatenate(
        [jnp.concatenate([real[i], imag[i]], axis=0) for i in range(count)], axis=1
    )
    high, low = split(columns)
    result = dot(tables["last"][...], jnp.concatenate([high, low, high], axis=0))
    return [result[:, i * SIDE : (i + 1) * SIDE] for i in range(count)]


TABLES = ("first", "edge", "twiddle", "forward", "back", "last")


def picked(place, values):
    result = jnp.float32(values[-1])
    for i, value in enumerate(values[:-1]):
        result = jnp.where(place == i, jnp.float32(value), result)
    return result


def rotations(place, starts, half_turn):
    table = phase_rows(starts, half_turn)
    cos = [picked(place, list(table[:, k])) for k in range(KMAX)]
    sin = [picked(place, list(table[:, KMAX + k])) for k in range(KMAX)]
    return cos, sin


def send_from(raw, halves):
    return jnp.where(lax.axis_index("angle") >= halves, 0, raw.shape[0] // 2)


def start_pieces(halves, offset, raw, pieces, sems):
    start = send_from(raw, halves) + offset
    copies = []
    for i, piece in enumerate(pieces):
        count = piece.shape[0]
        copies.append(pltpu.make_async_copy(raw.at[pl.ds(start, count)], piece, sems.at[i]))
        copies[-1].start()
        start = start + count
    return copies


def head_kernel(
    halves, half_turn, raw_far, flat_far, dark_far, basis_far,
    piece, mine, other, level, dark, raw, flat, basis, sems,
):
    blocks = 4
    block = raw.shape[0] // blocks
    pairs = [(flat_far, flat), (dark_far, dark), (basis_far, basis)]
    for i in range(blocks):
        rows = pl.ds(i * block, block)
        pairs.append((raw_far.at[rows], raw.at[rows]))
    start = send_from(raw, halves)
    pairs.append((raw_far.at[pl.ds(start, piece.shape[0])], piece))
    copies = [
        pltpu.make_async_copy(source, target, sems.at[i])
        for i, (source, target) in enumerate(pairs)
    ]
    for copy in copies:
        copy.start()
    copies[0].wait()
    copies[1].wait()
    level[...] = jnp.log(flat[...] - dark[...])
    turns = phase_rows(np.arange(blocks) * block, half_turn)
    cos_total, sin_total = [0.0] * KMAX, [0.0] * KMAX
    for i in range(blocks):
        copies[3 + i].wait()
        projected = level[...] - jnp.log(raw[i * block : (i + 1) * block] - dark[...])
        columns = jnp.concatenate(
            [
                projected[:, 8 * j : 8 * j + 8, :].reshape(block * 8, SIDE)
                for j in range(QUARTER // 8)
            ],
            axis=1,
        )
        high, low = split(columns)
        if i == 0:
            copies[2].wait()
        partial = dot(basis[...], jnp.concatenate([high, low, high], axis=0))
        for k in range(KMAX):
            c, s = float(turns[i, k]), float(turns[i, KMAX + k])
            cos_part = partial[8 * k : 8 * k + 8, :]
            sin_part = partial[8 * (KMAX + k) : 8 * (KMAX + k) + 8, :]
            cos_total[k] = cos_total[k] + (cos_part * c - sin_part * s)
            sin_total[k] = sin_total[k] + (sin_part * c + cos_part * s)
    place = lax.axis_index("angle")
    cos, sin = rotations(place % halves, np.arange(halves) * raw.shape[0], half_turn)
    odd = place % 2
    half = KMAX // 2
    for k in range(KMAX):
        cos_mode = cos_total[k] * cos[k] - sin_total[k] * sin[k]
        sin_mode = sin_total[k] * cos[k] + cos_total[k] * sin[k]
        spot = k % half
        is_mine = odd == k // half

        def put(ref):
            for i in range(QUARTER // 8):
                lanes = slice(i * SIDE, (i + 1) * SIDE)
                ref[spot, 8 * i : 8 * i + 8, :] = cos_mode[:, lanes]
                ref[half + spot, 8 * i : 8 * i + 8, :] = sin_mode[:, lanes]

        @pl.when(is_mine)
        def _():
            put(mine)

        @pl.when(jnp.logical_not(is_mine))
        def _():
            put(other)

    copies[-1].wait()


def add_kernel(halves, offset, raw, mine, received, total, *refs):
    pieces, sems = refs[:-1], refs[-1]
    copies = start_pieces(halves, offset, raw, pieces, sems)
    total[...] = mine[...] + received[...]
    for copy in copies:
        copy.wait()


def filter_modes(
    halves, half_turn, mine, other_a, other_b, far_mine, far_other,
    weight, correlation, edges, cutoff, starts, tables, modes, side, shifted, result,
):
    place = lax.axis_index("angle")
    odd = place % 2
    upper = place // halves
    half = KMAX // 2
    side[upper, odd] = mine[...]
    side[upper, 1 - odd] = other_a[...] + other_b[...]
    side[1 - upper, odd] = far_mine[...]
    side[1 - upper, 1 - odd] = far_other[...]
    views = [
        (side[0, m // KMAX, m % KMAX], side[1, m // KMAX, m % KMAX]) for m in range(MODES)
    ]
    sheets = transform_group(
        views, weight, correlation, edges, tables, tables["ramp_drop"], shifted, MODES
    )
    for m, sheet in enumerate(sheets):
        result[m] = sheet
    cos, sin = rotations(place, starts, half_turn)
    for k in range(KMAX):
        spot = (k // half) * KMAX + k % half
        scale = jnp.where(k < cutoff, (1.0 if k == 0 else 2.0) / half_turn, 0.0)
        c = cos[k] * scale
        s = sin[k] * scale
        cos_sheet, sin_sheet = result[spot], result[spot + half]
        for row, sheet in (
            (k, cos_sheet * c + sin_sheet * s),
            (KMAX + k, sin_sheet * c - cos_sheet * s),
        ):
            high, low = split(sheet)
            for i in range(HALF_SIDE // 8):
                lanes = slice(i * SIDE, (i + 1) * SIDE)
                for part, value in enumerate((high, low, high)):
                    place_row = part * 8 * MODES + 8 * row
                    modes[place_row : place_row + 8, lanes] = value[8 * i : 8 * i + 8]


def low_sheets(basis, modes):
    low = dot(basis, modes)

    def block(i, j):
        return low[8 * i : 8 * i + 8, j * SIDE : (j + 1) * SIDE]

    return block


def clean_rows(halves, offset, groups, raw, partner, level, dark, weight, correlation, edges, tables, shifted, emit):
    is_upper = lax.axis_index("angle") >= halves
    start = jnp.where(is_upper, raw.shape[0] // 2, 0) + offset
    first = 0
    for size in groups:
        views = []
        for i in range(first, first + size):
            here = level[...] - jnp.log(raw[start + i] - dark[...])
            there = level[...] - jnp.log(partner[i] - dark[...])
            views.append((jnp.where(is_upper, there, here), jnp.where(is_upper, here, there)))
        sheets = transform_group(
            views, weight, correlation, edges, tables, tables["ramp"], shifted, size
        )
        emit(first, sheets)
        first += size


def prepare(settings, tables, shifted):
    shifted[:, :QUARTER, :] = jnp.zeros((shifted.shape[0], QUARTER, SIDE), F32)
    weight = blend_weight(settings[0], settings[1])
    return weight, edge_response(tables["edge"][...], settings[2])


def early_kernel(
    halves, offset, next_offset, groups, waits, raw, partner, level, dark, settings, *refs,
):
    refs = refs[waits:]
    names = TABLES + ("ramp",)
    tables = dict(zip(names, refs))
    out, *pieces, shifted, sems = refs[len(names) :]
    copies = start_pieces(halves, next_offset, raw, pieces, sems)
    weight, edges = prepare(settings, tables, shifted)

    def emit(first, sheets):
        for i, sheet in enumerate(sheets):
            out[first + i] = sheet

    clean_rows(
        halves, offset, groups, raw, partner, level, dark, weight, settings[0], edges, tables, shifted, emit
    )
    for copy in copies:
        copy.wait()


def middle_kernel(
    halves, half_turn, starts, early_count, mine, other_a, other_b, far_mine, far_other, basis,
    settings, *refs,
):
    names = TABLES + ("ramp_drop",)
    early, refs = refs[:early_count], refs[early_count:]
    tables = dict(zip(names, refs))
    fixed, modes, side, shifted, result = refs[len(names) :]
    weight, edges = prepare(settings, tables, shifted)
    filter_modes(
        halves, half_turn, mine, other_a, other_b, far_mine, far_other,
        weight, settings[0], edges, settings[3], starts, tables, modes, side, shifted, result,
    )
    low = low_sheets(basis[...], modes[...])
    row = 0
    for part in early:
        for i in range(part.shape[0]):
            for j in range(HALF_SIDE // 8):
                fixed[row, 8 * j : 8 * j + 8, :] = part[i, 8 * j : 8 * j + 8, :] - low(row, j)
            row += 1


def late_kernel(halves, offset, groups, raw, partner, level, dark, modes, basis, settings, *refs):
    names = TABLES + ("ramp",)
    tables = dict(zip(names, refs))
    *finished, out, shifted, done, sems = refs[len(names) :]
    copies = []

    def send(source, target):
        copies.append(pltpu.make_async_copy(source, target, sems.at[len(copies)]))
        copies[-1].start()

    row = 0
    for part in finished:
        send(part, out.at[pl.ds(row, part.shape[0])])
        row += part.shape[0]
    weight, edges = prepare(settings, tables, shifted)
    low = low_sheets(basis[...], modes[...])
    target = done if finished else out

    def emit(first, sheets):
        for i, sheet in enumerate(sheets):
            for j in range(HALF_SIDE // 8):
                target[first + i, 8 * j : 8 * j + 8, :] = sheet[8 * j : 8 * j + 8] - low(first + i, j)
        if finished:
            send(done.at[pl.ds(first, len(sheets))], out.at[pl.ds(offset + first, len(sheets))])

    clean_rows(
        halves, offset, groups, raw, partner, level, dark, weight, settings[0], edges, tables, shifted, emit
    )
    for copy in copies:
        copy.wait()


VMEM_SPEC = pl.BlockSpec(memory_space=pltpu.VMEM)
SMEM_SPEC = pl.BlockSpec(memory_space=pltpu.SMEM)
ANY_SPEC = pl.BlockSpec(memory_space=pl.ANY)
MIB = 2**20
COST = pl.CostEstimate(flops=0, bytes_accessed=0, transcendentals=0)


def call(kernel, name, operands, out_shape, out_specs, scratch, limit=32 * MIB):
    specs = [spec for spec, _ in operands]
    return pl.pallas_call(
        kernel,
        out_shape=out_shape,
        in_specs=specs,
        out_specs=out_specs,
        scratch_shapes=scratch,
        compiler_params=pltpu.CompilerParams(vmem_limit_bytes=limit),
        cost_estimate=COST,
        name=name,
    )(*(value for _, value in operands))


def vmem(*values):
    return [(VMEM_SPEC, jnp.asarray(value)) for value in values]


def smem(*values):
    return [(SMEM_SPEC, jnp.asarray(value)) for value in values]


def table_operands(*extra):
    tables = transform_tables()
    return vmem(*(tables[name] for name in TABLES + extra))


def shifted_scratch(count):
    return pltpu.VMEM((count, 3 * QUARTER + 8, SIDE), F32)


def sheet_scratch(count):
    return pltpu.VMEM((count, HALF_SIDE, SIDE), F32)


def basis_pack(offset, count, half_turn):
    basis = np.kron(mode_basis(offset + count, half_turn)[offset:], np.eye(8))
    hi, lo = np_split(basis)
    return np.concatenate([hi, hi, lo], axis=1)


def far(*values):
    return [
        (ANY_SPEC, pltpu.with_memory_space_constraint(jnp.asarray(value), pltpu.HBM))
        for value in values
    ]


def piece_shapes(raw, counts):
    return [jax.ShapeDtypeStruct((count,) + raw.shape[1:], F32) for count in counts]


def head(raw, flat, dark, count, halves, half_turn):
    block = raw.shape[0] // 4
    hi, lo = np_split(np.kron(mode_basis(block, half_turn).T, np.eye(8)))
    basis = np.concatenate([hi, hi, lo], axis=1)
    shapes = piece_shapes(raw, [count])
    shapes += [jax.ShapeDtypeStruct((KMAX, QUARTER, SIDE), F32)] * 2
    shapes += [jax.ShapeDtypeStruct((QUARTER, SIDE), F32)] * 2
    return call(
        functools.partial(head_kernel, halves, half_turn), "head",
        far(raw, flat, dark, basis), shapes, [VMEM_SPEC] * len(shapes),
        [
            pltpu.VMEM(raw.shape, F32),
            pltpu.VMEM(flat.shape, F32),
            pltpu.VMEM(basis.shape, BF16),
            pltpu.SemaphoreType.DMA((8,)),
        ],
    )


def add_modes(raw, mine, received, counts, offset, halves):
    shapes = [jax.ShapeDtypeStruct(mine.shape, F32)] + piece_shapes(raw, counts)
    return call(
        functools.partial(add_kernel, halves, offset), "add_modes", vmem(raw, mine, received),
        shapes, [VMEM_SPEC] * len(shapes), [pltpu.SemaphoreType.DMA((len(counts),))],
    )


def early_sheets(raw, partner, level, dark, after, settings, groups, offset, counts, next_offset, halves):
    operands = vmem(raw, partner, level, dark) + smem(settings)
    operands += [(ANY_SPEC, value) for value in after] + table_operands("ramp")
    shapes = [jax.ShapeDtypeStruct((sum(groups), HALF_SIDE, SIDE), F32)] + piece_shapes(raw, counts)
    return call(
        functools.partial(early_kernel, halves, offset, next_offset, groups, len(after)), "early_sheets",
        operands, shapes, [VMEM_SPEC] * len(shapes),
        [shifted_scratch(max(groups)), pltpu.SemaphoreType.DMA((max(len(counts), 1),))],
    )


def middle_sheets(early, parts, settings, halves, half_turn, half_block):
    count = sum(part.shape[0] for part in early)
    place = np.arange(2 * halves)
    starts = place % halves * 2 * half_block + place // halves * half_block
    operands = vmem(*parts, basis_pack(0, count, half_turn)) + smem(settings)
    operands += vmem(*early) + table_operands("ramp_drop")
    return call(
        functools.partial(middle_kernel, halves, half_turn, starts, len(early)), "middle_sheets", operands,
        (
            jax.ShapeDtypeStruct((count, HALF_SIDE, SIDE), F32),
            jax.ShapeDtypeStruct((3 * 8 * MODES, HALF_SIDE // 8 * SIDE), BF16),
        ),
        (VMEM_SPEC, VMEM_SPEC),
        [
            pltpu.VMEM((2, 2, KMAX, QUARTER, SIDE), F32),
            shifted_scratch(MODES),
            sheet_scratch(MODES),
        ],
    )


def late_sheets(raw, partner, level, dark, modes, settings, groups, offset, halves, half_turn, finished=()):
    count = sum(groups)
    operands = vmem(raw, partner, level, dark, modes, basis_pack(offset, count, half_turn))
    operands += smem(settings) + table_operands("ramp") + vmem(*finished)
    total = raw.shape[0] // 2 if finished else count
    return call(
        functools.partial(late_kernel, halves, offset, groups), "late_sheets", operands,
        jax.ShapeDtypeStruct((total, HALF_SIDE, SIDE), F32),
        ANY_SPEC if finished else VMEM_SPEC,
        [
            shifted_scratch(max(groups)),
            sheet_scratch(count),
            pltpu.SemaphoreType.DMA((len(finished) + len(groups),)),
        ],
    )


def local(intensity, flat_field, dark_field, correlation, blend_width, padding, cutoff):
    angle_count = lax.axis_size("angle")
    halves = angle_count // 2
    top_bit = angle_count.bit_length() - 2
    angles, local_rows, pixels = intensity.shape
    half_block = angles // 2
    half_turn = half_block * angle_count
    counts = [sum(groups) for groups in CHUNKS]
    starts = [sum(counts[:i]) for i in range(len(counts))]
    raw = intensity.reshape(angles, QUARTER, SIDE)
    piece, mine, other, level, dark = head(
        raw, flat_field.reshape(QUARTER, SIDE), dark_field.reshape(QUARTER, SIDE),
        counts[0], halves, half_turn,
    )
    settings = jnp.concatenate([correlation, blend_width, padding, cutoff])
    partners = [swapped(piece, "angle", top_bit)]
    for bit in range(1, top_bit):
        mine = mine + swapped(mine, "angle", bit)
        other = other + swapped(other, "angle", bit)
    received = swapped(other, "angle", 0)
    other_more = swapped(mine, "angle", 0)
    mine_sum, piece = add_modes(raw, mine, received, counts[1:2], starts[1], halves)
    partners.append(swapped(piece, "angle", top_bit))
    far_mine = swapped(mine_sum, "angle", top_bit)
    first, *pieces = early_sheets(
        raw, partners[0], level, dark, (mine_sum, other_more), settings, CHUNKS[0], 0,
        counts[2:4], starts[2], halves,
    )
    partners += [swapped(piece, "angle", top_bit) for piece in pieces]
    far_other = swapped(far_mine, "angle", 0)
    second, *pieces = early_sheets(
        raw, partners[1], level, dark, (far_mine, first), settings, CHUNKS[1], starts[1],
        counts[4:], starts[4] if len(starts) > 4 else 0, halves,
    )
    partners += [swapped(piece, "angle", top_bit) for piece in pieces]
    early = [first, second]
    parts = (mine_sum, other, other_more, far_mine, far_other)
    fixed, modes = middle_sheets(early, parts, settings, halves, half_turn, half_block)
    finished = [fixed]
    for i in range(2, len(CHUNKS)):
        finished.append(
            late_sheets(
                raw, partners[i], level, dark, modes, settings, CHUNKS[i], starts[i],
                halves, half_turn, finished if i == len(CHUNKS) - 1 else (),
            )
        )
    return finished[-1].reshape(half_block, local_rows, 2 * pixels)


def solution(mesh):
    placed = (P("angle", "row", None), P("row", None), P("row", None), P(), P(), P(), P())
    return jax.shard_map(
        local, mesh=mesh, in_specs=placed, out_specs=P("angle", "row", None), check_vma=False
    )
```

time: 55.6 us -> 42.1 us (0.76)
  Pallas kernels: 29.3 us -> 21 us
  local copies, waits for them, and re-layouts: 5.78 us -> 0.07 us
  waiting for transfers between devices: 4.94 us -> 7.02 us
  other arithmetic: 0.99 us -> 0.08 us
    pallas_call x6 -> x8, Pallas kernels: 29.3 us -> 21 us  [call(): pl.pallas_call(kernel, out_shape=out_shape, in_specs=specs, out_specs=out...]
    unnamed x52 -> x26, local copies, waits for them, and re-layouts: 5.69 us -> 0.07 us
    ppermute x8 -> x9, waiting for transfers between devices: 4.94 us -> 7.02 us  [swapped(): return lax.ppermute(value, axis, pairs)]
    add x1 -> x0, other arithmetic: 0.99 us -> none  [local(): mine_sum = mine + swapped(other, 'angle', 0)]
    ppermute x8 -> x9, starting transfers between devices: 11.2 us -> 10.9 us  [swapped(): return lax.ppermute(value, axis, pairs)]
  transfers between devices with their start and end apart: 8 -> 9, of which waited for: 3 -> 2; matrix products, arithmetic and copies ran while one was open for 2% -> 0% of each run, Pallas kernels for 38% -> 35%
where the time goes in v2:
time: 42.1 us; the launch traced here: 41.9 us
  Pallas kernels  21 us (50%)
  starting transfers between devices  10.9 us (26%)
  waiting for transfers between devices  7.02 us (17%)
  between operations  2.85 us (7%)
    pallas_call x8, Pallas kernels, call(): pl.pallas_call(kernel, out_shape=out_shape, in_specs=specs, out_specs=out...  21 us
    ppermute x9, starting transfers between devices, swapped(): return lax.ppermute(value, axis, pairs)  10.9 us
    ppermute x9, waiting for transfers between devices, swapped(): return lax.ppermute(value, axis, pairs)  7.02 us
  transfers between devices with their start and end apart: 9, of which 2 were waited for; matrix products, arithmetic and copies ran while one was open for 0% of the time, Pallas kernels for 35%

profile of v2, /device:TPU:0, one launch (start us, length us, event | category | flops | bytes accessed | tf_op | source)
XLA Modules:
  0.0 41.9 jit_solution(161053294416570822)
XLA Ops:
  0.0 0.0 copy-start.5
  0.0 0.0 copy-start.6
  0.0 0.0 copy-start.7
  0.1 2.9 %head.1 = (f32[12,32,128]{2,1,0:T(8,128)S(1)}, f32[8,32,128]{2,1,0:T(8,128)S(1)}, f32[8,32,128]{2,1,0:T(8,128)S(1)}, f32[32,128]{1,0:T(8,128)S(1)}, f32[32,128]{1,0:T(8,128)S(1)}) custom-call(f32[128,32,128]{2,1,0:T(8,128)} %bitcast.4, f32[32,128]{1,0:T(8,128)} %bitcast.11, f32[32,128]{1,0:T(8,128)} %bitcast.12, bf16[128,768]{1,0:T(8,128)(2,1)} %constant.26.clone.basis_far), custom_call_target="tpu_custom_call" | custom-call | tf_op jit(solution)/shard_map/head/pallas_call | solution.py:473
  3.0 3.0 %collective-permute-start = (f32[8,32,128]{2,1,0:T(8,128)S(1)}, f32[8,32,128]{2,1,0:T(8,128)S(1)}, u32[]{:S(2)}, u32[]{:S(2)}) collective-permute-start(f32[8,32,128]{2,1,0:T(8,128)S(1)} %get-tuple-element.20.other_a), channel_id=1, source_target_pairs={{0,8},{8,0},{16,24},{24,16},{1,9},{9,1},{17,25},{25,17},{2,10},{10... | collective-permute-start | bytes 393224 | tf_op jit(solution)/shard_map/ppermute | solution.py:27
  6.0 1.5 %collective-permute-start.3 = (f32[12,32,128]{2,1,0:T(8,128)S(1)}, f32[12,32,128]{2,1,0:T(8,128)S(1)}, u32[]{:S(2)}, u32[]{:S(2)}) collective-permute-start(f32[12,32,128]{2,1,0:T(8,128)S(1)} %get-tuple-element.25), channel_id=1, source_target_pairs={{0,16},{8,24},{16,0},{24,8},{1,17},{9,25},{17,1},{25,9},{2,18},{10... | collective-permute-start | bytes 589832 | tf_op jit(solution)/shard_map/ppermute | solution.py:27
  7.5 0.5 %collective-permute-start.4 = (f32[8,32,128]{2,1,0:T(8,128)S(1)}, f32[8,32,128]{2,1,0:T(8,128)S(1)}, u32[]{:S(2)}, u32[]{:S(2)}) collective-permute-start(f32[8,32,128]{2,1,0:T(8,128)S(1)} %get-tuple-element.19.mine), channel_id=1, source_target_pairs={{0,8},{8,0},{16,24},{24,16},{1,9},{9,1},{17,25},{25,17},{2,10},{10... | collective-permute-start | bytes 393224 | tf_op jit(solution)/shard_map/ppermute | solution.py:27
  10.7 0.0 collective-permute-done.received
  10.7 0.2 add_modes.1
  10.9 1.8 %collective-permute-start.2 = (f32[8,32,128]{2,1,0:T(8,128)S(1)}, f32[8,32,128]{2,1,0:T(8,128)S(1)}, u32[]{:S(2)}, u32[]{:S(2)}) collective-permute-start(f32[8,32,128]{2,1,0:T(8,128)S(1)} %get-tuple-element.24.refs_0_.mine), channel_id=1, source_target_pairs={{0,16},{8,24},{16,0},{24,8},{1,17},{9,25},{17,1},{25,9},{2,18},{10... | collective-permute-start | bytes 393224 | tf_op jit(solution)/shard_map/ppermute | solution.py:27
  12.7 0.3 collective-permute-start.1
  13.0 0.1 pad_add_fusion.settings
  13.1 0.0 collective-permute-done.4.refs_1_.other_b
  13.2 2.8 %early_sheets.2 = (f32[12,64,128]{2,1,0:T(8,128)S(1)}, f32[16,32,128]{2,1,0:T(8,128)S(1)}, f32[14,32,128]{2,1,0:T(8,128)S(1)}) custom-call(f32[128,32,128]{2,1,0:T(8,128)S(1)} %bitcast.6, f32[12,32,128]{2,1,0:T(8,128)S(1)} %collective-permute-done.3.partner, f32[32,128]{1,0:T(8,128)S(1)} %get-tuple-element.22.level, f32[32,128]{1,0:T(8,128)S(1)} %get-tuple-element.23.dark, ...), custom_call_target="tpu_custom_call" | custom-call | tf_op jit(solution)/shard_map/early_sheets/pallas_call | solution.py:473
  16.0 0.0 copy-start.8
  16.0 0.0 copy-start.9
  16.0 1.8 %collective-permute-start.7 = (f32[16,32,128]{2,1,0:T(8,128)S(1)}, f32[16,32,128]{2,1,0:T(8,128)S(1)}, u32[]{:S(2)}, u32[]{:S(2)}) collective-permute-start(f32[16,32,128]{2,1,0:T(8,128)S(1)} %get-tuple-element.31), channel_id=1, source_target_pairs={{0,16},{8,24},{16,0},{24,8},{1,17},{9,25},{17,1},{25,9},{2,18},{10... | collective-permute-start | bytes 786440 | tf_op jit(solution)/shard_map/ppermute | solution.py:27
  17.8 0.3 collective-permute-start.8
  18.1 2.5 %collective-permute-done.1.partner = f32[10,32,128]{2,1,0:T(8,128)S(1)} collective-permute-done((f32[10,32,128]{2,1,0:T(8,128)S(1)}, f32[10,32,128]{2,1,0:T(8,128)S(1)}, u32[]{:S(2)}, u32[]{:S(2)}) %collective-permute-start.1) | collective-permute-done | bytes 163872 | tf_op jit(solution)/shard_map/ppermute | solution.py:27
  20.6 2.5 %early_sheets.3 = (f32[10,64,128]{2,1,0:T(8,128)S(1)}, f32[12,32,128]{2,1,0:T(8,128)S(1)}) custom-call(f32[128,32,128]{2,1,0:T(8,128)S(1)} %bitcast.7, f32[10,32,128]{2,1,0:T(8,128)S(1)} %collective-permute-done.1.partner, f32[32,128]{1,0:T(8,128)S(1)} %get-tuple-element.22.level, f32[32,128]{1,0:T(8,128)S(1)} %get-tuple-element.23.dark, ...), custom_call_target="tpu_custom_call" | custom-call | tf_op jit(solution)/shard_map/early_sheets/pallas_call | solution.py:473
  23.2 0.0 copy-start.11
  23.2 1.2 %collective-permute-start.5 = (f32[12,32,128]{2,1,0:T(8,128)S(1)}, f32[12,32,128]{2,1,0:T(8,128)S(1)}, u32[]{:S(2)}, u32[]{:S(2)}) collective-permute-start(f32[12,32,128]{2,1,0:T(8,128)S(1)} %get-tuple-element.27), channel_id=1, source_target_pairs={{0,16},{8,24},{16,0},{24,8},{1,17},{9,25},{17,1},{25,9},{2,18},{10... | collective-permute-start | bytes 589832 | tf_op jit(solution)/shard_map/ppermute | solution.py:27
  24.3 0.5 %collective-permute-start.6 = (f32[8,32,128]{2,1,0:T(8,128)S(1)}, f32[8,32,128]{2,1,0:T(8,128)S(1)}, u32[]{:S(2)}, u32[]{:S(2)}) collective-permute-start(f32[8,32,128]{2,1,0:T(8,128)S(1)} %collective-permute-done.2.refs_0_.far_mine), channel_id=1, source_target_pairs={{0,8},{8,0},{16,24},{24,16},{1,9},{9,1},{17,25},{25,17},{2,10},{10... | collective-permute-start | bytes 393224 | tf_op jit(solution)/shard_map/ppermute | solution.py:27
  24.8 4.5 %collective-permute-done.6.far_other = f32[8,32,128]{2,1,0:T(8,128)S(1)} collective-permute-done((f32[8,32,128]{2,1,0:T(8,128)S(1)}, f32[8,32,128]{2,1,0:T(8,128)S(1)}, u32[]{:S(2)}, u32[]{:S(2)}) %collective-permute-start.6) | collective-permute-done | bytes 131104 | tf_op jit(solution)/shard_map/ppermute | solution.py:27
  29.3 3.3 %middle_sheets.1 = (f32[22,64,128]{2,1,0:T(8,128)S(1)}, bf16[384,1024]{1,0:T(8,128)(2,1)S(1)}) custom-call(f32[8,32,128]{2,1,0:T(8,128)S(1)} %get-tuple-element.24.refs_0_.mine, f32[8,32,128]{2,1,0:T(8,128)S(1)} %get-tuple-element.20.other_a, f32[8,32,128]{2,1,0:T(8,128)S(1)} %collective-permute-done.4.refs_1_.other_b, ...), custom_call_target="tpu_custom_call" | custom-call | tf_op jit(solution)/shard_map/middle_sheets/pallas_call | solution.py:473
  32.6 0.0 copy-start.10
  32.7 2.8 %late_sheets.4.refs_9_ = f32[14,64,128]{2,1,0:T(8,128)S(1)} custom-call(f32[128,32,128]{2,1,0:T(8,128)S(1)} %bitcast.8, f32[14,32,128]{2,1,0:T(8,128)S(1)} %collective-permute-done.8.partner, f32[32,128]{1,0:T(8,128)S(1)} %get-tuple-element.22.level, f32[32,128]{1,0:T(8,128)S(1)} %get-tuple-element.23.dark, bf16[384,1024]{1,0:T(8,128)(2,1)S(1)} %get-tuple-element.29.modes, ...), custom_call_target="tpu_custom_call" | custom-call | tf_op jit(solution)/shard_map/late_sheets/pallas_call | solution.py:473
  35.4 0.0 copy-start.12
  35.4 0.0 collective-permute-done.7.partner
  35.4 3.0 %late_sheets.3.refs_8_ = f32[16,64,128]{2,1,0:T(8,128)S(1)} custom-call(f32[128,32,128]{2,1,0:T(8,128)S(1)} %bitcast.9, f32[16,32,128]{2,1,0:T(8,128)S(1)} %collective-permute-done.7.partner, f32[32,128]{1,0:T(8,128)S(1)} %get-tuple-element.22.level, f32[32,128]{1,0:T(8,128)S(1)} %get-tuple-element.23.dark, bf16[384,1024]{1,0:T(8,128)(2,1)S(1)} %get-tuple-element.29.modes, ...), custom_call_target="tpu_custom_call" | custom-call | tf_op jit(solution)/shard_map/late_sheets/pallas_call | solution.py:473
  38.5 0.0 collective-permute-done.5.partner
  38.5 3.4 %late_sheets.5 = f32[64,64,128]{2,1,0:T(8,128)} custom-call(f32[128,32,128]{2,1,0:T(8,128)S(1)} %bitcast.10, f32[12,32,128]{2,1,0:T(8,128)S(1)} %collective-permute-done.5.partner, f32[32,128]{1,0:T(8,128)S(1)} %get-tuple-element.22.level, f32[32,128]{1,0:T(8,128)S(1)} %get-tuple-element.23.dark, bf16[384,1024]{1,0:T(8,128)(2,1)S(1)} %get-tuple-element.29.modes, ...), custom_call_target="tpu_custom_call" | custom-call | tf_op jit(solution)/shard_map/late_sheets/pallas_call | solution.py:473
  (21 shorter events, 0.0 us)
Async XLA Ops:
  0.0 10.7 %copy-start = (f32[128,1,4096]{2,1,0:T(1,128)S(1)}, f32[128,1,4096]{2,1,0:T(1,128)}, u32[]{:S(2)}) copy-start(f32[128,1,4096]{2,1,0:T(1,128)} %param.20) | copy-start | bytes 6291460
  0.0 13.1 %copy-start.1 = (bf16[768,256]{1,0:T(8,128)(2,1)S(1)}, bf16[768,256]{1,0:T(8,128)(2,1)}, u32[]{:S(2)}) copy-start(bf16[768,256]{1,0:T(8,128)(2,1)} %constant.31.clone.refs_6_.refs_4_) | copy-start | bytes 1179652
  0.0 13.1 %copy-start.2 = (bf16[768,256]{1,0:T(8,128)(2,1)S(1)}, bf16[768,256]{1,0:T(8,128)(2,1)}, u32[]{:S(2)}) copy-start(bf16[768,256]{1,0:T(8,128)(2,1)} %constant.30.clone.refs_5_.refs_3_) | copy-start | bytes 1179652
  0.0 13.1 %copy-start.3 = (f32[128,256]{1,0:T(8,128)S(1)}, f32[128,256]{1,0:T(8,128)}, u32[]{:S(2)}) copy-start(f32[128,256]{1,0:T(8,128)} %constant.29.clone.refs_4_.refs_2_) | copy-start | bytes 393220
  0.0 13.1 %copy-start.4 = (f32[128,256]{1,0:T(8,128)S(1)}, f32[128,256]{1,0:T(8,128)}, u32[]{:S(2)}) copy-start(f32[128,256]{1,0:T(8,128)} %constant.33.clone.refs_8_.refs_6_) | copy-start | bytes 393220
  0.0 13.1 %copy-start.5 = (bf16[128,192]{1,0:T(8,128)(2,1)S(1)}, bf16[128,192]{1,0:T(8,128)(2,1)}, u32[]{:S(2)}) copy-start(bf16[128,192]{1,0:T(8,128)(2,1)} %constant.27.clone.refs_2_.refs_0_) | copy-start | bytes 147460
  0.0 13.1 %copy-start.6 = (bf16[64,384]{1,0:T(8,128)(2,1)S(1)}, bf16[64,384]{1,0:T(8,128)(2,1)}, u32[]{:S(2)}) copy-start(bf16[64,384]{1,0:T(8,128)(2,1)} %constant.32.clone.refs_7_.refs_5_) | copy-start | bytes 147460
  0.0 13.1 %copy-start.7 = (bf16[128,128]{1,0:T(8,128)(2,1)S(1)}, bf16[128,128]{1,0:T(8,128)(2,1)}, u32[]{:S(2)}) copy-start(bf16[128,128]{1,0:T(8,128)(2,1)} %constant.28.clone.refs_3_.refs_1_) | copy-start | bytes 98308
  3.0 7.7 %collective-permute-start = (f32[8,32,128]{2,1,0:T(8,128)S(1)}, f32[8,32,128]{2,1,0:T(8,128)S(1)}, u32[]{:S(2)}, u32[]{:S(2)}) collective-permute-start(f32[8,32,128]{2,1,0:T(8,128)S(1)} %get-tuple-element.20.other_a), channel_id=1, source_target_pairs={{0,8},{8,0},{16,24},{24,16},{1,9},{9,1},{17,25},{25,17},{2,10},{10... | collective-permute-start | bytes 393224 | tf_op jit(solution)/shard_map/ppermute | solution.py:27
  6.0 7.1 %collective-permute-start.3 = (f32[12,32,128]{2,1,0:T(8,128)S(1)}, f32[12,32,128]{2,1,0:T(8,128)S(1)}, u32[]{:S(2)}, u32[]{:S(2)}) collective-permute-start(f32[12,32,128]{2,1,0:T(8,128)S(1)} %get-tuple-element.25), channel_id=1, source_target_pairs={{0,16},{8,24},{16,0},{24,8},{1,17},{9,25},{17,1},{25,9},{2,18},{10... | collective-permute-start | bytes 589832 | tf_op jit(solution)/shard_map/ppermute | solution.py:27
  7.5 5.6 %collective-permute-start.4 = (f32[8,32,128]{2,1,0:T(8,128)S(1)}, f32[8,32,128]{2,1,0:T(8,128)S(1)}, u32[]{:S(2)}, u32[]{:S(2)}) collective-permute-start(f32[8,32,128]{2,1,0:T(8,128)S(1)} %get-tuple-element.19.mine), channel_id=1, source_target_pairs={{0,8},{8,0},{16,24},{24,16},{1,9},{9,1},{17,25},{25,17},{2,10},{10... | collective-permute-start | bytes 393224 | tf_op jit(solution)/shard_map/ppermute | solution.py:27
  10.9 7.2 %collective-permute-start.2 = (f32[8,32,128]{2,1,0:T(8,128)S(1)}, f32[8,32,128]{2,1,0:T(8,128)S(1)}, u32[]{:S(2)}, u32[]{:S(2)}) collective-permute-start(f32[8,32,128]{2,1,0:T(8,128)S(1)} %get-tuple-element.24.refs_0_.mine), channel_id=1, source_target_pairs={{0,16},{8,24},{16,0},{24,8},{1,17},{9,25},{17,1},{25,9},{2,18},{10... | collective-permute-start | bytes 393224 | tf_op jit(solution)/shard_map/ppermute | solution.py:27
  12.7 7.9 %collective-permute-start.1 = (f32[10,32,128]{2,1,0:T(8,128)S(1)}, f32[10,32,128]{2,1,0:T(8,128)S(1)}, u32[]{:S(2)}, u32[]{:S(2)}) collective-permute-start(f32[10,32,128]{2,1,0:T(8,128)S(1)} %get-tuple-element.21), channel_id=1, source_target_pairs={{0,16},{8,24},{16,0},{24,8},{1,17},{9,25},{17,1},{25,9},{2,18},{10... | collective-permute-start | bytes 491528 | tf_op jit(solution)/shard_map/ppermute | solution.py:27
  16.0 13.3 %copy-start.8 = (bf16[176,384]{1,0:T(8,128)(2,1)S(1)}, bf16[176,384]{1,0:T(8,128)(2,1)}, u32[]{:S(2)}) copy-start(bf16[176,384]{1,0:T(8,128)(2,1)} %constant.34.clone.basis) | copy-start | bytes 405508
  16.0 13.3 %copy-start.9 = (f32[128,256]{1,0:T(8,128)S(1)}, f32[128,256]{1,0:T(8,128)}, u32[]{:S(2)}) copy-start(f32[128,256]{1,0:T(8,128)} %constant.35.clone.refs_8_) | copy-start | bytes 393220
  16.0 19.4 %collective-permute-start.7 = (f32[16,32,128]{2,1,0:T(8,128)S(1)}, f32[16,32,128]{2,1,0:T(8,128)S(1)}, u32[]{:S(2)}, u32[]{:S(2)}) collective-permute-start(f32[16,32,128]{2,1,0:T(8,128)S(1)} %get-tuple-element.31), channel_id=1, source_target_pairs={{0,16},{8,24},{16,0},{24,8},{1,17},{9,25},{17,1},{25,9},{2,18},{10... | collective-permute-start | bytes 786440 | tf_op jit(solution)/shard_map/ppermute | solution.py:27
  17.8 14.8 %collective-permute-start.8 = (f32[14,32,128]{2,1,0:T(8,128)S(1)}, f32[14,32,128]{2,1,0:T(8,128)S(1)}, u32[]{:S(2)}, u32[]{:S(2)}) collective-permute-start(f32[14,32,128]{2,1,0:T(8,128)S(1)} %get-tuple-element.32), channel_id=1, source_target_pairs={{0,16},{8,24},{16,0},{24,8},{1,17},{9,25},{17,1},{25,9},{2,18},{10... | collective-permute-start | bytes 688136 | tf_op jit(solution)/shard_map/ppermute | solution.py:27
  23.2 9.5 %copy-start.11 = (bf16[112,384]{1,0:T(8,128)(2,1)S(1)}, bf16[112,384]{1,0:T(8,128)(2,1)}, u32[]{:S(2)}) copy-start(bf16[112,384]{1,0:T(8,128)(2,1)} %constant.37.clone.basis) | copy-start | bytes 258052
  23.2 15.3 %collective-permute-start.5 = (f32[12,32,128]{2,1,0:T(8,128)S(1)}, f32[12,32,128]{2,1,0:T(8,128)S(1)}, u32[]{:S(2)}, u32[]{:S(2)}) collective-permute-start(f32[12,32,128]{2,1,0:T(8,128)S(1)} %get-tuple-element.27), channel_id=1, source_target_pairs={{0,16},{8,24},{16,0},{24,8},{1,17},{9,25},{17,1},{25,9},{2,18},{10... | collective-permute-start | bytes 589832 | tf_op jit(solution)/shard_map/ppermute | solution.py:27
  24.3 5.0 %collective-permute-start.6 = (f32[8,32,128]{2,1,0:T(8,128)S(1)}, f32[8,32,128]{2,1,0:T(8,128)S(1)}, u32[]{:S(2)}, u32[]{:S(2)}) collective-permute-start(f32[8,32,128]{2,1,0:T(8,128)S(1)} %collective-permute-done.2.refs_0_.far_mine), channel_id=1, source_target_pairs={{0,8},{8,0},{16,24},{24,16},{1,9},{9,1},{17,25},{25,17},{2,10},{10... | collective-permute-start | bytes 393224 | tf_op jit(solution)/shard_map/ppermute | solution.py:27
  32.6 2.8 %copy-start.10 = (bf16[128,384]{1,0:T(8,128)(2,1)S(1)}, bf16[128,384]{1,0:T(8,128)(2,1)}, u32[]{:S(2)}) copy-start(bf16[128,384]{1,0:T(8,128)(2,1)} %constant.36.clone.basis) | copy-start | bytes 294916
  35.4 3.1 %copy-start.12 = (bf16[96,384]{1,0:T(8,128)(2,1)S(1)}, bf16[96,384]{1,0:T(8,128)(2,1)}, u32[]{:S(2)}) copy-start(bf16[96,384]{1,0:T(8,128)(2,1)} %constant.38.clone.basis) | copy-start | bytes 221188

commit v3 on v2

--- a/solution.py
+++ b/solution.py
@@ -16,7 +16,8 @@
 HALF_SIDE = SIDE // 2
 QUARTER = SIDE // 4
 MODES = 2 * KMAX
-CHUNKS = ((12,), (10,), (16,), (14,), (12,))
+MODE_GROUP = 8
+CHUNKS = ((8,8,8),(6,4),(6,6),(6,4),(4,4))
 BF16 = jnp.bfloat16
 F32 = jnp.float32
 
@@ -143,28 +144,31 @@
     return dot(edge_table, boxes)
 
 
-def transform_group(views, weight, correlation, edges, tables, gain, shifted, count):
+def transform_group(views, weight, correlation, edges, tables, gain, shifted, base, emit):
+    count = len(views)
     whole = correlation // SIDE
     part = correlation % SIDE
     lane = lax.broadcasted_iota(jnp.int32, (HALF_SIDE, SIDE), 1)
     in_row = lane < SIDE - part
     keep = 1.0 - weight[:QUARTER]
     stitched = []
-    for i, (main, back) in enumerate(views):
+    for i, view in enumerate(views):
+        main, back = view()
         rolled = pltpu.roll(main, SIDE - part, 1)
         last = jnp.broadcast_to(main[QUARTER - 1 :, SIDE - 1 :], (QUARTER + 8, SIDE))
-        shifted[i, QUARTER : 2 * QUARTER, :] = rolled
-        shifted[i, 2 * QUARTER :, :] = last
+        shifted[base + i, QUARTER : 2 * QUARTER, :] = rolled
+        shifted[base + i, 2 * QUARTER :, :] = last
         right = jnp.where(
             in_row,
-            shifted[i, pl.ds(whole, HALF_SIDE), :],
-            shifted[i, pl.ds(whole + 1, HALF_SIDE), :],
+            shifted[base + i, pl.ds(whole, HALF_SIDE), :],
+            shifted[base + i, pl.ds(whole + 1, HALF_SIDE), :],
         )
         sheet = weight * right
         top = sheet[:QUARTER] + keep * flipped(back)
         stitched.append(jnp.concatenate([top, sheet[QUARTER:]], axis=0))
     high, low = split(jnp.concatenate(stitched, axis=1))
     grown = dot(tables["first"][...], jnp.concatenate([high, low, high], axis=0))
+    yield
     after, before = edges[:, :SIDE], edges[:, SIDE:]
     cos_turn, sin_turn = tables["twiddle"][:, :SIDE], tables["twiddle"][:, SIDE:]
     real, imag = [], []
@@ -185,9 +189,11 @@
         turned.append(jnp.concatenate([real[i] * c + imag[i] * s, imag[i] * c - real[i] * s], axis=1))
     high, low = split(jnp.concatenate(turned, axis=0))
     spectrum = dot(jnp.concatenate([high, low, high], axis=1), tables["forward"][...])
+    yield
     gains = jnp.concatenate([gain[...]] * (count // 2), axis=0)
     high, low = split(spectrum * gains)
     inner = dot(jnp.concatenate([high, low, high], axis=1), tables["back"][...])
+    yield
     real, imag = [], []
     for i in range(count):
         rows = slice((i % 2) * HALF_SIDE, (i % 2 + 1) * HALF_SIDE)
@@ -202,7 +208,16 @@
     )
     high, low = split(columns)
     result = dot(tables["last"][...], jnp.concatenate([high, low, high], axis=0))
-    return [result[:, i * SIDE : (i + 1) * SIDE] for i in range(count)]
+    yield
+    emit(base, [result[:, i * SIDE : (i + 1) * SIDE] for i in range(count)])
+
+
+def take_turns(groups):
+    groups = list(groups)
+    while groups:
+        for group in list(groups):
+            if next(group, groups) is groups:
+                groups.remove(group)
 
 
 TABLES = ("first", "edge", "twiddle", "forward", "back", "last")
@@ -239,7 +254,7 @@
 
 def head_kernel(
     halves, half_turn, raw_far, flat_far, dark_far, basis_far,
-    piece, mine, other, level, dark, raw, flat, basis, sems,
+    mine, other, level, dark, raw, flat, basis, sems,
 ):
     blocks = 4
     block = raw.shape[0] // blocks
@@ -247,8 +262,6 @@
     for i in range(blocks):
         rows = pl.ds(i * block, block)
         pairs.append((raw_far.at[rows], raw.at[rows]))
-    start = send_from(raw, halves)
-    pairs.append((raw_far.at[pl.ds(start, piece.shape[0])], piece))
     copies = [
         pltpu.make_async_copy(source, target, sems.at[i])
         for i, (source, target) in enumerate(pairs)
@@ -304,7 +317,9 @@
         def _():
             put(other)
 
-    copies[-1].wait()
+
+def piece_kernel(halves, raw_far, piece, sems):
+    start_pieces(halves, 0, raw_far, [piece], sems)[0].wait()
 
 
 def add_kernel(halves, offset, raw, mine, received, total, *refs):
@@ -327,14 +342,21 @@
     side[upper, 1 - odd] = other_a[...] + other_b[...]
     side[1 - upper, odd] = far_mine[...]
     side[1 - upper, 1 - odd] = far_other[...]
-    views = [
-        (side[0, m // KMAX, m % KMAX], side[1, m // KMAX, m % KMAX]) for m in range(MODES)
-    ]
-    sheets = transform_group(
-        views, weight, correlation, edges, tables, tables["ramp_drop"], shifted, MODES
-    )
-    for m, sheet in enumerate(sheets):
-        result[m] = sheet
+
+    def view(m):
+        return lambda: (side[0, m // KMAX, m % KMAX], side[1, m // KMAX, m % KMAX])
+
+    def emit(first, sheets):
+        for i, sheet in enumerate(sheets):
+            result[first + i] = sheet
+
+    take_turns(
+        transform_group(
+            [view(m) for m in range(first, first + MODE_GROUP)],
+            weight, correlation, edges, tables, tables["ramp_drop"], shifted, first, emit,
+        )
+        for first in range(0, MODES, MODE_GROUP)
+    )
     cos, sin = rotations(place, starts, half_turn)
     for k in range(KMAX):
         spot = (k // half) * KMAX + k % half
@@ -366,18 +388,23 @@
 def clean_rows(halves, offset, groups, raw, partner, level, dark, weight, correlation, edges, tables, shifted, emit):
     is_upper = lax.axis_index("angle") >= halves
     start = jnp.where(is_upper, raw.shape[0] // 2, 0) + offset
-    first = 0
-    for size in groups:
-        views = []
-        for i in range(first, first + size):
+
+    def view(i):
+        def load():
             here = level[...] - jnp.log(raw[start + i] - dark[...])
             there = level[...] - jnp.log(partner[i] - dark[...])
-            views.append((jnp.where(is_upper, there, here), jnp.where(is_upper, here, there)))
-        sheets = transform_group(
-            views, weight, correlation, edges, tables, tables["ramp"], shifted, size
+            return jnp.where(is_upper, there, here), jnp.where(is_upper, here, there)
+
+        return load
+
+    firsts = [sum(groups[:i]) for i in range(len(groups))]
+    take_turns(
+        transform_group(
+            [view(i) for i in range(first, first + size)],
+            weight, correlation, edges, tables, tables["ramp"], shifted, first, emit,
         )
-        emit(first, sheets)
-        first += size
+        for first, size in zip(firsts, groups)
+    )
 
 
 def prepare(settings, tables, shifted):
@@ -429,10 +456,23 @@
             row += 1
 
 
-def late_kernel(halves, offset, groups, raw, partner, level, dark, modes, basis, settings, *refs):
+class Joined:
+    def __init__(self, refs):
+        self.rows = [(ref, i) for ref in refs for i in range(ref.shape[0])]
+
+    def __getitem__(self, row):
+        ref, i = self.rows[row]
+        return ref[i]
+
+
+def late_kernel(
+    halves, offset, groups, writes, finished_count, partner_count, raw, level, dark, modes, basis, settings, *refs,
+):
     names = TABLES + ("ramp",)
+    partner, refs = Joined(refs[:partner_count]), refs[partner_count:]
     tables = dict(zip(names, refs))
-    *finished, out, shifted, done, sems = refs[len(names) :]
+    finished = refs[len(names) : len(names) + finished_count]
+    out, shifted, done, sems = refs[-4:]
     copies = []
 
     def send(source, target):
@@ -440,18 +480,19 @@
         copies[-1].start()
 
     row = 0
-    for part in finished:
-        send(part, out.at[pl.ds(row, part.shape[0])])
-        row += part.shape[0]
+    if writes == "all":
+        for part in finished:
+            send(part, out.at[pl.ds(row, part.shape[0])])
+            row += part.shape[0]
     weight, edges = prepare(settings, tables, shifted)
     low = low_sheets(basis[...], modes[...])
-    target = done if finished else out
+    target = done if writes else out
 
     def emit(first, sheets):
         for i, sheet in enumerate(sheets):
             for j in range(HALF_SIDE // 8):
                 target[first + i, 8 * j : 8 * j + 8, :] = sheet[8 * j : 8 * j + 8] - low(first + i, j)
-        if finished:
+        if writes:
             send(done.at[pl.ds(first, len(sheets))], out.at[pl.ds(offset + first, len(sheets))])
 
     clean_rows(
@@ -465,10 +506,10 @@
 SMEM_SPEC = pl.BlockSpec(memory_space=pltpu.SMEM)
 ANY_SPEC = pl.BlockSpec(memory_space=pl.ANY)
 MIB = 2**20
-COST = pl.CostEstimate(flops=0, bytes_accessed=0, transcendentals=0)
-
-
-def call(kernel, name, operands, out_shape, out_specs, scratch, limit=32 * MIB):
+HEAD_COST = 16 * MIB
+
+
+def call(kernel, name, operands, out_shape, out_specs, scratch, limit=32 * MIB, aliases=(), cost=0):
     specs = [spec for spec, _ in operands]
     return pl.pallas_call(
         kernel,
@@ -476,8 +517,9 @@
         in_specs=specs,
         out_specs=out_specs,
         scratch_shapes=scratch,
+        input_output_aliases=dict(aliases),
         compiler_params=pltpu.CompilerParams(vmem_limit_bytes=limit),
-        cost_estimate=COST,
+        cost_estimate=pl.CostEstimate(flops=0, bytes_accessed=cost, transcendentals=0),
         name=name,
     )(*(value for _, value in operands))
 
@@ -520,12 +562,11 @@
     return [jax.ShapeDtypeStruct((count,) + raw.shape[1:], F32) for count in counts]
 
 
-def head(raw, flat, dark, count, halves, half_turn):
+def head(raw, flat, dark, halves, half_turn):
     block = raw.shape[0] // 4
     hi, lo = np_split(np.kron(mode_basis(block, half_turn).T, np.eye(8)))
     basis = np.concatenate([hi, hi, lo], axis=1)
-    shapes = piece_shapes(raw, [count])
-    shapes += [jax.ShapeDtypeStruct((KMAX, QUARTER, SIDE), F32)] * 2
+    shapes = [jax.ShapeDtypeStruct((KMAX, QUARTER, SIDE), F32)] * 2
     shapes += [jax.ShapeDtypeStruct((QUARTER, SIDE), F32)] * 2
     return call(
         functools.partial(head_kernel, halves, half_turn), "head",
@@ -534,8 +575,16 @@
             pltpu.VMEM(raw.shape, F32),
             pltpu.VMEM(flat.shape, F32),
             pltpu.VMEM(basis.shape, BF16),
-            pltpu.SemaphoreType.DMA((8,)),
+            pltpu.SemaphoreType.DMA((7,)),
         ],
+        cost=HEAD_COST,
+    )
+
+
+def first_piece(raw, count, halves):
+    return call(
+        functools.partial(piece_kernel, halves), "first_piece", far(raw),
+        piece_shapes(raw, [count])[0], VMEM_SPEC, [pltpu.SemaphoreType.DMA((1,))],
     )
 
 
@@ -554,7 +603,7 @@
     return call(
         functools.partial(early_kernel, halves, offset, next_offset, groups, len(after)), "early_sheets",
         operands, shapes, [VMEM_SPEC] * len(shapes),
-        [shifted_scratch(max(groups)), pltpu.SemaphoreType.DMA((max(len(counts), 1),))],
+        [shifted_scratch(sum(groups)), pltpu.SemaphoreType.DMA((max(len(counts), 1),))],
     )
 
 
@@ -579,20 +628,26 @@
     )
 
 
-def late_sheets(raw, partner, level, dark, modes, settings, groups, offset, halves, half_turn, finished=()):
+def late_sheets(
+    raw, partners, level, dark, modes, settings, groups, offset, halves, half_turn, finished, writes,
+):
     count = sum(groups)
-    operands = vmem(raw, partner, level, dark, modes, basis_pack(offset, count, half_turn))
-    operands += smem(settings) + table_operands("ramp") + vmem(*finished)
-    total = raw.shape[0] // 2 if finished else count
+    operands = vmem(raw, level, dark, modes, basis_pack(offset, count, half_turn))
+    operands += smem(settings) + vmem(*partners) + table_operands("ramp")
+    operands += vmem(*finished) if writes == "all" else [(ANY_SPEC, value) for value in finished]
+    total = raw.shape[0] // 2 if writes else count
     return call(
-        functools.partial(late_kernel, halves, offset, groups), "late_sheets", operands,
-        jax.ShapeDtypeStruct((total, HALF_SIDE, SIDE), F32),
-        ANY_SPEC if finished else VMEM_SPEC,
+        functools.partial(
+            late_kernel, halves, offset, groups, writes, len(finished), len(partners)
+        ),
+        "late_sheets", operands, jax.ShapeDtypeStruct((total, HALF_SIDE, SIDE), F32),
+        ANY_SPEC if writes else VMEM_SPEC,
         [
-            shifted_scratch(max(groups)),
+            shifted_scratch(sum(groups)),
             sheet_scratch(count),
             pltpu.SemaphoreType.DMA((len(finished) + len(groups),)),
         ],
+        aliases={len(operands) - 1: 0} if writes == "own" else {},
     )
 
 
@@ -606,12 +661,11 @@
     counts = [sum(groups) for groups in CHUNKS]
     starts = [sum(counts[:i]) for i in range(len(counts))]
     raw = intensity.reshape(angles, QUARTER, SIDE)
-    piece, mine, other, level, dark = head(
-        raw, flat_field.reshape(QUARTER, SIDE), dark_field.reshape(QUARTER, SIDE),
-        counts[0], halves, half_turn,
+    partners = [swapped(first_piece(raw, counts[0], halves), "angle", top_bit)]
+    mine, other, level, dark = head(
+        raw, flat_field.reshape(QUARTER, SIDE), dark_field.reshape(QUARTER, SIDE), halves, half_turn
     )
     settings = jnp.concatenate([correlation, blend_width, padding, cutoff])
-    partners = [swapped(piece, "angle", top_bit)]
     for bit in range(1, top_bit):
         mine = mine + swapped(mine, "angle", bit)
         other = other + swapped(other, "angle", bit)
@@ -634,15 +688,16 @@
     early = [first, second]
     parts = (mine_sum, other, other_more, far_mine, far_other)
     fixed, modes = middle_sheets(early, parts, settings, halves, half_turn, half_block)
-    finished = [fixed]
-    for i in range(2, len(CHUNKS)):
-        finished.append(
-            late_sheets(
-                raw, partners[i], level, dark, modes, settings, CHUNKS[i], starts[i],
-                halves, half_turn, finished if i == len(CHUNKS) - 1 else (),
-            )
-        )
-    return finished[-1].reshape(half_block, local_rows, 2 * pixels)
+    groups = CHUNKS[2] + CHUNKS[3]
+    out = late_sheets(
+        raw, partners[2:4], level, dark, modes, settings, groups, starts[2],
+        halves, half_turn, [fixed], "all",
+    )
+    out = late_sheets(
+        raw, partners[4:], level, dark, modes, settings, CHUNKS[4], starts[4],
+        halves, half_turn, [out], "own",
+    )
+    return out.reshape(half_block, local_rows, 2 * pixels)
 
 
 def solution(mesh):

time: 42.1 us -> 36.5 us (0.87)
  waiting for transfers between devices: 7.02 us -> 2.45 us
  Pallas kernels: 21 us -> 19.5 us
  starting transfers between devices: 10.9 us -> 11.4 us
    ppermute x9, waiting for transfers between devices: 7.02 us -> 2.45 us  [swapped(): return lax.ppermute(value, axis, pairs)]
    pallas_call x8, Pallas kernels: 21 us -> 19.5 us  [call(): pl.pallas_call(kernel, out_shape=out_shape, in_specs=specs, out_specs=out...]
    ppermute x9, starting transfers between devices: 10.9 us -> 11.4 us  [swapped(): return lax.ppermute(value, axis, pairs)]
  transfers between devices with their start and end apart: 9 -> 9, of which waited for: 2 -> 2; matrix products, arithmetic and copies ran while one was open for 0% -> 0% of each run, Pallas kernels for 35% -> 44%
where the time goes in v3:
time: 36.5 us; the launch traced here: 36.3 us
  Pallas kernels  19.5 us (53%)
  starting transfers between devices  11.4 us (31%)
  between operations  2.8 us (8%)
  waiting for transfers between devices  2.45 us (7%)
    pallas_call x8, Pallas kernels, call(): pl.pallas_call(kernel, out_shape=out_shape, in_specs=specs, out_specs=out...  19.5 us
    ppermute x9, starting transfers between devices, swapped(): return lax.ppermute(value, axis, pairs)  11.4 us
    ppermute x9, waiting for transfers between devices, swapped(): return lax.ppermute(value, axis, pairs)  2.45 us
  transfers between devices with their start and end apart: 9, of which 2 were waited for; matrix products, arithmetic and copies ran while one was open for 0% of the time, Pallas kernels for 44%

profile of v3, /device:TPU:0, one launch (start us, length us, event | category | flops | bytes accessed | tf_op | source)
XLA Modules:
  0.0 36.3 jit_solution(16021758593129118695)
XLA Ops:
  0.0 1.2 %first_piece.1 = f32[24,32,128]{2,1,0:T(8,128)S(1)} custom-call(f32[128,32,128]{2,1,0:T(8,128)} %bitcast.4), custom_call_target="tpu_custom_call" | custom-call | tf_op jit(solution)/shard_map/first_piece/pallas_call | solution.py:514
  1.2 3.0 %collective-permute-start.4 = (f32[24,32,128]{2,1,0:T(8,128)S(1)}, f32[24,32,128]{2,1,0:T(8,128)S(1)}, u32[]{:S(2)}, u32[]{:S(2)}) collective-permute-start(f32[24,32,128]{2,1,0:T(8,128)S(1)} %first_piece.1), channel_id=1, source_target_pairs={{0,16},{8,24},{16,0},{24,8},{1,17},{9,25},{17,1},{25,9},{2,18},{10... | collective-permute-start | bytes 1179656 | tf_op jit(solution)/shard_map/ppermute | solution.py:28
  4.2 0.0 copy-start.5
  4.2 0.0 copy-start.6
  4.2 0.0 copy-start.7
  4.2 2.9 %head.1 = (f32[8,32,128]{2,1,0:T(8,128)S(1)}, f32[8,32,128]{2,1,0:T(8,128)S(1)}, f32[32,128]{1,0:T(8,128)S(1)}, f32[32,128]{1,0:T(8,128)S(1)}) custom-call(f32[128,32,128]{2,1,0:T(8,128)} %bitcast.5, f32[32,128]{1,0:T(8,128)} %bitcast.11, f32[32,128]{1,0:T(8,128)} %bitcast.12, bf16[128,768]{1,0:T(8,128)(2,1)} %constant.24.clone.basis_far), custom_call_target="tpu_custom_call" | custom-call | bytes 16777216 | tf_op jit(solution)/shard_map/head/pallas_call | solution.py:514
  7.1 1.6 %collective-permute-start = (f32[8,32,128]{2,1,0:T(8,128)S(1)}, f32[8,32,128]{2,1,0:T(8,128)S(1)}, u32[]{:S(2)}, u32[]{:S(2)}) collective-permute-start(f32[8,32,128]{2,1,0:T(8,128)S(1)} %get-tuple-element.21.other_a), channel_id=1, source_target_pairs={{0,8},{8,0},{16,24},{24,16},{1,9},{9,1},{17,25},{25,17},{2,10},{10... | collective-permute-start | bytes 393224 | tf_op jit(solution)/shard_map/ppermute | solution.py:28
  8.7 0.5 %collective-permute-start.1 = (f32[8,32,128]{2,1,0:T(8,128)S(1)}, f32[8,32,128]{2,1,0:T(8,128)S(1)}, u32[]{:S(2)}, u32[]{:S(2)}) collective-permute-start(f32[8,32,128]{2,1,0:T(8,128)S(1)} %get-tuple-element.20.mine), channel_id=1, source_target_pairs={{0,8},{8,0},{16,24},{24,16},{1,9},{9,1},{17,25},{25,17},{2,10},{10... | collective-permute-start | bytes 393224 | tf_op jit(solution)/shard_map/ppermute | solution.py:28
  11.8 1.7 %collective-permute-done.received = f32[8,32,128]{2,1,0:T(8,128)S(1)} collective-permute-done((f32[8,32,128]{2,1,0:T(8,128)S(1)}, f32[8,32,128]{2,1,0:T(8,128)S(1)}, u32[]{:S(2)}, u32[]{:S(2)}) %collective-permute-start) | collective-permute-done | bytes 131104 | tf_op jit(solution)/shard_map/ppermute | solution.py:28
  13.5 0.2 add_modes.1
  13.8 0.1 collective-permute-start.2
  13.9 2.0 %collective-permute-start.5 = (f32[10,32,128]{2,1,0:T(8,128)S(1)}, f32[10,32,128]{2,1,0:T(8,128)S(1)}, u32[]{:S(2)}, u32[]{:S(2)}) collective-permute-start(f32[10,32,128]{2,1,0:T(8,128)S(1)} %get-tuple-element.24), channel_id=1, source_target_pairs={{0,16},{8,24},{16,0},{24,8},{1,17},{9,25},{17,1},{25,9},{2,18},{10... | collective-permute-start | bytes 491528 | tf_op jit(solution)/shard_map/ppermute | solution.py:28
  15.9 0.1 pad_add_fusion.settings
  15.9 0.0 collective-permute-done.1.refs_1_.other_b
  15.9 0.0 collective-permute-done.4.partner
  16.0 3.7 %early_sheets.2 = (f32[24,64,128]{2,1,0:T(8,128)S(1)}, f32[12,32,128]{2,1,0:T(8,128)S(1)}, f32[10,32,128]{2,1,0:T(8,128)S(1)}) custom-call(f32[128,32,128]{2,1,0:T(8,128)S(1)} %bitcast.7, f32[24,32,128]{2,1,0:T(8,128)S(1)} %collective-permute-done.4.partner, f32[32,128]{1,0:T(8,128)S(1)} %get-tuple-element.18.level, f32[32,128]{1,0:T(8,128)S(1)} %get-tuple-element.19.dark, ...), custom_call_target="tpu_custom_call" | custom-call | tf_op jit(solution)/shard_map/early_sheets/pallas_call | solution.py:514
  19.7 0.1 collective-permute-start.7
  19.9 1.9 %collective-permute-start.8 = (f32[10,32,128]{2,1,0:T(8,128)S(1)}, f32[10,32,128]{2,1,0:T(8,128)S(1)}, u32[]{:S(2)}, u32[]{:S(2)}) collective-permute-start(f32[10,32,128]{2,1,0:T(8,128)S(1)} %get-tuple-element.29), channel_id=1, source_target_pairs={{0,16},{8,24},{16,0},{24,8},{1,17},{9,25},{17,1},{25,9},{2,18},{10... | collective-permute-start | bytes 491528 | tf_op jit(solution)/shard_map/ppermute | solution.py:28
  21.8 0.0 collective-permute-done.2.refs_0_.far_mine
  21.8 1.5 %collective-permute-start.3 = (f32[8,32,128]{2,1,0:T(8,128)S(1)}, f32[8,32,128]{2,1,0:T(8,128)S(1)}, u32[]{:S(2)}, u32[]{:S(2)}) collective-permute-start(f32[8,32,128]{2,1,0:T(8,128)S(1)} %collective-permute-done.2.refs_0_.far_mine), channel_id=1, source_target_pairs={{0,8},{8,0},{16,24},{24,16},{1,9},{9,1},{17,25},{25,17},{2,10},{10... | collective-permute-start | bytes 393224 | tf_op jit(solution)/shard_map/ppermute | solution.py:28
  23.3 0.0 collective-permute-done.5.partner
  23.3 2.2 %early_sheets.3 = (f32[10,64,128]{2,1,0:T(8,128)S(1)}, f32[8,32,128]{2,1,0:T(8,128)S(1)}) custom-call(f32[128,32,128]{2,1,0:T(8,128)S(1)} %bitcast.8, f32[10,32,128]{2,1,0:T(8,128)S(1)} %collective-permute-done.5.partner, f32[32,128]{1,0:T(8,128)S(1)} %get-tuple-element.18.level, f32[32,128]{1,0:T(8,128)S(1)} %get-tuple-element.19.dark, ...), custom_call_target="tpu_custom_call" | custom-call | tf_op jit(solution)/shard_map/early_sheets/pallas_call | solution.py:514
  25.5 0.0 copy-start.9
  25.5 0.6 %collective-permute-start.6 = (f32[8,32,128]{2,1,0:T(8,128)S(1)}, f32[8,32,128]{2,1,0:T(8,128)S(1)}, u32[]{:S(2)}, u32[]{:S(2)}) collective-permute-start(f32[8,32,128]{2,1,0:T(8,128)S(1)} %get-tuple-element.27), channel_id=1, source_target_pairs={{0,16},{8,24},{16,0},{24,8},{1,17},{9,25},{17,1},{25,9},{2,18},{10... | collective-permute-start | bytes 393224 | tf_op jit(solution)/shard_map/ppermute | solution.py:28
  26.1 0.7 %collective-permute-done.3.far_other = f32[8,32,128]{2,1,0:T(8,128)S(1)} collective-permute-done((f32[8,32,128]{2,1,0:T(8,128)S(1)}, f32[8,32,128]{2,1,0:T(8,128)S(1)}, u32[]{:S(2)}, u32[]{:S(2)}) %collective-permute-start.3) | collective-permute-done | bytes 131104 | tf_op jit(solution)/shard_map/ppermute | solution.py:28
  26.8 2.9 %middle_sheets.1 = (f32[34,64,128]{2,1,0:T(8,128)S(1)}, bf16[384,1024]{1,0:T(8,128)(2,1)S(1)}) custom-call(f32[8,32,128]{2,1,0:T(8,128)S(1)} %get-tuple-element.22.refs_0_.mine, f32[8,32,128]{2,1,0:T(8,128)S(1)} %get-tuple-element.21.other_a, f32[8,32,128]{2,1,0:T(8,128)S(1)} %collective-permute-done.1.refs_1_.other_b, ...), custom_call_target="tpu_custom_call" | custom-call | tf_op jit(solution)/shard_map/middle_sheets/pallas_call | solution.py:514
  29.7 0.0 collective-permute-done.8.refs_1_
  29.7 0.0 collective-permute-done.7.refs_0_
  29.7 0.0 copy-start.11
  29.7 4.0 %late_sheets.2.refs_8_ = f32[64,64,128]{2,1,0:T(8,128)} custom-call(f32[128,32,128]{2,1,0:T(8,128)S(1)} %bitcast.9, f32[32,128]{1,0:T(8,128)S(1)} %get-tuple-element.18.level, f32[32,128]{1,0:T(8,128)S(1)} %get-tuple-element.19.dark, bf16[384,1024]{1,0:T(8,128)(2,1)S(1)} %get-tuple-element.26.modes, bf16[176,384]{1,0:T(8,128)(2,1)S(1)} %copy-done.9, ...), custom_call_target="tpu_custom_call" | custom-call | tf_op jit(solution)/shard_map/late_sheets/pallas_call | solution.py:514
  33.7 0.0 collective-permute-done.6.refs_0_
  33.8 2.5 %late_sheets.3 = f32[64,64,128]{2,1,0:T(8,128)} custom-call(f32[128,32,128]{2,1,0:T(8,128)S(1)} %bitcast.10, f32[32,128]{1,0:T(8,128)S(1)} %get-tuple-element.18.level, f32[32,128]{1,0:T(8,128)S(1)} %get-tuple-element.19.dark, bf16[384,1024]{1,0:T(8,128)(2,1)S(1)} %get-tuple-element.26.modes, ...), custom_call_target="tpu_custom_call", output_to_operand_aliasing={{}: (14, {})} | custom-call | tf_op jit(solution)/shard_map/late_sheets/pallas_call | solution.py:514
  (19 shorter events, 0.0 us)
Async XLA Ops:
  0.0 13.5 %copy-start = (f32[128,1,4096]{2,1,0:T(1,128)S(1)}, f32[128,1,4096]{2,1,0:T(1,128)}, u32[]{:S(2)}) copy-start(f32[128,1,4096]{2,1,0:T(1,128)} %param.19) | copy-start | bytes 6291460
  1.2 14.8 %collective-permute-start.4 = (f32[24,32,128]{2,1,0:T(8,128)S(1)}, f32[24,32,128]{2,1,0:T(8,128)S(1)}, u32[]{:S(2)}, u32[]{:S(2)}) collective-permute-start(f32[24,32,128]{2,1,0:T(8,128)S(1)} %first_piece.1), channel_id=1, source_target_pairs={{0,16},{8,24},{16,0},{24,8},{1,17},{9,25},{17,1},{25,9},{2,18},{10... | collective-permute-start | bytes 1179656 | tf_op jit(solution)/shard_map/ppermute | solution.py:28
  4.2 11.8 %copy-start.1 = (bf16[768,256]{1,0:T(8,128)(2,1)S(1)}, bf16[768,256]{1,0:T(8,128)(2,1)}, u32[]{:S(2)}) copy-start(bf16[768,256]{1,0:T(8,128)(2,1)} %constant.29.clone.refs_6_.refs_5_) | copy-start | bytes 1179652
  4.2 11.8 %copy-start.2 = (bf16[768,256]{1,0:T(8,128)(2,1)S(1)}, bf16[768,256]{1,0:T(8,128)(2,1)}, u32[]{:S(2)}) copy-start(bf16[768,256]{1,0:T(8,128)(2,1)} %constant.28.clone.refs_5_.refs_4_) | copy-start | bytes 1179652
  4.2 11.8 %copy-start.3 = (f32[128,256]{1,0:T(8,128)S(1)}, f32[128,256]{1,0:T(8,128)}, u32[]{:S(2)}) copy-start(f32[128,256]{1,0:T(8,128)} %constant.27.clone.refs_4_.refs_3_) | copy-start | bytes 393220
  4.2 11.8 %copy-start.4 = (f32[128,256]{1,0:T(8,128)S(1)}, f32[128,256]{1,0:T(8,128)}, u32[]{:S(2)}) copy-start(f32[128,256]{1,0:T(8,128)} %constant.31.clone.refs_8_.refs_7_) | copy-start | bytes 393220
  4.2 11.8 %copy-start.5 = (bf16[128,192]{1,0:T(8,128)(2,1)S(1)}, bf16[128,192]{1,0:T(8,128)(2,1)}, u32[]{:S(2)}) copy-start(bf16[128,192]{1,0:T(8,128)(2,1)} %constant.25.clone.refs_2_.refs_1_) | copy-start | bytes 147460
  4.2 11.8 %copy-start.6 = (bf16[64,384]{1,0:T(8,128)(2,1)S(1)}, bf16[64,384]{1,0:T(8,128)(2,1)}, u32[]{:S(2)}) copy-start(bf16[64,384]{1,0:T(8,128)(2,1)} %constant.30.clone.refs_7_.refs_6_) | copy-start | bytes 147460
  4.2 11.8 %copy-start.7 = (bf16[128,128]{1,0:T(8,128)(2,1)S(1)}, bf16[128,128]{1,0:T(8,128)(2,1)}, u32[]{:S(2)}) copy-start(bf16[128,128]{1,0:T(8,128)(2,1)} %constant.26.clone.refs_3_.refs_2_) | copy-start | bytes 98308
  7.1 6.4 %collective-permute-start = (f32[8,32,128]{2,1,0:T(8,128)S(1)}, f32[8,32,128]{2,1,0:T(8,128)S(1)}, u32[]{:S(2)}, u32[]{:S(2)}) collective-permute-start(f32[8,32,128]{2,1,0:T(8,128)S(1)} %get-tuple-element.21.other_a), channel_id=1, source_target_pairs={{0,8},{8,0},{16,24},{24,16},{1,9},{9,1},{17,25},{25,17},{2,10},{10... | collective-permute-start | bytes 393224 | tf_op jit(solution)/shard_map/ppermute | solution.py:28
  8.7 7.3 %collective-permute-start.1 = (f32[8,32,128]{2,1,0:T(8,128)S(1)}, f32[8,32,128]{2,1,0:T(8,128)S(1)}, u32[]{:S(2)}, u32[]{:S(2)}) collective-permute-start(f32[8,32,128]{2,1,0:T(8,128)S(1)} %get-tuple-element.20.mine), channel_id=1, source_target_pairs={{0,8},{8,0},{16,24},{24,16},{1,9},{9,1},{17,25},{25,17},{2,10},{10... | collective-permute-start | bytes 393224 | tf_op jit(solution)/shard_map/ppermute | solution.py:28
  13.8 8.1 %collective-permute-start.2 = (f32[8,32,128]{2,1,0:T(8,128)S(1)}, f32[8,32,128]{2,1,0:T(8,128)S(1)}, u32[]{:S(2)}, u32[]{:S(2)}) collective-permute-start(f32[8,32,128]{2,1,0:T(8,128)S(1)} %get-tuple-element.22.refs_0_.mine), channel_id=1, source_target_pairs={{0,16},{8,24},{16,0},{24,8},{1,17},{9,25},{17,1},{25,9},{2,18},{10... | collective-permute-start | bytes 393224 | tf_op jit(solution)/shard_map/ppermute | solution.py:28
  13.9 9.4 %collective-permute-start.5 = (f32[10,32,128]{2,1,0:T(8,128)S(1)}, f32[10,32,128]{2,1,0:T(8,128)S(1)}, u32[]{:S(2)}, u32[]{:S(2)}) collective-permute-start(f32[10,32,128]{2,1,0:T(8,128)S(1)} %get-tuple-element.24), channel_id=1, source_target_pairs={{0,16},{8,24},{16,0},{24,8},{1,17},{9,25},{17,1},{25,9},{2,18},{10... | collective-permute-start | bytes 491528 | tf_op jit(solution)/shard_map/ppermute | solution.py:28
  19.7 10.0 %collective-permute-start.7 = (f32[12,32,128]{2,1,0:T(8,128)S(1)}, f32[12,32,128]{2,1,0:T(8,128)S(1)}, u32[]{:S(2)}, u32[]{:S(2)}) collective-permute-start(f32[12,32,128]{2,1,0:T(8,128)S(1)} %get-tuple-element.28), channel_id=1, source_target_pairs={{0,16},{8,24},{16,0},{24,8},{1,17},{9,25},{17,1},{25,9},{2,18},{10... | collective-permute-start | bytes 589832 | tf_op jit(solution)/shard_map/ppermute | solution.py:28
  19.9 9.8 %collective-permute-start.8 = (f32[10,32,128]{2,1,0:T(8,128)S(1)}, f32[10,32,128]{2,1,0:T(8,128)S(1)}, u32[]{:S(2)}, u32[]{:S(2)}) collective-permute-start(f32[10,32,128]{2,1,0:T(8,128)S(1)} %get-tuple-element.29), channel_id=1, source_target_pairs={{0,16},{8,24},{16,0},{24,8},{1,17},{9,25},{17,1},{25,9},{2,18},{10... | collective-permute-start | bytes 491528 | tf_op jit(solution)/shard_map/ppermute | solution.py:28
  21.8 5.0 %collective-permute-start.3 = (f32[8,32,128]{2,1,0:T(8,128)S(1)}, f32[8,32,128]{2,1,0:T(8,128)S(1)}, u32[]{:S(2)}, u32[]{:S(2)}) collective-permute-start(f32[8,32,128]{2,1,0:T(8,128)S(1)} %collective-permute-done.2.refs_0_.far_mine), channel_id=1, source_target_pairs={{0,8},{8,0},{16,24},{24,16},{1,9},{9,1},{17,25},{25,17},{2,10},{10... | collective-permute-start | bytes 393224 | tf_op jit(solution)/shard_map/ppermute | solution.py:28
  23.3 3.5 %copy-start.8 = (bf16[272,384]{1,0:T(8,128)(2,1)S(1)}, bf16[272,384]{1,0:T(8,128)(2,1)}, u32[]{:S(2)}) copy-start(bf16[272,384]{1,0:T(8,128)(2,1)} %constant.32.clone.basis) | copy-start | bytes 626692
  23.3 3.5 %copy-start.10 = (f32[128,256]{1,0:T(8,128)S(1)}, f32[128,256]{1,0:T(8,128)}, u32[]{:S(2)}) copy-start(f32[128,256]{1,0:T(8,128)} %constant.33.clone.refs_8_) | copy-start | bytes 393220
  25.5 4.2 %copy-start.9 = (bf16[176,384]{1,0:T(8,128)(2,1)S(1)}, bf16[176,384]{1,0:T(8,128)(2,1)}, u32[]{:S(2)}) copy-start(bf16[176,384]{1,0:T(8,128)(2,1)} %constant.34.clone.basis) | copy-start | bytes 405508
  25.5 8.2 %collective-permute-start.6 = (f32[8,32,128]{2,1,0:T(8,128)S(1)}, f32[8,32,128]{2,1,0:T(8,128)S(1)}, u32[]{:S(2)}, u32[]{:S(2)}) collective-permute-start(f32[8,32,128]{2,1,0:T(8,128)S(1)} %get-tuple-element.27), channel_id=1, source_target_pairs={{0,16},{8,24},{16,0},{24,8},{1,17},{9,25},{17,1},{25,9},{2,18},{10... | collective-permute-start | bytes 393224 | tf_op jit(solution)/shard_map/ppermute | solution.py:28
  29.7 4.0 %copy-start.11 = (bf16[64,384]{1,0:T(8,128)(2,1)S(1)}, bf16[64,384]{1,0:T(8,128)(2,1)}, u32[]{:S(2)}) copy-start(bf16[64,384]{1,0:T(8,128)(2,1)} %constant.35.clone.basis) | copy-start | bytes 147460

commit v4 on v3

--- a/solution.py
+++ b/solution.py
@@ -17,7 +17,7 @@
 QUARTER = SIDE // 4
 MODES = 2 * KMAX
 MODE_GROUP = 8
-CHUNKS = ((8,8,8),(6,4),(6,6),(6,4),(4,4))
+CHUNKS = ((8,8,10),(6,4),(6,6),(4,4),(4,4))
 BF16 = jnp.bfloat16
 F32 = jnp.float32
 
@@ -322,7 +322,8 @@
     start_pieces(halves, 0, raw_far, [piece], sems)[0].wait()
 
 
-def add_kernel(halves, offset, raw, mine, received, total, *refs):
+def add_kernel(halves, offset, raw, mine, received, *refs):
+    total, *refs = refs[4:]
     pieces, sems = refs[:-1], refs[-1]
     copies = start_pieces(halves, offset, raw, pieces, sems)
     total[...] = mine[...] + received[...]
@@ -385,7 +386,10 @@
     return block
 
 
-def clean_rows(halves, offset, groups, raw, partner, level, dark, weight, correlation, edges, tables, shifted, emit):
+def clean_rows(
+    halves, offset, groups, raw, partner, level, dark, weight, correlation, edges, tables, shifted, emit,
+    beside=(),
+):
     is_upper = lax.axis_index("angle") >= halves
     start = jnp.where(is_upper, raw.shape[0] // 2, 0) + offset
 
@@ -398,13 +402,14 @@
         return load
 
     firsts = [sum(groups[:i]) for i in range(len(groups))]
-    take_turns(
+    turns = [
         transform_group(
             [view(i) for i in range(first, first + size)],
             weight, correlation, edges, tables, tables["ramp"], shifted, first, emit,
         )
         for first, size in zip(firsts, groups)
-    )
+    ]
+    take_turns(turns + list(beside))
 
 
 def prepare(settings, tables, shifted):
@@ -414,8 +419,9 @@
 
 
 def early_kernel(
-    halves, offset, next_offset, groups, waits, raw, partner, level, dark, settings, *refs,
+    halves, offset, next_offset, groups, waits, raw, partner, level, dark, *refs,
 ):
+    settings, refs = [ref[0] for ref in refs[:4]], refs[4:]
     refs = refs[waits:]
     names = TABLES + ("ramp",)
     tables = dict(zip(names, refs))
@@ -436,8 +442,9 @@
 
 def middle_kernel(
     halves, half_turn, starts, early_count, mine, other_a, other_b, far_mine, far_other, basis,
-    settings, *refs,
+    *refs,
 ):
+    settings, refs = [ref[0] for ref in refs[:4]], refs[4:]
     names = TABLES + ("ramp_drop",)
     early, refs = refs[:early_count], refs[early_count:]
     tables = dict(zip(names, refs))
@@ -466,37 +473,41 @@
 
 
 def late_kernel(
-    halves, offset, groups, writes, finished_count, partner_count, raw, level, dark, modes, basis, settings, *refs,
+    halves, offset, groups, partner_count, writes, raw, level, dark, modes, basis, finished, *refs,
 ):
+    settings, refs = [ref[0] for ref in refs[:4]], refs[4:]
     names = TABLES + ("ramp",)
     partner, refs = Joined(refs[:partner_count]), refs[partner_count:]
     tables = dict(zip(names, refs))
-    finished = refs[len(names) : len(names) + finished_count]
-    out, shifted, done, sems = refs[-4:]
+    refs = refs[len(names) :]
+    out, done, shifted, sems = refs[1:] if writes else refs
     copies = []
 
-    def send(source, target):
+    def send(source, first):
+        target = out.at[pl.ds(first, source.shape[0])]
         copies.append(pltpu.make_async_copy(source, target, sems.at[len(copies)]))
         copies[-1].start()
 
-    row = 0
-    if writes == "all":
-        for part in finished:
-            send(part, out.at[pl.ds(row, part.shape[0])])
-            row += part.shape[0]
+    send(finished, offset - finished.shape[0])
     weight, edges = prepare(settings, tables, shifted)
-    low = low_sheets(basis[...], modes[...])
-    target = done if writes else out
+    lows = []
+
+    def low_turn():
+        lows.append(low_sheets(basis[...], modes[...]))
+        yield
 
     def emit(first, sheets):
         for i, sheet in enumerate(sheets):
             for j in range(HALF_SIDE // 8):
-                target[first + i, 8 * j : 8 * j + 8, :] = sheet[8 * j : 8 * j + 8] - low(first + i, j)
+                done[first + i, 8 * j : 8 * j + 8, :] = (
+                    sheet[8 * j : 8 * j + 8] - lows[0](first + i, j)
+                )
         if writes:
-            send(done.at[pl.ds(first, len(sheets))], out.at[pl.ds(offset + first, len(sheets))])
+            send(done.at[pl.ds(first, len(sheets))], offset + first)
 
     clean_rows(
-        halves, offset, groups, raw, partner, level, dark, weight, settings[0], edges, tables, shifted, emit
+        halves, offset, groups, raw, partner, level, dark, weight, settings[0], edges, tables, shifted, emit,
+        [low_turn()],
     )
     for copy in copies:
         copy.wait()
@@ -588,16 +599,17 @@
     )
 
 
-def add_modes(raw, mine, received, counts, offset, halves):
+def add_modes(raw, mine, received, settings, counts, offset, halves):
     shapes = [jax.ShapeDtypeStruct(mine.shape, F32)] + piece_shapes(raw, counts)
     return call(
-        functools.partial(add_kernel, halves, offset), "add_modes", vmem(raw, mine, received),
+        functools.partial(add_kernel, halves, offset), "add_modes",
+        vmem(raw, mine, received) + smem(*settings),
         shapes, [VMEM_SPEC] * len(shapes), [pltpu.SemaphoreType.DMA((len(counts),))],
     )
 
 
 def early_sheets(raw, partner, level, dark, after, settings, groups, offset, counts, next_offset, halves):
-    operands = vmem(raw, partner, level, dark) + smem(settings)
+    operands = vmem(raw, partner, level, dark) + smem(*settings)
     operands += [(ANY_SPEC, value) for value in after] + table_operands("ramp")
     shapes = [jax.ShapeDtypeStruct((sum(groups), HALF_SIDE, SIDE), F32)] + piece_shapes(raw, counts)
     return call(
@@ -611,7 +623,7 @@
     count = sum(part.shape[0] for part in early)
     place = np.arange(2 * halves)
     starts = place % halves * 2 * half_block + place // halves * half_block
-    operands = vmem(*parts, basis_pack(0, count, half_turn)) + smem(settings)
+    operands = vmem(*parts, basis_pack(0, count, half_turn)) + smem(*settings)
     operands += vmem(*early) + table_operands("ramp_drop")
     return call(
         functools.partial(middle_kernel, halves, half_turn, starts, len(early)), "middle_sheets", operands,
@@ -629,25 +641,24 @@
 
 
 def late_sheets(
-    raw, partners, level, dark, modes, settings, groups, offset, halves, half_turn, finished, writes,
+    raw, partners, level, dark, modes, settings, groups, offset, halves, half_turn, finished, out=None,
 ):
     count = sum(groups)
-    operands = vmem(raw, level, dark, modes, basis_pack(offset, count, half_turn))
-    operands += smem(settings) + vmem(*partners) + table_operands("ramp")
-    operands += vmem(*finished) if writes == "all" else [(ANY_SPEC, value) for value in finished]
-    total = raw.shape[0] // 2 if writes else count
+    writes = out is not None
+    operands = vmem(raw, level, dark, modes, basis_pack(offset, count, half_turn), finished)
+    operands += smem(*settings) + vmem(*partners) + table_operands("ramp")
+    aliases = {}
+    if writes:
+        aliases = {len(operands): 0}
+        operands.append((ANY_SPEC, out))
+    result = jax.ShapeDtypeStruct((raw.shape[0] // 2, HALF_SIDE, SIDE), F32)
+    rows = jax.ShapeDtypeStruct((count, HALF_SIDE, SIDE), F32)
+    scratch = [shifted_scratch(count), pltpu.SemaphoreType.DMA((1 + len(groups),))]
     return call(
-        functools.partial(
-            late_kernel, halves, offset, groups, writes, len(finished), len(partners)
-        ),
-        "late_sheets", operands, jax.ShapeDtypeStruct((total, HALF_SIDE, SIDE), F32),
-        ANY_SPEC if writes else VMEM_SPEC,
-        [
-            shifted_scratch(sum(groups)),
-            sheet_scratch(count),
-            pltpu.SemaphoreType.DMA((len(finished) + len(groups),)),
-        ],
-        aliases={len(operands) - 1: 0} if writes == "own" else {},
+        functools.partial(late_kernel, halves, offset, groups, len(partners), writes), "late_sheets",
+        operands, [result] if writes else [result, rows],
+        [ANY_SPEC] if writes else [ANY_SPEC, VMEM_SPEC],
+        [sheet_scratch(count)] * writes + scratch, aliases=aliases,
     )
 
 
@@ -665,13 +676,13 @@
     mine, other, level, dark = head(
         raw, flat_field.reshape(QUARTER, SIDE), dark_field.reshape(QUARTER, SIDE), halves, half_turn
     )
-    settings = jnp.concatenate([correlation, blend_width, padding, cutoff])
+    settings = (correlation, blend_width, padding, cutoff)
     for bit in range(1, top_bit):
         mine = mine + swapped(mine, "angle", bit)
         other = other + swapped(other, "angle", bit)
     received = swapped(other, "angle", 0)
     other_more = swapped(mine, "angle", 0)
-    mine_sum, piece = add_modes(raw, mine, received, counts[1:2], starts[1], halves)
+    mine_sum, piece = add_modes(raw, mine, received, settings, counts[1:2], starts[1], halves)
     partners.append(swapped(piece, "angle", top_bit))
     far_mine = swapped(mine_sum, "angle", top_bit)
     first, *pieces = early_sheets(
@@ -688,14 +699,13 @@
     early = [first, second]
     parts = (mine_sum, other, other_more, far_mine, far_other)
     fixed, modes = middle_sheets(early, parts, settings, halves, half_turn, half_block)
-    groups = CHUNKS[2] + CHUNKS[3]
-    out = late_sheets(
-        raw, partners[2:4], level, dark, modes, settings, groups, starts[2],
-        halves, half_turn, [fixed], "all",
-    )
-    out = late_sheets(
+    out, late = late_sheets(
+        raw, partners[2:4], level, dark, modes, settings, CHUNKS[2] + CHUNKS[3], starts[2],
+        halves, half_turn, fixed,
+    )
+    (out,) = late_sheets(
         raw, partners[4:], level, dark, modes, settings, CHUNKS[4], starts[4],
-        halves, half_turn, [out], "own",
+        halves, half_turn, late, out,
     )
     return out.reshape(half_block, local_rows, 2 * pixels)
 

time: 36.5 us -> 34.1 us (0.934)
  Pallas kernels: 19.5 us -> 16.4 us
  starting transfers between devices: 11.4 us -> 11.9 us
    pallas_call x8, Pallas kernels: 19.5 us -> 16.4 us  [call(): pl.pallas_call(kernel, out_shape=out_shape, in_specs=specs, out_specs=out...]
    ppermute x9, starting transfers between devices: 11.4 us -> 11.9 us  [swapped(): return lax.ppermute(value, axis, pairs)]
  transfers between devices with their start and end apart: 9 -> 9, of which waited for: 2 -> 2; matrix products, arithmetic and copies ran while one was open for 0% -> 0% of each run, Pallas kernels for 44% -> 39%
where the time goes in v4:
time: 34.1 us; the launch traced here: 33.9 us
  Pallas kernels  16.4 us (48%)
  starting transfers between devices  11.9 us (35%)
  waiting for transfers between devices  2.79 us (8%)
  between operations  2.78 us (8%)
    pallas_call x8, Pallas kernels, call(): pl.pallas_call(kernel, out_shape=out_shape, in_specs=specs, out_specs=out...  16.4 us
    ppermute x9, starting transfers between devices, swapped(): return lax.ppermute(value, axis, pairs)  11.9 us
    ppermute x9, waiting for transfers between devices, swapped(): return lax.ppermute(value, axis, pairs)  2.79 us
  transfers between devices with their start and end apart: 9, of which 2 were waited for; matrix products, arithmetic and copies ran while one was open for 0% of the time, Pallas kernels for 39%

profile of v4, /device:TPU:0, one launch (start us, length us, event | category | flops | bytes accessed | tf_op | source)
XLA Modules:
  0.0 33.9 jit_solution(8126362299848905353)
XLA Ops:
  0.0 1.2 %first_piece.1 = f32[26,32,128]{2,1,0:T(8,128)S(1)} custom-call(f32[128,32,128]{2,1,0:T(8,128)} %bitcast.4), custom_call_target="tpu_custom_call" | custom-call | tf_op jit(solution)/shard_map/first_piece/pallas_call | solution.py:525
  1.2 3.0 %collective-permute-start.4 = (f32[26,32,128]{2,1,0:T(8,128)S(1)}, f32[26,32,128]{2,1,0:T(8,128)S(1)}, u32[]{:S(2)}, u32[]{:S(2)}) collective-permute-start(f32[26,32,128]{2,1,0:T(8,128)S(1)} %first_piece.1), channel_id=1, source_target_pairs={{0,16},{8,24},{16,0},{24,8},{1,17},{9,25},{17,1},{25,9},{2,18},{10... | collective-permute-start | bytes 1277960 | tf_op jit(solution)/shard_map/ppermute | solution.py:28
  4.2 0.0 copy-start.5
  4.2 0.0 copy-start.6
  4.2 0.0 copy-start.7
  4.3 2.9 %head.1 = (f32[8,32,128]{2,1,0:T(8,128)S(1)}, f32[8,32,128]{2,1,0:T(8,128)S(1)}, f32[32,128]{1,0:T(8,128)S(1)}, f32[32,128]{1,0:T(8,128)S(1)}) custom-call(f32[128,32,128]{2,1,0:T(8,128)} %bitcast.5, f32[32,128]{1,0:T(8,128)} %bitcast.11, f32[32,128]{1,0:T(8,128)} %bitcast.12, bf16[128,768]{1,0:T(8,128)(2,1)} %constant.24.clone.basis_far), custom_call_target="tpu_custom_call" | custom-call | bytes 16777216 | tf_op jit(solution)/shard_map/head/pallas_call | solution.py:525
  7.1 1.6 %collective-permute-start = (f32[8,32,128]{2,1,0:T(8,128)S(1)}, f32[8,32,128]{2,1,0:T(8,128)S(1)}, u32[]{:S(2)}, u32[]{:S(2)}) collective-permute-start(f32[8,32,128]{2,1,0:T(8,128)S(1)} %get-tuple-element.23.other_a), channel_id=1, source_target_pairs={{0,8},{8,0},{16,24},{24,16},{1,9},{9,1},{17,25},{25,17},{2,10},{10... | collective-permute-start | bytes 393224 | tf_op jit(solution)/shard_map/ppermute | solution.py:28
  8.7 0.5 %collective-permute-start.1 = (f32[8,32,128]{2,1,0:T(8,128)S(1)}, f32[8,32,128]{2,1,0:T(8,128)S(1)}, u32[]{:S(2)}, u32[]{:S(2)}) collective-permute-start(f32[8,32,128]{2,1,0:T(8,128)S(1)} %get-tuple-element.22.mine), channel_id=1, source_target_pairs={{0,8},{8,0},{16,24},{24,16},{1,9},{9,1},{17,25},{25,17},{2,10},{10... | collective-permute-start | bytes 393224 | tf_op jit(solution)/shard_map/ppermute | solution.py:28
  11.8 1.7 %collective-permute-done.received = f32[8,32,128]{2,1,0:T(8,128)S(1)} collective-permute-done((f32[8,32,128]{2,1,0:T(8,128)S(1)}, f32[8,32,128]{2,1,0:T(8,128)S(1)}, u32[]{:S(2)}, u32[]{:S(2)}) %collective-permute-start) | collective-permute-done | bytes 131104 | tf_op jit(solution)/shard_map/ppermute | solution.py:28
  13.5 0.2 add_modes.1
  13.8 0.1 collective-permute-start.5
  13.9 2.0 %collective-permute-start.2 = (f32[8,32,128]{2,1,0:T(8,128)S(1)}, f32[8,32,128]{2,1,0:T(8,128)S(1)}, u32[]{:S(2)}, u32[]{:S(2)}) collective-permute-start(f32[8,32,128]{2,1,0:T(8,128)S(1)} %get-tuple-element.24.refs_4_.mine), channel_id=1, source_target_pairs={{0,16},{8,24},{16,0},{24,8},{1,17},{9,25},{17,1},{25,9},{2,18},{10... | collective-permute-start | bytes 393224 | tf_op jit(solution)/shard_map/ppermute | solution.py:28
  15.9 0.0 collective-permute-done.1.refs_5_.other_b
  15.9 0.0 collective-permute-done.4.partner
  15.9 0.0 copy-done.2
  15.9 3.3 %early_sheets.2 = (f32[26,64,128]{2,1,0:T(8,128)S(1)}, f32[12,32,128]{2,1,0:T(8,128)S(1)}, f32[8,32,128]{2,1,0:T(8,128)S(1)}) custom-call(f32[128,32,128]{2,1,0:T(8,128)S(1)} %bitcast.7, f32[26,32,128]{2,1,0:T(8,128)S(1)} %collective-permute-done.4.partner, f32[32,128]{1,0:T(8,128)S(1)} %get-tuple-element.20.level, f32[32,128]{1,0:T(8,128)S(1)} %get-tuple-element.21.dark, ...), custom_call_target="tpu_custom_call" | custom-call | tf_op jit(solution)/shard_map/early_sheets/pallas_call | solution.py:525
  19.3 1.1 %collective-permute-start.6 = (f32[12,32,128]{2,1,0:T(8,128)S(1)}, f32[12,32,128]{2,1,0:T(8,128)S(1)}, u32[]{:S(2)}, u32[]{:S(2)}) collective-permute-start(f32[12,32,128]{2,1,0:T(8,128)S(1)} %get-tuple-element.30), channel_id=1, source_target_pairs={{0,16},{8,24},{16,0},{24,8},{1,17},{9,25},{17,1},{25,9},{2,18},{10... | collective-permute-start | bytes 589832 | tf_op jit(solution)/shard_map/ppermute | solution.py:28
  20.4 1.0 %collective-permute-done.2.refs_4_.far_mine = f32[8,32,128]{2,1,0:T(8,128)S(1)} collective-permute-done((f32[8,32,128]{2,1,0:T(8,128)S(1)}, f32[8,32,128]{2,1,0:T(8,128)S(1)}, u32[]{:S(2)}, u32[]{:S(2)}) %collective-permute-start.2) | collective-permute-done | bytes 131104 | tf_op jit(solution)/shard_map/ppermute | solution.py:28
  21.4 1.5 %collective-permute-start.3 = (f32[8,32,128]{2,1,0:T(8,128)S(1)}, f32[8,32,128]{2,1,0:T(8,128)S(1)}, u32[]{:S(2)}, u32[]{:S(2)}) collective-permute-start(f32[8,32,128]{2,1,0:T(8,128)S(1)} %collective-permute-done.2.refs_4_.far_mine), channel_id=1, source_target_pairs={{0,8},{8,0},{16,24},{24,16},{1,9},{9,1},{17,25},{25,17},{2,10},{10... | collective-permute-start | bytes 393224 | tf_op jit(solution)/shard_map/ppermute | solution.py:28
  22.9 1.9 %collective-permute-start.7 = (f32[8,32,128]{2,1,0:T(8,128)S(1)}, f32[8,32,128]{2,1,0:T(8,128)S(1)}, u32[]{:S(2)}, u32[]{:S(2)}) collective-permute-start(f32[8,32,128]{2,1,0:T(8,128)S(1)} %get-tuple-element.31), channel_id=1, source_target_pairs={{0,16},{8,24},{16,0},{24,8},{1,17},{9,25},{17,1},{25,9},{2,18},{10... | collective-permute-start | bytes 393224 | tf_op jit(solution)/shard_map/ppermute | solution.py:28
  24.8 0.0 collective-permute-done.5.partner
  24.8 1.6 %early_sheets.3 = (f32[10,64,128]{2,1,0:T(8,128)S(1)}, f32[8,32,128]{2,1,0:T(8,128)S(1)}) custom-call(f32[128,32,128]{2,1,0:T(8,128)S(1)} %bitcast.8, f32[10,32,128]{2,1,0:T(8,128)S(1)} %collective-permute-done.5.partner, f32[32,128]{1,0:T(8,128)S(1)} %get-tuple-element.20.level, f32[32,128]{1,0:T(8,128)S(1)} %get-tuple-element.21.dark, s32[1]{0:T(128)S(6)} %copy.23.refs_0_, ...), custom_call_target="tpu_custom_call" | custom-call | tf_op jit(solution)/shard_map/early_sheets/pallas_call | solution.py:525
  26.4 0.0 copy-start.10
  26.4 0.2 collective-permute-start.8
  26.6 0.0 collective-permute-done.3.far_other
  26.6 2.3 %middle_sheets.1 = (f32[36,64,128]{2,1,0:T(8,128)S(1)}, bf16[384,1024]{1,0:T(8,128)(2,1)S(1)}) custom-call(f32[8,32,128]{2,1,0:T(8,128)S(1)} %get-tuple-element.24.refs_4_.mine, f32[8,32,128]{2,1,0:T(8,128)S(1)} %get-tuple-element.23.other_a, f32[8,32,128]{2,1,0:T(8,128)S(1)} %collective-permute-done.1.refs_5_.other_b, ...), custom_call_target="tpu_custom_call" | custom-call | tf_op jit(solution)/shard_map/middle_sheets/pallas_call | solution.py:525
  29.0 0.0 collective-permute-done.7.refs_5_
  29.0 0.0 collective-permute-done.6.refs_4_
  29.0 0.0 copy-start.11
  29.0 2.8 %late_sheets.2 = (f32[64,64,128]{2,1,0:T(8,128)}, f32[20,64,128]{2,1,0:T(8,128)S(1)}) custom-call(f32[128,32,128]{2,1,0:T(8,128)S(1)} %bitcast.9, f32[32,128]{1,0:T(8,128)S(1)} %get-tuple-element.20.level, f32[32,128]{1,0:T(8,128)S(1)} %get-tuple-element.21.dark, bf16[384,1024]{1,0:T(8,128)(2,1)S(1)} %get-tuple-element.28.modes, ...), custom_call_target="tpu_custom_call" | custom-call | tf_op jit(solution)/shard_map/late_sheets/pallas_call | solution.py:525
  31.9 0.0 collective-permute-done.8.refs_4_
  31.9 2.0 %late_sheets.3 = f32[64,64,128]{2,1,0:T(8,128)} custom-call(f32[128,32,128]{2,1,0:T(8,128)S(1)} %bitcast.10, f32[32,128]{1,0:T(8,128)S(1)} %get-tuple-element.20.level, f32[32,128]{1,0:T(8,128)S(1)} %get-tuple-element.21.dark, bf16[384,1024]{1,0:T(8,128)(2,1)S(1)} %get-tuple-element.28.modes, ...), custom_call_target="tpu_custom_call", output_to_operand_aliasing={{}: (18, {})} | custom-call | tf_op jit(solution)/shard_map/late_sheets/pallas_call | solution.py:525
  (18 shorter events, 0.0 us)
Async XLA Ops:
  0.0 13.5 %copy-start = (f32[128,1,4096]{2,1,0:T(1,128)S(1)}, f32[128,1,4096]{2,1,0:T(1,128)}, u32[]{:S(2)}) copy-start(f32[128,1,4096]{2,1,0:T(1,128)} %param.19) | copy-start | bytes 6291460
  1.2 14.7 %collective-permute-start.4 = (f32[26,32,128]{2,1,0:T(8,128)S(1)}, f32[26,32,128]{2,1,0:T(8,128)S(1)}, u32[]{:S(2)}, u32[]{:S(2)}) collective-permute-start(f32[26,32,128]{2,1,0:T(8,128)S(1)} %first_piece.1), channel_id=1, source_target_pairs={{0,16},{8,24},{16,0},{24,8},{1,17},{9,25},{17,1},{25,9},{2,18},{10... | collective-permute-start | bytes 1277960 | tf_op jit(solution)/shard_map/ppermute | solution.py:28
  4.2 11.7 %copy-start.1 = (bf16[768,256]{1,0:T(8,128)(2,1)S(1)}, bf16[768,256]{1,0:T(8,128)(2,1)}, u32[]{:S(2)}) copy-start(bf16[768,256]{1,0:T(8,128)(2,1)} %constant.29.clone.refs_10_.refs_9_) | copy-start | bytes 1179652
  4.2 11.7 %copy-start.2 = (bf16[768,256]{1,0:T(8,128)(2,1)S(1)}, bf16[768,256]{1,0:T(8,128)(2,1)}, u32[]{:S(2)}) copy-start(bf16[768,256]{1,0:T(8,128)(2,1)} %constant.28.clone.refs_9_.refs_8_) | copy-start | bytes 1179652
  4.2 11.7 %copy-start.3 = (f32[128,256]{1,0:T(8,128)S(1)}, f32[128,256]{1,0:T(8,128)}, u32[]{:S(2)}) copy-start(f32[128,256]{1,0:T(8,128)} %constant.27.clone.refs_8_.refs_7_) | copy-start | bytes 393220
  4.2 11.7 %copy-start.4 = (f32[128,256]{1,0:T(8,128)S(1)}, f32[128,256]{1,0:T(8,128)}, u32[]{:S(2)}) copy-start(f32[128,256]{1,0:T(8,128)} %constant.31.clone.refs_12_.refs_11_) | copy-start | bytes 393220
  4.2 11.7 %copy-start.5 = (bf16[128,192]{1,0:T(8,128)(2,1)S(1)}, bf16[128,192]{1,0:T(8,128)(2,1)}, u32[]{:S(2)}) copy-start(bf16[128,192]{1,0:T(8,128)(2,1)} %constant.25.clone.refs_6_.refs_5_) | copy-start | bytes 147460
  4.2 11.7 %copy-start.6 = (bf16[64,384]{1,0:T(8,128)(2,1)S(1)}, bf16[64,384]{1,0:T(8,128)(2,1)}, u32[]{:S(2)}) copy-start(bf16[64,384]{1,0:T(8,128)(2,1)} %constant.30.clone.refs_11_.refs_10_) | copy-start | bytes 147460
  4.2 11.7 %copy-start.7 = (bf16[128,128]{1,0:T(8,128)(2,1)S(1)}, bf16[128,128]{1,0:T(8,128)(2,1)}, u32[]{:S(2)}) copy-start(bf16[128,128]{1,0:T(8,128)(2,1)} %constant.26.clone.refs_7_.refs_6_) | copy-start | bytes 98308
  7.1 6.4 %collective-permute-start = (f32[8,32,128]{2,1,0:T(8,128)S(1)}, f32[8,32,128]{2,1,0:T(8,128)S(1)}, u32[]{:S(2)}, u32[]{:S(2)}) collective-permute-start(f32[8,32,128]{2,1,0:T(8,128)S(1)} %get-tuple-element.23.other_a), channel_id=1, source_target_pairs={{0,8},{8,0},{16,24},{24,16},{1,9},{9,1},{17,25},{25,17},{2,10},{10... | collective-permute-start | bytes 393224 | tf_op jit(solution)/shard_map/ppermute | solution.py:28
  8.7 7.2 %collective-permute-start.1 = (f32[8,32,128]{2,1,0:T(8,128)S(1)}, f32[8,32,128]{2,1,0:T(8,128)S(1)}, u32[]{:S(2)}, u32[]{:S(2)}) collective-permute-start(f32[8,32,128]{2,1,0:T(8,128)S(1)} %get-tuple-element.22.mine), channel_id=1, source_target_pairs={{0,8},{8,0},{16,24},{24,16},{1,9},{9,1},{17,25},{25,17},{2,10},{10... | collective-permute-start | bytes 393224 | tf_op jit(solution)/shard_map/ppermute | solution.py:28
  13.8 11.0 %collective-permute-start.5 = (f32[10,32,128]{2,1,0:T(8,128)S(1)}, f32[10,32,128]{2,1,0:T(8,128)S(1)}, u32[]{:S(2)}, u32[]{:S(2)}) collective-permute-start(f32[10,32,128]{2,1,0:T(8,128)S(1)} %get-tuple-element.26), channel_id=1, source_target_pairs={{0,16},{8,24},{16,0},{24,8},{1,17},{9,25},{17,1},{25,9},{2,18},{10... | collective-permute-start | bytes 491528 | tf_op jit(solution)/shard_map/ppermute | solution.py:28
  13.9 7.5 %collective-permute-start.2 = (f32[8,32,128]{2,1,0:T(8,128)S(1)}, f32[8,32,128]{2,1,0:T(8,128)S(1)}, u32[]{:S(2)}, u32[]{:S(2)}) collective-permute-start(f32[8,32,128]{2,1,0:T(8,128)S(1)} %get-tuple-element.24.refs_4_.mine), channel_id=1, source_target_pairs={{0,16},{8,24},{16,0},{24,8},{1,17},{9,25},{17,1},{25,9},{2,18},{10... | collective-permute-start | bytes 393224 | tf_op jit(solution)/shard_map/ppermute | solution.py:28
  19.3 9.7 %collective-permute-start.6 = (f32[12,32,128]{2,1,0:T(8,128)S(1)}, f32[12,32,128]{2,1,0:T(8,128)S(1)}, u32[]{:S(2)}, u32[]{:S(2)}) collective-permute-start(f32[12,32,128]{2,1,0:T(8,128)S(1)} %get-tuple-element.30), channel_id=1, source_target_pairs={{0,16},{8,24},{16,0},{24,8},{1,17},{9,25},{17,1},{25,9},{2,18},{10... | collective-permute-start | bytes 589832 | tf_op jit(solution)/shard_map/ppermute | solution.py:28
  21.4 5.2 %collective-permute-start.3 = (f32[8,32,128]{2,1,0:T(8,128)S(1)}, f32[8,32,128]{2,1,0:T(8,128)S(1)}, u32[]{:S(2)}, u32[]{:S(2)}) collective-permute-start(f32[8,32,128]{2,1,0:T(8,128)S(1)} %collective-permute-done.2.refs_4_.far_mine), channel_id=1, source_target_pairs={{0,8},{8,0},{16,24},{24,16},{1,9},{9,1},{17,25},{25,17},{2,10},{10... | collective-permute-start | bytes 393224 | tf_op jit(solution)/shard_map/ppermute | solution.py:28
  22.9 6.1 %collective-permute-start.7 = (f32[8,32,128]{2,1,0:T(8,128)S(1)}, f32[8,32,128]{2,1,0:T(8,128)S(1)}, u32[]{:S(2)}, u32[]{:S(2)}) collective-permute-start(f32[8,32,128]{2,1,0:T(8,128)S(1)} %get-tuple-element.31), channel_id=1, source_target_pairs={{0,16},{8,24},{16,0},{24,8},{1,17},{9,25},{17,1},{25,9},{2,18},{10... | collective-permute-start | bytes 393224 | tf_op jit(solution)/shard_map/ppermute | solution.py:28
  24.8 1.8 %copy-start.8 = (bf16[288,384]{1,0:T(8,128)(2,1)S(1)}, bf16[288,384]{1,0:T(8,128)(2,1)}, u32[]{:S(2)}) copy-start(bf16[288,384]{1,0:T(8,128)(2,1)} %constant.32.clone.basis) | copy-start | bytes 663556
  24.8 1.8 %copy-start.9 = (f32[128,256]{1,0:T(8,128)S(1)}, f32[128,256]{1,0:T(8,128)}, u32[]{:S(2)}) copy-start(f32[128,256]{1,0:T(8,128)} %constant.33.clone.refs_12_) | copy-start | bytes 393220
  26.4 2.6 %copy-start.10 = (bf16[160,384]{1,0:T(8,128)(2,1)S(1)}, bf16[160,384]{1,0:T(8,128)(2,1)}, u32[]{:S(2)}) copy-start(bf16[160,384]{1,0:T(8,128)(2,1)} %constant.34.clone.basis) | copy-start | bytes 368644
  26.4 5.4 %collective-permute-start.8 = (f32[8,32,128]{2,1,0:T(8,128)S(1)}, f32[8,32,128]{2,1,0:T(8,128)S(1)}, u32[]{:S(2)}, u32[]{:S(2)}) collective-permute-start(f32[8,32,128]{2,1,0:T(8,128)S(1)} %get-tuple-element.33), channel_id=1, source_target_pairs={{0,16},{8,24},{16,0},{24,8},{1,17},{9,25},{17,1},{25,9},{2,18},{10... | collective-permute-start | bytes 393224 | tf_op jit(solution)/shard_map/ppermute | solution.py:28
  29.0 2.9 %copy-start.11 = (bf16[64,384]{1,0:T(8,128)(2,1)S(1)}, bf16[64,384]{1,0:T(8,128)(2,1)}, u32[]{:S(2)}) copy-start(bf16[64,384]{1,0:T(8,128)(2,1)} %constant.35.clone.basis) | copy-start | bytes 147460

commit v5 on v4

--- a/solution.py
+++ b/solution.py
@@ -17,7 +17,7 @@
 QUARTER = SIDE // 4
 MODES = 2 * KMAX
 MODE_GROUP = 8
-CHUNKS = ((8,8,10),(6,4),(6,6),(4,4),(4,4))
+CHUNKS = ((12, 16), (4, 4, 4), (4, 4, 4, 2), (2, 4), (4,))
 BF16 = jnp.bfloat16
 F32 = jnp.float32
 
@@ -700,11 +700,11 @@
     parts = (mine_sum, other, other_more, far_mine, far_other)
     fixed, modes = middle_sheets(early, parts, settings, halves, half_turn, half_block)
     out, late = late_sheets(
-        raw, partners[2:4], level, dark, modes, settings, CHUNKS[2] + CHUNKS[3], starts[2],
+        raw, partners[2:3], level, dark, modes, settings, CHUNKS[2], starts[2],
         halves, half_turn, fixed,
     )
     (out,) = late_sheets(
-        raw, partners[4:], level, dark, modes, settings, CHUNKS[4], starts[4],
+        raw, partners[3:], level, dark, modes, settings, CHUNKS[3] + CHUNKS[4], starts[3],
         halves, half_turn, late, out,
     )
     return out.reshape(half_block, local_rows, 2 * pixels)

time: 34.1 us -> 33 us (0.968)
  waiting for transfers between devices: 2.79 us -> 1.86 us
  Pallas kernels: 16.4 us -> 15.6 us
  starting transfers between devices: 11.9 us -> 12.5 us
    ppermute x9, waiting for transfers between devices: 2.79 us -> 1.86 us  [swapped(): return lax.ppermute(value, axis, pairs)]
    pallas_call x8, Pallas kernels: 16.4 us -> 15.6 us  [call(): pl.pallas_call(kernel, out_shape=out_shape, in_specs=specs, out_specs=out...]
    ppermute x9, starting transfers between devices: 11.9 us -> 12.5 us  [swapped(): return lax.ppermute(value, axis, pairs)]
  transfers between devices with their start and end apart: 9 -> 9, of which waited for: 2 -> 2; matrix products, arithmetic and copies ran while one was open for 0% -> 0% of each run, Pallas kernels for 39% -> 37%
where the time goes in v5:
time: 33 us; the launch traced here: 32.8 us
  Pallas kernels  15.6 us (47%)
  starting transfers between devices  12.5 us (38%)
  between operations  2.8 us (8%)
  waiting for transfers between devices  1.86 us (6%)
    pallas_call x8, Pallas kernels, call(): pl.pallas_call(kernel, out_shape=out_shape, in_specs=specs, out_specs=out...  15.6 us
    ppermute x9, starting transfers between devices, swapped(): return lax.ppermute(value, axis, pairs)  12.5 us
    ppermute x9, waiting for transfers between devices, swapped(): return lax.ppermute(value, axis, pairs)  1.86 us
  transfers between devices with their start and end apart: 9, of which 2 were waited for; matrix products, arithmetic and copies ran while one was open for 0% of the time, Pallas kernels for 37%

profile of v5, /device:TPU:0, one launch (start us, length us, event | category | flops | bytes accessed | tf_op | source)
XLA Modules:
  0.0 32.8 jit_solution(10697923062647910329)
XLA Ops:
  0.0 1.2 %first_piece.1 = f32[28,32,128]{2,1,0:T(8,128)S(1)} custom-call(f32[128,32,128]{2,1,0:T(8,128)} %bitcast.4), custom_call_target="tpu_custom_call" | custom-call | tf_op jit(solution)/shard_map/first_piece/pallas_call | solution.py:525
  1.2 3.0 %collective-permute-start.4 = (f32[28,32,128]{2,1,0:T(8,128)S(1)}, f32[28,32,128]{2,1,0:T(8,128)S(1)}, u32[]{:S(2)}, u32[]{:S(2)}) collective-permute-start(f32[28,32,128]{2,1,0:T(8,128)S(1)} %first_piece.1), channel_id=1, source_target_pairs={{0,16},{8,24},{16,0},{24,8},{1,17},{9,25},{17,1},{25,9},{2,18},{10... | collective-permute-start | bytes 1376264 | tf_op jit(solution)/shard_map/ppermute | solution.py:28
  4.2 0.0 copy-start.5
  4.2 0.0 copy-start.6
  4.3 0.0 copy-start.7
  4.3 2.9 %head.1 = (f32[8,32,128]{2,1,0:T(8,128)S(1)}, f32[8,32,128]{2,1,0:T(8,128)S(1)}, f32[32,128]{1,0:T(8,128)S(1)}, f32[32,128]{1,0:T(8,128)S(1)}) custom-call(f32[128,32,128]{2,1,0:T(8,128)} %bitcast.5, f32[32,128]{1,0:T(8,128)} %bitcast.11, f32[32,128]{1,0:T(8,128)} %bitcast.12, bf16[128,768]{1,0:T(8,128)(2,1)} %constant.24.clone.basis_far), custom_call_target="tpu_custom_call" | custom-call | bytes 16777216 | tf_op jit(solution)/shard_map/head/pallas_call | solution.py:525
  7.1 1.6 %collective-permute-start = (f32[8,32,128]{2,1,0:T(8,128)S(1)}, f32[8,32,128]{2,1,0:T(8,128)S(1)}, u32[]{:S(2)}, u32[]{:S(2)}) collective-permute-start(f32[8,32,128]{2,1,0:T(8,128)S(1)} %get-tuple-element.23.other_a), channel_id=1, source_target_pairs={{0,8},{8,0},{16,24},{24,16},{1,9},{9,1},{17,25},{25,17},{2,10},{10... | collective-permute-start | bytes 393224 | tf_op jit(solution)/shard_map/ppermute | solution.py:28
  8.7 0.5 %collective-permute-start.1 = (f32[8,32,128]{2,1,0:T(8,128)S(1)}, f32[8,32,128]{2,1,0:T(8,128)S(1)}, u32[]{:S(2)}, u32[]{:S(2)}) collective-permute-start(f32[8,32,128]{2,1,0:T(8,128)S(1)} %get-tuple-element.22.mine), channel_id=1, source_target_pairs={{0,8},{8,0},{16,24},{24,16},{1,9},{9,1},{17,25},{25,17},{2,10},{10... | collective-permute-start | bytes 393224 | tf_op jit(solution)/shard_map/ppermute | solution.py:28
  11.8 1.7 %collective-permute-done.received = f32[8,32,128]{2,1,0:T(8,128)S(1)} collective-permute-done((f32[8,32,128]{2,1,0:T(8,128)S(1)}, f32[8,32,128]{2,1,0:T(8,128)S(1)}, u32[]{:S(2)}, u32[]{:S(2)}) %collective-permute-start) | collective-permute-done | bytes 131104 | tf_op jit(solution)/shard_map/ppermute | solution.py:28
  13.6 0.0 copy-done
  13.6 0.3 add_modes.1
  13.8 0.1 collective-permute-start.2
  14.0 2.0 %collective-permute-start.5 = (f32[12,32,128]{2,1,0:T(8,128)S(1)}, f32[12,32,128]{2,1,0:T(8,128)S(1)}, u32[]{:S(2)}, u32[]{:S(2)}) collective-permute-start(f32[12,32,128]{2,1,0:T(8,128)S(1)} %get-tuple-element.26), channel_id=1, source_target_pairs={{0,16},{8,24},{16,0},{24,8},{1,17},{9,25},{17,1},{25,9},{2,18},{10... | collective-permute-start | bytes 589832 | tf_op jit(solution)/shard_map/ppermute | solution.py:28
  15.9 0.0 collective-permute-done.1.refs_5_.other_b
  15.9 0.0 collective-permute-done.4.partner
  16.0 3.4 %early_sheets.2 = (f32[28,64,128]{2,1,0:T(8,128)S(1)}, f32[14,32,128]{2,1,0:T(8,128)S(1)}, f32[6,32,128]{2,1,0:T(8,128)S(1)}) custom-call(f32[128,32,128]{2,1,0:T(8,128)S(1)} %bitcast.7, f32[28,32,128]{2,1,0:T(8,128)S(1)} %collective-permute-done.4.partner, f32[32,128]{1,0:T(8,128)S(1)} %get-tuple-element.20.level, f32[32,128]{1,0:T(8,128)S(1)} %get-tuple-element.21.dark, ...), custom_call_target="tpu_custom_call" | custom-call | tf_op jit(solution)/shard_map/early_sheets/pallas_call | solution.py:525
  19.4 1.8 %collective-permute-start.6 = (f32[14,32,128]{2,1,0:T(8,128)S(1)}, f32[14,32,128]{2,1,0:T(8,128)S(1)}, u32[]{:S(2)}, u32[]{:S(2)}) collective-permute-start(f32[14,32,128]{2,1,0:T(8,128)S(1)} %get-tuple-element.30), channel_id=1, source_target_pairs={{0,16},{8,24},{16,0},{24,8},{1,17},{9,25},{17,1},{25,9},{2,18},{10... | collective-permute-start | bytes 688136 | tf_op jit(solution)/shard_map/ppermute | solution.py:28
  21.2 0.0 collective-permute-done.2.refs_4_.far_mine
  21.2 1.5 %collective-permute-start.3 = (f32[8,32,128]{2,1,0:T(8,128)S(1)}, f32[8,32,128]{2,1,0:T(8,128)S(1)}, u32[]{:S(2)}, u32[]{:S(2)}) collective-permute-start(f32[8,32,128]{2,1,0:T(8,128)S(1)} %collective-permute-done.2.refs_4_.far_mine), channel_id=1, source_target_pairs={{0,8},{8,0},{16,24},{24,16},{1,9},{9,1},{17,25},{25,17},{2,10},{10... | collective-permute-start | bytes 393224 | tf_op jit(solution)/shard_map/ppermute | solution.py:28
  22.7 0.5 %collective-permute-start.7 = (f32[6,32,128]{2,1,0:T(8,128)S(1)}, f32[6,32,128]{2,1,0:T(8,128)S(1)}, u32[]{:S(2)}, u32[]{:S(2)}) collective-permute-start(f32[6,32,128]{2,1,0:T(8,128)S(1)} %get-tuple-element.32), channel_id=1, source_target_pairs={{0,16},{8,24},{16,0},{24,8},{1,17},{9,25},{17,1},{25,9},{2,18},{10... | collective-permute-start | bytes 294920 | tf_op jit(solution)/shard_map/ppermute | solution.py:28
  23.2 0.1 collective-permute-done.5.partner
  23.3 1.6 %early_sheets.3 = (f32[12,64,128]{2,1,0:T(8,128)S(1)}, f32[4,32,128]{2,1,0:T(8,128)S(1)}) custom-call(f32[128,32,128]{2,1,0:T(8,128)S(1)} %bitcast.8, f32[12,32,128]{2,1,0:T(8,128)S(1)} %collective-permute-done.5.partner, f32[32,128]{1,0:T(8,128)S(1)} %get-tuple-element.20.level, f32[32,128]{1,0:T(8,128)S(1)} %get-tuple-element.21.dark, s32[1]{0:T(128)S(6)} %copy.23.refs_0_, ...), custom_call_target="tpu_custom_call" | custom-call | tf_op jit(solution)/shard_map/early_sheets/pallas_call | solution.py:525
  24.9 0.0 copy-start.10
  24.9 1.5 %collective-permute-start.8 = (f32[4,32,128]{2,1,0:T(8,128)S(1)}, f32[4,32,128]{2,1,0:T(8,128)S(1)}, u32[]{:S(2)}, u32[]{:S(2)}) collective-permute-start(f32[4,32,128]{2,1,0:T(8,128)S(1)} %get-tuple-element.33), channel_id=1, source_target_pairs={{0,16},{8,24},{16,0},{24,8},{1,17},{9,25},{17,1},{25,9},{2,18},{10... | collective-permute-start | bytes 196616 | tf_op jit(solution)/shard_map/ppermute | solution.py:28
  26.4 0.0 collective-permute-done.3.far_other
  26.4 2.4 %middle_sheets.1 = (f32[40,64,128]{2,1,0:T(8,128)S(1)}, bf16[384,1024]{1,0:T(8,128)(2,1)S(1)}) custom-call(f32[8,32,128]{2,1,0:T(8,128)S(1)} %get-tuple-element.24.refs_4_.mine, f32[8,32,128]{2,1,0:T(8,128)S(1)} %get-tuple-element.23.other_a, f32[8,32,128]{2,1,0:T(8,128)S(1)} %collective-permute-done.1.refs_5_.other_b, ...), custom_call_target="tpu_custom_call" | custom-call | tf_op jit(solution)/shard_map/middle_sheets/pallas_call | solution.py:525
  28.8 0.0 collective-permute-done.6.refs_4_
  28.8 0.0 copy-start.11
  28.8 1.8 %late_sheets.2 = (f32[64,64,128]{2,1,0:T(8,128)}, f32[14,64,128]{2,1,0:T(8,128)S(1)}) custom-call(f32[128,32,128]{2,1,0:T(8,128)S(1)} %bitcast.9, f32[32,128]{1,0:T(8,128)S(1)} %get-tuple-element.20.level, f32[32,128]{1,0:T(8,128)S(1)} %get-tuple-element.21.dark, bf16[384,1024]{1,0:T(8,128)(2,1)S(1)} %get-tuple-element.28.modes, ...), custom_call_target="tpu_custom_call" | custom-call | tf_op jit(solution)/shard_map/late_sheets/pallas_call | solution.py:525
  30.6 0.0 collective-permute-done.8.refs_5_
  30.6 0.0 collective-permute-done.7.refs_4_
  30.6 2.2 %late_sheets.3 = f32[64,64,128]{2,1,0:T(8,128)} custom-call(f32[128,32,128]{2,1,0:T(8,128)S(1)} %bitcast.10, f32[32,128]{1,0:T(8,128)S(1)} %get-tuple-element.20.level, f32[32,128]{1,0:T(8,128)S(1)} %get-tuple-element.21.dark, bf16[384,1024]{1,0:T(8,128)(2,1)S(1)} %get-tuple-element.28.modes, ...), custom_call_target="tpu_custom_call", output_to_operand_aliasing={{}: (19, {})} | custom-call | tf_op jit(solution)/shard_map/late_sheets/pallas_call | solution.py:525
  (18 shorter events, 0.0 us)
Async XLA Ops:
  0.0 13.6 %copy-start = (f32[128,1,4096]{2,1,0:T(1,128)S(1)}, f32[128,1,4096]{2,1,0:T(1,128)}, u32[]{:S(2)}) copy-start(f32[128,1,4096]{2,1,0:T(1,128)} %param.19) | copy-start | bytes 6291460
  1.2 14.7 %collective-permute-start.4 = (f32[28,32,128]{2,1,0:T(8,128)S(1)}, f32[28,32,128]{2,1,0:T(8,128)S(1)}, u32[]{:S(2)}, u32[]{:S(2)}) collective-permute-start(f32[28,32,128]{2,1,0:T(8,128)S(1)} %first_piece.1), channel_id=1, source_target_pairs={{0,16},{8,24},{16,0},{24,8},{1,17},{9,25},{17,1},{25,9},{2,18},{10... | collective-permute-start | bytes 1376264 | tf_op jit(solution)/shard_map/ppermute | solution.py:28
  4.2 11.7 %copy-start.1 = (bf16[768,256]{1,0:T(8,128)(2,1)S(1)}, bf16[768,256]{1,0:T(8,128)(2,1)}, u32[]{:S(2)}) copy-start(bf16[768,256]{1,0:T(8,128)(2,1)} %constant.29.clone.refs_10_.refs_9_) | copy-start | bytes 1179652
  4.2 11.7 %copy-start.2 = (bf16[768,256]{1,0:T(8,128)(2,1)S(1)}, bf16[768,256]{1,0:T(8,128)(2,1)}, u32[]{:S(2)}) copy-start(bf16[768,256]{1,0:T(8,128)(2,1)} %constant.28.clone.refs_9_.refs_8_) | copy-start | bytes 1179652
  4.2 11.7 %copy-start.3 = (f32[128,256]{1,0:T(8,128)S(1)}, f32[128,256]{1,0:T(8,128)}, u32[]{:S(2)}) copy-start(f32[128,256]{1,0:T(8,128)} %constant.27.clone.refs_8_.refs_7_) | copy-start | bytes 393220
  4.2 11.7 %copy-start.4 = (f32[128,256]{1,0:T(8,128)S(1)}, f32[128,256]{1,0:T(8,128)}, u32[]{:S(2)}) copy-start(f32[128,256]{1,0:T(8,128)} %constant.31.clone.refs_12_.refs_11_) | copy-start | bytes 393220
  4.2 11.7 %copy-start.5 = (bf16[128,192]{1,0:T(8,128)(2,1)S(1)}, bf16[128,192]{1,0:T(8,128)(2,1)}, u32[]{:S(2)}) copy-start(bf16[128,192]{1,0:T(8,128)(2,1)} %constant.25.clone.refs_6_.refs_5_) | copy-start | bytes 147460
  4.2 11.7 %copy-start.6 = (bf16[64,384]{1,0:T(8,128)(2,1)S(1)}, bf16[64,384]{1,0:T(8,128)(2,1)}, u32[]{:S(2)}) copy-start(bf16[64,384]{1,0:T(8,128)(2,1)} %constant.30.clone.refs_11_.refs_10_) | copy-start | bytes 147460
  4.3 11.7 %copy-start.7 = (bf16[128,128]{1,0:T(8,128)(2,1)S(1)}, bf16[128,128]{1,0:T(8,128)(2,1)}, u32[]{:S(2)}) copy-start(bf16[128,128]{1,0:T(8,128)(2,1)} %constant.26.clone.refs_7_.refs_6_) | copy-start | bytes 98308
  7.1 6.4 %collective-permute-start = (f32[8,32,128]{2,1,0:T(8,128)S(1)}, f32[8,32,128]{2,1,0:T(8,128)S(1)}, u32[]{:S(2)}, u32[]{:S(2)}) collective-permute-start(f32[8,32,128]{2,1,0:T(8,128)S(1)} %get-tuple-element.23.other_a), channel_id=1, source_target_pairs={{0,8},{8,0},{16,24},{24,16},{1,9},{9,1},{17,25},{25,17},{2,10},{10... | collective-permute-start | bytes 393224 | tf_op jit(solution)/shard_map/ppermute | solution.py:28
  8.7 7.2 %collective-permute-start.1 = (f32[8,32,128]{2,1,0:T(8,128)S(1)}, f32[8,32,128]{2,1,0:T(8,128)S(1)}, u32[]{:S(2)}, u32[]{:S(2)}) collective-permute-start(f32[8,32,128]{2,1,0:T(8,128)S(1)} %get-tuple-element.22.mine), channel_id=1, source_target_pairs={{0,8},{8,0},{16,24},{24,16},{1,9},{9,1},{17,25},{25,17},{2,10},{10... | collective-permute-start | bytes 393224 | tf_op jit(solution)/shard_map/ppermute | solution.py:28
  13.8 7.4 %collective-permute-start.2 = (f32[8,32,128]{2,1,0:T(8,128)S(1)}, f32[8,32,128]{2,1,0:T(8,128)S(1)}, u32[]{:S(2)}, u32[]{:S(2)}) collective-permute-start(f32[8,32,128]{2,1,0:T(8,128)S(1)} %get-tuple-element.24.refs_4_.mine), channel_id=1, source_target_pairs={{0,16},{8,24},{16,0},{24,8},{1,17},{9,25},{17,1},{25,9},{2,18},{10... | collective-permute-start | bytes 393224 | tf_op jit(solution)/shard_map/ppermute | solution.py:28
  14.0 9.3 %collective-permute-start.5 = (f32[12,32,128]{2,1,0:T(8,128)S(1)}, f32[12,32,128]{2,1,0:T(8,128)S(1)}, u32[]{:S(2)}, u32[]{:S(2)}) collective-permute-start(f32[12,32,128]{2,1,0:T(8,128)S(1)} %get-tuple-element.26), channel_id=1, source_target_pairs={{0,16},{8,24},{16,0},{24,8},{1,17},{9,25},{17,1},{25,9},{2,18},{10... | collective-permute-start | bytes 589832 | tf_op jit(solution)/shard_map/ppermute | solution.py:28
  19.4 9.3 %collective-permute-start.6 = (f32[14,32,128]{2,1,0:T(8,128)S(1)}, f32[14,32,128]{2,1,0:T(8,128)S(1)}, u32[]{:S(2)}, u32[]{:S(2)}) collective-permute-start(f32[14,32,128]{2,1,0:T(8,128)S(1)} %get-tuple-element.30), channel_id=1, source_target_pairs={{0,16},{8,24},{16,0},{24,8},{1,17},{9,25},{17,1},{25,9},{2,18},{10... | collective-permute-start | bytes 688136 | tf_op jit(solution)/shard_map/ppermute | solution.py:28
  21.2 5.2 %collective-permute-start.3 = (f32[8,32,128]{2,1,0:T(8,128)S(1)}, f32[8,32,128]{2,1,0:T(8,128)S(1)}, u32[]{:S(2)}, u32[]{:S(2)}) collective-permute-start(f32[8,32,128]{2,1,0:T(8,128)S(1)} %collective-permute-done.2.refs_4_.far_mine), channel_id=1, source_target_pairs={{0,8},{8,0},{16,24},{24,16},{1,9},{9,1},{17,25},{25,17},{2,10},{10... | collective-permute-start | bytes 393224 | tf_op jit(solution)/shard_map/ppermute | solution.py:28
  22.7 7.9 %collective-permute-start.7 = (f32[6,32,128]{2,1,0:T(8,128)S(1)}, f32[6,32,128]{2,1,0:T(8,128)S(1)}, u32[]{:S(2)}, u32[]{:S(2)}) collective-permute-start(f32[6,32,128]{2,1,0:T(8,128)S(1)} %get-tuple-element.32), channel_id=1, source_target_pairs={{0,16},{8,24},{16,0},{24,8},{1,17},{9,25},{17,1},{25,9},{2,18},{10... | collective-permute-start | bytes 294920 | tf_op jit(solution)/shard_map/ppermute | solution.py:28
  23.3 3.1 %copy-start.8 = (bf16[320,384]{1,0:T(8,128)(2,1)S(1)}, bf16[320,384]{1,0:T(8,128)(2,1)}, u32[]{:S(2)}) copy-start(bf16[320,384]{1,0:T(8,128)(2,1)} %constant.32.clone.basis) | copy-start | bytes 737284
  23.3 3.1 %copy-start.9 = (f32[128,256]{1,0:T(8,128)S(1)}, f32[128,256]{1,0:T(8,128)}, u32[]{:S(2)}) copy-start(f32[128,256]{1,0:T(8,128)} %constant.33.clone.refs_12_) | copy-start | bytes 393220
  24.9 3.9 %copy-start.10 = (bf16[112,384]{1,0:T(8,128)(2,1)S(1)}, bf16[112,384]{1,0:T(8,128)(2,1)}, u32[]{:S(2)}) copy-start(bf16[112,384]{1,0:T(8,128)(2,1)} %constant.34.clone.basis) | copy-start | bytes 258052
  24.9 5.7 %collective-permute-start.8 = (f32[4,32,128]{2,1,0:T(8,128)S(1)}, f32[4,32,128]{2,1,0:T(8,128)S(1)}, u32[]{:S(2)}, u32[]{:S(2)}) collective-permute-start(f32[4,32,128]{2,1,0:T(8,128)S(1)} %get-tuple-element.33), channel_id=1, source_target_pairs={{0,16},{8,24},{16,0},{24,8},{1,17},{9,25},{17,1},{25,9},{2,18},{10... | collective-permute-start | bytes 196616 | tf_op jit(solution)/shard_map/ppermute | solution.py:28
  28.8 1.8 %copy-start.11 = (bf16[80,384]{1,0:T(8,128)(2,1)S(1)}, bf16[80,384]{1,0:T(8,128)(2,1)}, u32[]{:S(2)}) copy-start(bf16[80,384]{1,0:T(8,128)(2,1)} %constant.35.clone.basis) | copy-start | bytes 184324
